TPU v7x, 512 devices: a whole 4x4x16 slice. The times are simulated.
512 devices in a mesh: dp: 128 (over z, x, core), rep: 4 (over y).
Axes of the slice: x: 4, y: 4, z: 16, core: 2. Of those that a mesh axis runs over, the one named last changes fastest.
Arguments:
- hot_ids: int32 [131072, 2], P(('dp', 'rep')), may hold values from 0 to 1023
- cold_owner: int32 [262144, 1], P(('dp', 'rep')), may hold values from 0 to 127; in each aligned block of 512 rows (0 to 511, 512 to 1023, ...) at most 8 rows name the same one
- cold_offset: int32 [262144], P(('dp', 'rep')), may hold values from 0 to 511
- labels: int32 [131072], P(('dp', 'rep')), may hold values 0 or 1
- top_weight: bfloat16 [512, 1024], replicated, may hold values from -0.25 to 0.25
- out_weight: float32 [1024], replicated, may hold values from -0.5 to 0.5
- cold_table: float32 [65536, 128], P('dp'), may hold values from -6 to 6
- cold_accum: float32 [65536, 128], P('dp'), may hold values from 0.0001 to 0.01
- hot_cache: float32 [1024, 128], replicated, may hold values from -6 to 6
- hot_accum: float32 [1024, 128], replicated, may hold values from 0.01 to 1
- pending: float32 [524288, 128], P(('dp', 'rep')), may hold values from -0.3 to 0.3
- refresh_blocks: int32 [3], replicated, may hold values from 0 to 7, as said below
- block_clock: int32 [8], replicated, may hold values from 0 to 8
Outputs:
- cold_table_new: float32 [65536, 128], P('dp')
- cold_accum_new: float32 [65536, 128], P('dp')
- hot_cache_new: float32 [1024, 128], replicated
- hot_accum_new: float32 [1024, 128], replicated
- pending_new: float32 [524288, 128], P(('dp', 'rep'))
- top_grad: float32 [512, 1024], P(('dp', 'rep'))
- out_grad: float32 [1024], replicated
Inputs may be any that keep to these rules, and one draw needn't show every extreme that they name: `cold_owner`: within the lookups of one device (512 rows), no owner is named more than 8 times. `refresh_blocks`: the block numbers are distinct.
All inputs are finite; a program needn't handle non-finite values. No bound on the sum of `labels` on one device may be relied on, other than what follows from the above.
Results may differ from a plain program's by a relative error of at most 0.00165.
The roundings to bfloat16 on the way count: a program that leaves them out, or rounds other values in their place, can miss the bound.
Values may be sent and summed in bfloat16 or wider, within the bound.
No kernel may reach another device: no remote copies, remote signals or barrier semaphores. Data moves between devices by JAX's collectives and lax.ppermute only.
A program may use at most 64 MiB of HBM per device.

v0:
```python
import jax
import jax.numpy as jnp
from jax import lax
from jax.sharding import Mesh
from jax.sharding import PartitionSpec as P

BLOCK = 128
DP = ("dp_0", "dp_1", "dp_2")
DP_REP = ("dp_0", "dp_1", "dp_2", "rep")


step_size = 0.5
epsilon = 1e-08


def cut_along(shard, dim, count):
    dims = shard.shape
    pieces = shard.reshape(*dims[:dim], count, dims[dim] // count, *dims[dim + 1 :])
    return jnp.moveaxis(pieces, dim, 0)


def sum_at_owner(shard, axis, dim):
    count = lax.axis_size(axis)
    pieces = lax.all_to_all(cut_along(shard, dim, count), axis, 0, 0, tiled=True)
    return jnp.sum(pieces, axis=0)


def sum_by_axis(shard, axes, dim):
    far, near = axes
    pieces = cut_along(shard, dim, lax.axis_size(far))
    nearer = sum_at_owner(pieces, near, dim + 1)
    arrived = lax.all_to_all(nearer, far, split_axis=0, concat_axis=0, tiled=True)
    return arrived.sum(axis=0)


def in_one_piece(arrays, axis, dim, along):
    widths = [a.shape[along] for a in arrays]
    both = jnp.concatenate(arrays, axis=along)
    result = lax.all_gather(both, axis, axis=dim, tiled=True)
    return tuple(jnp.split(result, [sum(widths[:k]) for k in range(1, len(widths))], axis=along))


def padded_to(lines, count):
    spare = -lines.shape[0] % count
    if not spare:
        return lines
    return jnp.concatenate([lines, jnp.zeros((spare, *lines.shape[1:]), lines.dtype)])


def copy_for_each(shard, axis):
    copies = jnp.broadcast_to(shard, (lax.axis_size(axis), *shard.shape))
    return lax.all_to_all(copies, axis, split_axis=0, concat_axis=0, tiled=True)


def joined_along(pieces, dim):
    pieces = jnp.moveaxis(pieces, 0, dim)
    dims = pieces.shape
    return pieces.reshape(*dims[:dim], dims[dim] * dims[dim + 1], *dims[dim + 2 :])


def gather_axes(shard, axes, dim):
    far, near = axes
    pieces = copy_for_each(copy_for_each(shard, far), near)
    return joined_along(pieces.swapaxes(0, 1).reshape(-1, *shard.shape), dim)


def sum_by_parts(shard, axes):
    padded = padded_to(shard, lax.axis_size(axes[0]) * lax.axis_size(axes[1]))
    whole = gather_axes(sum_by_axis(padded, axes, 0), axes, 0)
    return lax.slice_in_dim(whole, 0, len(shard)).reshape(shard.shape)


def together(arrays, axis):
    ends = [0]
    for a in arrays:
        ends.append(ends[-1] + a.size)
    subtotal = sum_by_parts(jnp.concatenate([a.ravel() for a in arrays]), axis)
    return tuple((subtotal[b:e].reshape(a.shape) for a, b, e in zip(arrays, ends, ends[1:])))


def adagrad(table_rows, accum_rows, gradient):
    accum_next = accum_rows + gradient * gradient
    return (table_rows - step_size * gradient / (jnp.sqrt(accum_next) + epsilon), accum_next)


def local(
    hot_ids,
    cold_owner,
    cold_offset,
    labels,
    top_weight,
    out_weight,
    cold_table,
    cold_accum,
    hot_cache,
    hot_accum,
    pending,
    refresh_blocks,
    block_clock,
):
    width = hot_cache.shape[1]
    samples = hot_ids.shape[0]
    hot_feats = hot_ids.shape[1]
    lookups = cold_offset.shape[0]
    cold_feats = lookups // samples
    owners_count = lax.axis_size(DP)
    capacity = max(2, 2 * lookups // owners_count)
    owners = cold_owner[:, 0]
    matches = (owners[:, None] == jnp.arange(owners_count, dtype=jnp.int32)[None, :]).astype(
        jnp.int32
    )
    earlier = jnp.cumsum(matches, axis=0) - matches
    positions = jnp.sum(earlier * matches, axis=1)
    targets = owners * capacity + positions
    requests = jnp.zeros((owners_count * capacity,), jnp.int32).at[targets].set(cold_offset)
    requests = requests.reshape(owners_count, capacity)
    asked = lax.all_to_all(requests, DP, split_axis=0, concat_axis=0, tiled=True)
    found = cold_table[asked].astype(jnp.bfloat16)
    returned = lax.all_to_all(found, DP, split_axis=0, concat_axis=0, tiled=True)
    cold_rows = returned.reshape(owners_count * capacity, width)[targets]
    cold_rows = cold_rows.reshape(samples, cold_feats, width)
    hot_rows = hot_cache[hot_ids].astype(jnp.bfloat16)
    inputs = jnp.concatenate([hot_rows, cold_rows], axis=1).reshape(
        samples, (hot_feats + cold_feats) * width
    )
    preact = jnp.dot(inputs, top_weight, preferred_element_type=jnp.float32)
    hidden = jax.nn.silu(preact).astype(jnp.bfloat16)
    hidden_wide = hidden.astype(jnp.float32)
    logits = jnp.dot(hidden_wide, out_weight, precision=lax.Precision.HIGHEST)
    errors = jax.nn.sigmoid(logits) - labels.astype(jnp.float32)
    gates = jax.nn.sigmoid(preact)
    slope = gates * (1.0 + preact * (1.0 - gates))
    dhidden = (errors[:, None] * out_weight[None, :] * slope).astype(jnp.bfloat16)
    head_term = jnp.dot(errors, hidden_wide, precision=lax.Precision.HIGHEST)
    top_grad = sum_by_axis(
        lax.dot_general(
            inputs, dhidden, (((0,), (0,)), ((), ())), preferred_element_type=jnp.float32
        ),
        (("dp_0", "dp_1"), ("dp_2", "rep")),
        0,
    )
    dinputs = lax.dot_general(
        dhidden, top_weight, (((1,), (1,)), ((), ())), preferred_element_type=jnp.float32
    ).astype(jnp.bfloat16)
    dinputs = dinputs.reshape(samples, hot_feats + cold_feats, width)
    cold_dx = dinputs[:, hot_feats:].reshape(lookups, width)
    outgoing = jnp.zeros((owners_count * capacity, width), jnp.bfloat16).at[targets].set(cold_dx)
    outgoing = outgoing.reshape(owners_count, capacity, width)
    incoming = lax.all_to_all(outgoing, DP, split_axis=0, concat_axis=0, tiled=True)
    own_rows = cold_table.shape[0]
    cold_grad = (
        jnp.zeros((own_rows, width), jnp.float32)
        .at[asked.reshape(-1)]
        .add(incoming.reshape(-1, width).astype(jnp.float32))
    )
    quarter = own_rows // lax.axis_size("rep")
    offset_rows = lax.axis_index("rep") * quarter
    cold_share = sum_at_owner(cold_grad, "rep", 0)
    table_share = lax.dynamic_slice_in_dim(cold_table, offset_rows, quarter, 0)
    accum_share = lax.dynamic_slice_in_dim(cold_accum, offset_rows, quarter, 0)
    table_updated, accum_updated = adagrad(table_share, accum_share, cold_share)
    cold_table_new, cold_accum_new = in_one_piece((table_updated, accum_updated), "rep", 0, 1)
    hot_count = hot_cache.shape[0]
    blocks_count = hot_count // BLOCK
    hot_dx = dinputs[:, :hot_feats].reshape(samples * hot_feats, width).astype(jnp.float32)
    hot_grad = jnp.zeros((hot_count, width), jnp.float32).at[hot_ids.reshape(-1)].add(hot_dx)
    carried = (pending + hot_grad).reshape(blocks_count, BLOCK, width)
    picked = carried[refresh_blocks]
    divisors = 1.0 + block_clock[refresh_blocks].astype(jnp.float32)
    cache_blocks = hot_cache.reshape(blocks_count, BLOCK, width)
    accum_blocks = hot_accum.reshape(blocks_count, BLOCK, width)
    cache_chosen = cache_blocks[refresh_blocks]
    accum_chosen = accum_blocks[refresh_blocks]
    picked_sum, out_grad = together((picked, head_term), (("dp_0", "dp_1"), ("dp_2", "rep")))
    flush = picked_sum / divisors[:, None, None]
    cache_part, accum_part = adagrad(cache_chosen, accum_chosen, flush)
    hot_cache_new = cache_blocks.at[refresh_blocks].set(cache_part).reshape(hot_count, width)
    hot_accum_new = accum_blocks.at[refresh_blocks].set(accum_part).reshape(hot_count, width)
    pending_new = carried.at[refresh_blocks].set(0.0).reshape(hot_count, width)
    return (
        cold_table_new,
        cold_accum_new,
        hot_cache_new,
        hot_accum_new,
        pending_new,
        top_grad,
        out_grad,
    )


def solution(mesh):
    split = Mesh(mesh.devices.reshape(16, 4, 2, mesh.shape["rep"]), ("dp_0", "dp_1", "dp_2", "rep"))
    in_specs = (
        P(DP_REP, None),
        P(DP_REP, None),
        P(DP_REP),
        P(DP_REP),
        P(),
        P(),
        P(DP, None),
        P(DP, None),
        P(),
        P(),
        P(DP_REP, None),
        P(),
        P(),
    )
    out_specs = (P(DP, None), P(DP, None), P(), P(), P(DP_REP, None), P(DP_REP, None), P())
    return jax.shard_map(local, mesh=split, in_specs=in_specs, out_specs=out_specs, check_vma=False)
```

profile of v0, /device:TPU:1, one launch (start us, length us, event | category | flops | bytes accessed | tf_op | source)
XLA Modules:
  0.0 246.3 jit_solution(8379218844756459183)
XLA Ops:
  3.4 2.6 %scatter_custom_fusion = s32[1024]{0:T(1024)S(1)} fusion(s32[512]{0:T(512)S(1)} %bitcast.114, s32[512]{0:T(512)} %param.15, s32[]{:T(128)} %constant.13.clone.1), kind=kCustom, calls=%fused_computation.57 | custom fusion | bytes 4608 | tf_op jit(solution)/shard_map/scatter | solution.py:115
  6.1 35.1 %all_to_all.65 = s32[128,1,8]{2,1,0:T(1,128)S(1)} all-to-all(s32[128,1,8]{2,1,0:T(1,128)S(1)} %bitcast.105), channel_id=1, replica_groups=mesh['dp_0'=16,'dp_1'=4,'dp_2'=2,'rep'=4] {'dp_0','dp_1','dp_2'}, dimensions={0} | all-to-all | bytes 8192 | tf_op jit(solution)/shard_map/all_to_all | solution.py:117
  41.4 4.1 %gather_fusion.1 = bf16[1024,128]{1,0:T(8,128)(2,1)} fusion(f32[512,128]{1,0:T(8,128)S(1)} %copy-done.2, s32[1024]{0:T(1024)S(1)} %broadcast_clamp_fusion), kind=kCustom, calls=%fused_computation.1 | custom fusion | bytes 528384 | tf_op jit(solution)/shard_map/gather | solution.py:118
  45.5 5.7 %all-to-all-start.1 = ((bf16[128,8,128]{2,1,0:T(8,128)(2,1)}), bf16[128,8,128]{2,1,0:T(8,128)(2,1)S(1)}, u32[]{:S(2)}, u32[]{:S(2)}) async-start(bf16[128,8,128]{2,1,0:T(8,128)(2,1)} %bitcast.65), calls=%async_computation.1 | async-start | bytes 524288 | tf_op jit(solution)/shard_map/all_to_all | solution.py:119
  52.9 18.9 %all-to-all-done.1 = bf16[128,8,128]{2,1,0:T(8,128)(2,1)S(1)} async-done(((bf16[128,8,128]{2,1,0:T(8,128)(2,1)}), bf16[128,8,128]{2,1,0:T(8,128)(2,1)S(1)}, u32[]{:S(2)}, u32[]{:S(2)}) %all-to-all-start.1) | async-done | bytes 262176 | tf_op jit(solution)/shard_map/all_to_all | solution.py:119
  71.7 1.3 gather_fusion.2
  76.2 3.5 %scatter_custom_fusion.3 = f32[1024,128]{1,0:T(8,128)S(1)} fusion(f32[1024,128]{1,0:T(8,128)S(1)} %copy-done.9, s32[512]{0:T(512)S(1)} %bitcast.122, bf16[512,128]{1,0:T(8,128)(2,1)S(1)} %bitcast.101), kind=kCustom, calls=%fused_computation.23 | custom fusion | flops 131072 | bytes 655360 | tf_op jit(solution)/shard_map/scatter-add | solution.py:166
  80.8 11.2 %all_to_all.66 = f32[8,64,98]{2,1,0:T(8,128)S(1)} all-to-all(f32[8,64,98]{2,1,0:T(8,128)S(1)} %copy.51), channel_id=1, replica_groups=mesh['dp_0'=16,'dp_1'=4,'dp_2'=2,'rep'=4] {'dp_2','rep'}, dimensions={0} | all-to-all | bytes 401408 | tf_op jit(solution)/shard_map/all_to_all | solution.py:24
  92.1 20.6 %all_to_all.67 = f32[64,1,98]{2,1,0:T(1,128)S(1)} all-to-all(f32[64,1,98]{2,1,0:T(1,128)S(1)} %bitcast.106), channel_id=1, replica_groups=mesh['dp_0'=16,'dp_1'=4,'dp_2'=2,'rep'=4] {'dp_0','dp_1'}, dimensions={0} | all-to-all | bytes 50176 | tf_op jit(solution)/shard_map/all_to_all | solution.py:32
  112.8 17.4 %all_to_all.68 = f32[64,1,98]{2,1,0:T(1,128)S(1)} all-to-all(f32[64,1,98]{2,1,0:T(1,128)S(1)} %broadcast_in_dim.18), channel_id=1, replica_groups=mesh['dp_0'=16,'dp_1'=4,'dp_2'=2,'rep'=4] {'dp_0','dp_1'}, dimensions={0} | all-to-all | bytes 50176 | tf_op jit(solution)/shard_map/all_to_all | solution.py:52
  130.9 6.2 %all-to-all-start.7 = ((f32[8,64,98]{2,1,0:T(8,128)}), f32[8,64,98]{2,1,0:T(8,128)S(1)}, u32[]{:S(2)}, u32[]{:S(2)}) async-start(f32[8,64,98]{2,1,0:T(8,128)} %broadcast_in_dim.19), calls=%async_computation.7 | async-start | bytes 524288 | tf_op jit(solution)/shard_map/all_to_all | solution.py:52
  137.1 2.4 scatter_custom_fusion.1
  139.6 4.1 %all-to-all-done.7 = f32[8,64,98]{2,1,0:T(8,128)S(1)} async-done(((f32[8,64,98]{2,1,0:T(8,128)}), f32[8,64,98]{2,1,0:T(8,128)S(1)}, u32[]{:S(2)}, u32[]{:S(2)}) %all-to-all-start.7) | async-done | bytes 200736 | tf_op jit(solution)/shard_map/all_to_all | solution.py:52
  144.4 5.5 %all-to-all-start.2 = ((bf16[128,8,128]{2,1,0:T(8,128)(2,1)}), bf16[128,8,128]{2,1,0:T(8,128)(2,1)S(1)}, u32[]{:S(2)}, u32[]{:S(2)}) async-start(bf16[128,8,128]{2,1,0:T(8,128)(2,1)} %bitcast.18), calls=%async_computation.2 | async-start | bytes 524288 | tf_op jit(solution)/shard_map/all_to_all | solution.py:149
  150.0 1.9 convolution_bitcast_fusion
  151.9 2.6 %copy.53 = f32[8,64,1,1024]{3,1,2,0:T(8,128)} copy(f32[8,64,1,1024]{3,0,1,2:T(8,128)S(1)} %convolution_bitcast_fusion) | data formatting | bytes 4194304 | tf_op jit(solution)/shard_map/transpose | solution.py:19
  154.5 16.1 %all-to-all-done.2 = bf16[128,8,128]{2,1,0:T(8,128)(2,1)S(1)} async-done(((bf16[128,8,128]{2,1,0:T(8,128)(2,1)}), bf16[128,8,128]{2,1,0:T(8,128)(2,1)S(1)}, u32[]{:S(2)}, u32[]{:S(2)}) %all-to-all-start.2) | async-done | bytes 262176 | tf_op jit(solution)/shard_map/all_to_all | solution.py:149
  171.3 3.9 %all-to-all-start.8 = ((f32[8,64,1,1024]{3,1,2,0:T(8,128)}), f32[8,64,1,1024]{3,1,2,0:T(8,128)S(1)}, u32[]{:S(2)}, u32[]{:S(2)}) async-start(f32[8,64,1,1024]{3,1,2,0:T(8,128)} %copy.53), calls=%async_computation.8 | async-start | bytes 4194304 | tf_op jit(solution)/shard_map/all_to_all | solution.py:24
  175.9 2.3 gather_fusion.3
  178.2 2.3 gather_fusion.6
  181.9 7.1 %scatter_custom_fusion.2 = f32[512,128]{1,0:T(8,128)} fusion(s32[1024]{0:T(1024)S(1)} %bitcast.121, bf16[128,8,128]{2,1,0:T(8,128)(2,1)} %copy-done.10, f32[]{:T(128)} %constant.15.clone.1), kind=kCustom, calls=%fused_computation.19 | custom fusion | flops 262144 | bytes 524292 | tf_op jit(solution)/shard_map/scatter-add | solution.py:154
  188.9 12.5 %all-to-all-done.8 = f32[8,64,1,1024]{3,1,2,0:T(8,128)S(1)} async-done(((f32[8,64,1,1024]{3,1,2,0:T(8,128)}), f32[8,64,1,1024]{3,1,2,0:T(8,128)S(1)}, u32[]{:S(2)}, u32[]{:S(2)}) %all-to-all-start.8) | async-done | bytes 2097184 | tf_op jit(solution)/shard_map/all_to_all | solution.py:24
  201.5 4.0 %all-to-all-start.3 = ((f32[4,128,128]{2,1,0:T(8,128)}), f32[4,128,128]{2,1,0:T(8,128)}, u32[]{:S(2)}, u32[]{:S(2)}) async-start(f32[4,128,128]{2,1,0:T(8,128)} %bitcast.93), calls=%async_computation.3 | async-start | bytes 524288 | tf_op jit(solution)/shard_map/all_to_all | solution.py:24
  206.2 2.3 scatter_fusion.2
  208.5 1.8 copy.52
  210.3 1.8 reshape_reshape.8
  213.4 1.6 slice.41
  215.9 1.9 reduce_sum.66
  217.8 7.4 %all-to-all-start.9 = ((f32[64,1,1024]{2,1,0:T(1,128)}), f32[64,1,1024]{2,1,0:T(1,128)S(1)}, u32[]{:S(2)}, u32[]{:S(2)}) async-start(f32[64,1,1024]{2,1,0:T(1,128)} %reduce_sum.66), calls=%async_computation.9 | async-start | bytes 524288 | tf_op jit(solution)/shard_map/all_to_all | solution.py:32
  225.2 1.3 multiply_add_fusion
  229.9 12.0 %all_gather.3 = f32[512,256]{1,0:T(8,128)S(1)} all-gather(f32[128,256]{1,0:T(8,128)S(1)} %pad_maximum_fusion.2), channel_id=1, replica_groups=mesh['dp_0'=16,'dp_1'=4,'dp_2'=2,'rep'=4] {'rep'}, dimensions={0}, use_global_device_ids=true | all-gather | bytes 655360 | tf_op jit(solution)/shard_map/all_gather | solution.py:39
  242.7 2.8 %all-to-all-done.9 = f32[64,1,1024]{2,1,0:T(1,128)S(1)} async-done(((f32[64,1,1024]{2,1,0:T(1,128)}), f32[64,1,1024]{2,1,0:T(1,128)S(1)}, u32[]{:S(2)}, u32[]{:S(2)}) %all-to-all-start.9) | async-done | bytes 262176 | tf_op jit(solution)/shard_map/all_to_all | solution.py:32
  (99 shorter events, 20.8 us)
Async XLA Ops:
  0.6 72.9 %copy-start = (bf16[512,1024]{1,0:T(8,128)(2,1)S(1)}, bf16[512,1024]{1,0:T(8,128)(2,1)}, u32[]{:S(2)}) copy-start(bf16[512,1024]{1,0:T(8,128)(2,1)} %param.17) | copy-start | bytes 3145732
  0.6 2.1 copy-start.13
  0.7 1.3 copy-start.12
  1.8 49.9 %copy-start.3 = (f32[1024,128]{1,0:T(8,128)}, f32[1024,128]{1,0:T(8,128)S(1)}, u32[]{:S(2)}) copy-start(f32[1024,128]{1,0:T(8,128)S(1)} %copy.61) | copy-start | bytes 1572868
  1.8 39.5 %copy-start.2 = (f32[512,128]{1,0:T(8,128)S(1)}, f32[512,128]{1,0:T(8,128)}, u32[]{:S(2)}) copy-start(f32[512,128]{1,0:T(8,128)} %param.19) | copy-start | bytes 786436
  3.2 48.0 %copy-start.14 = (s32[256,2]{0,1:T(2,128)S(1)}, s32[256,2]{0,1:T(2,128)}, u32[]{:S(2)}) copy-start(s32[256,2]{0,1:T(2,128)} %param.13) | copy-start | bytes 6148
  41.4 11.5 %copy-start.17 = (s32[3]{0:T(128)S(1)}, s32[3]{0:T(128)}, u32[]{:S(2)}) copy-start(s32[3]{0:T(128)} %param.24) | copy-start | bytes 40
  45.5 26.3 %all-to-all-start.1 = ((bf16[128,8,128]{2,1,0:T(8,128)(2,1)}), bf16[128,8,128]{2,1,0:T(8,128)(2,1)S(1)}, u32[]{:S(2)}, u32[]{:S(2)}) async-start(bf16[128,8,128]{2,1,0:T(8,128)(2,1)} %bitcast.65), calls=%async_computation.1 | async-start | bytes 524288 | tf_op jit(solution)/shard_map/all_to_all | solution.py:119
  73.6 0.7 copy-start.15
  73.6 1.2 copy-start.16
  74.2 1.0 copy-start.18
  75.2 1.0 copy-start.9
  79.7 64.7 %copy-start.8 = (f32[1024,128]{1,0:T(8,128)}, f32[1024,128]{1,0:T(8,128)S(1)}, u32[]{:S(2)}) copy-start(f32[1024,128]{1,0:T(8,128)S(1)} %scatter_custom_fusion.3) | copy-start | bytes 1572868
  130.9 12.8 %all-to-all-start.7 = ((f32[8,64,98]{2,1,0:T(8,128)}), f32[8,64,98]{2,1,0:T(8,128)S(1)}, u32[]{:S(2)}, u32[]{:S(2)}) async-start(f32[8,64,98]{2,1,0:T(8,128)} %broadcast_in_dim.19), calls=%async_computation.7 | async-start | bytes 524288 | tf_op jit(solution)/shard_map/all_to_all | solution.py:52
  143.7 0.7 copy-start.11
  144.4 26.2 %all-to-all-start.2 = ((bf16[128,8,128]{2,1,0:T(8,128)(2,1)}), bf16[128,8,128]{2,1,0:T(8,128)(2,1)S(1)}, u32[]{:S(2)}, u32[]{:S(2)}) async-start(bf16[128,8,128]{2,1,0:T(8,128)(2,1)} %bitcast.18), calls=%async_computation.2 | async-start | bytes 524288 | tf_op jit(solution)/shard_map/all_to_all | solution.py:149
  154.5 20.7 %copy-start.1 = (s32[8]{0:T(128)S(1)}, s32[8]{0:T(128)}, u32[]{:S(2)}) copy-start(s32[8]{0:T(128)} %param.25) | copy-start | bytes 100
  170.6 0.7 copy-start.10
  171.3 30.2 %all-to-all-start.8 = ((f32[8,64,1,1024]{3,1,2,0:T(8,128)}), f32[8,64,1,1024]{3,1,2,0:T(8,128)S(1)}, u32[]{:S(2)}, u32[]{:S(2)}) async-start(f32[8,64,1,1024]{3,1,2,0:T(8,128)} %copy.53), calls=%async_computation.8 | async-start | bytes 4194304 | tf_op jit(solution)/shard_map/all_to_all | solution.py:24
  201.5 16.3 %all-to-all-start.3 = ((f32[4,128,128]{2,1,0:T(8,128)}), f32[4,128,128]{2,1,0:T(8,128)}, u32[]{:S(2)}, u32[]{:S(2)}) async-start(f32[4,128,128]{2,1,0:T(8,128)} %bitcast.93), calls=%async_computation.3 | async-start | bytes 524288 | tf_op jit(solution)/shard_map/all_to_all | solution.py:24
  215.9 10.6 %copy-start.6 = (f32[1024,128]{1,0:T(8,128)S(1)}, f32[1024,128]{1,0:T(8,128)}, u32[]{:S(2)}) copy-start(f32[1024,128]{1,0:T(8,128)} %copy.62) | copy-start | bytes 1572868
  215.9 11.3 %copy-start.4 = (f32[1024,128]{1,0:T(8,128)S(1)}, f32[1024,128]{1,0:T(8,128)}, u32[]{:S(2)}) copy-start(f32[1024,128]{1,0:T(8,128)} %copy-done.3) | copy-start | bytes 1572868
  217.8 27.7 %all-to-all-start.9 = ((f32[64,1,1024]{2,1,0:T(1,128)}), f32[64,1,1024]{2,1,0:T(1,128)S(1)}, u32[]{:S(2)}, u32[]{:S(2)}) async-start(f32[64,1,1024]{2,1,0:T(1,128)} %reduce_sum.66), calls=%async_computation.9 | async-start | bytes 524288 | tf_op jit(solution)/shard_map/all_to_all | solution.py:32
  227.2 19.1 %copy-start.7 = (f32[8,128,128]{2,1,0:T(8,128)}, f32[8,128,128]{2,1,0:T(8,128)S(1)}, u32[]{:S(2)}) copy-start(f32[8,128,128]{2,1,0:T(8,128)S(1)} %scatter_fusion.1) | copy-start | bytes 1572868
  227.8 18.5 %copy-start.5 = (f32[8,128,128]{2,1,0:T(8,128)}, f32[8,128,128]{2,1,0:T(8,128)S(1)}, u32[]{:S(2)}) copy-start(f32[8,128,128]{2,1,0:T(8,128)S(1)} %scatter_fusion) | copy-start | bytes 1572868
where the time goes:
time: 249 us; the launch traced here: 246 us
  blocking collectives  96.3 us (39%)
  waiting for transfers between devices  54.4 us (22%)
  local copies, waits for them, and re-layouts  40.3 us (16%)
  starting transfers between devices  32.8 us (13%)
  other arithmetic  17.4 us (7%)
  matrix products  3.97 us (2%)
    all_to_all x1, blocking collectives, local(): lax.all_to_all(requests, DP, split_axis=0, concat_axis=0, tiled=True)  35.1 us
    all_to_all x1, blocking collectives, sum_by_axis(): lax.all_to_all(nearer, far, split_axis=0, concat_axis=0, tiled=True)  20.6 us
    all_to_all x1, waiting for transfers between devices, local(): lax.all_to_all(found, DP, split_axis=0, concat_axis=0, tiled=True)  18.9 us
    all_to_all x1, blocking collectives, copy_for_each(): return lax.all_to_all(copies, axis, split_axis=0, concat_axis=0, tiled=True)  17.4 us
    all_to_all x1, waiting for transfers between devices, local(): lax.all_to_all(outgoing, DP, split_axis=0, concat_axis=0, tiled=True)  16.1 us
    all_to_all x2, waiting for transfers between devices, sum_at_owner(): lax.all_to_all(cut_along(shard, dim, count), axis, 0, 0, tiled=True)  12.5 us
    all_gather x1, blocking collectives, in_one_piece(): result = lax.all_gather(both, axis, axis=dim, tiled=True)  12 us
    all_to_all x1, blocking collectives, sum_at_owner(): lax.all_to_all(cut_along(shard, dim, count), axis, 0, 0, tiled=True)  11.2 us
  transfers between devices with their start and end apart: 6, of which 5 were waited for; matrix products, arithmetic and copies ran while one was open for 16% of the time, Pallas kernels for 0%

commit v1 on v0

v1 whole, which is shorter than its diff:
```python
import jax
import jax.numpy as jnp
from jax import lax
from jax.experimental import pallas as pl
from jax.experimental.pallas import tpu as pltpu
from jax.sharding import Mesh
from jax.sharding import PartitionSpec as P

BLOCK = 128
SLOTS = 8
DP = ("dp_0", "dp_1", "dp_2")
DP_REP = ("dp_0", "dp_1", "dp_2", "rep")
PLANE = ("dp_2", "rep", "dp_1")

step_size = 0.5
epsilon = 1e-08

F32 = jnp.float32
BF16 = jnp.bfloat16
EXACT = lax.Precision.HIGHEST
VMEM = pl.BlockSpec(memory_space=pltpu.VMEM)
SMEM = pl.BlockSpec(memory_space=pltpu.SMEM)


def call(kernel, outs, args, smem=0, scratch=(), flops=10**8, moved=10**6):
    shapes = [jax.ShapeDtypeStruct(s, d) for s, d in outs]
    return pl.pallas_call(
        kernel,
        out_shape=shapes,
        in_specs=[SMEM] * smem + [VMEM] * (len(args) - smem),
        out_specs=[VMEM] * len(outs),
        scratch_shapes=[pltpu.VMEM(s, d) for s, d in scratch],
        compiler_params=pltpu.CompilerParams(vmem_limit_bytes=40 * 2**20),
        cost_estimate=pl.CostEstimate(flops=flops, bytes_accessed=moved, transcendentals=0),
    )(*args)


def iota(shape, dim):
    return lax.broadcasted_iota(jnp.int32, shape, dim)


def iota_f(shape, dim):
    return iota(shape, dim).astype(F32)


def ones_where(mask):
    return jnp.where(mask, 1.0, 0.0).astype(BF16)


def column_of(row, eye):
    return jnp.sum(jnp.where(eye, row, 0.0), axis=1, keepdims=True)


def dot(a, b, precision=None):
    return jnp.dot(a, b, preferred_element_type=F32, precision=precision)


def dot_t(a, b):
    return lax.dot_general(a, b, (((1,), (1,)), ((), ())), preferred_element_type=F32)


def requests_kernel(owner_ref, offset_ref, request_ref, target_ref):
    square = (BLOCK, BLOCK)
    eye = iota(square, 0) == iota(square, 1)
    groups = owner_ref.shape[0]
    lookups = groups * BLOCK
    owner = owner_ref[...].astype(F32)
    offset = offset_ref[...].astype(F32)
    rows = [owner[s : s + 1, :] for s in range(groups)]
    owner_col = jnp.concatenate([column_of(row, eye) for row in rows], axis=0)
    offset_col = jnp.concatenate([column_of(offset[s : s + 1, :], eye) for s in range(groups)], axis=0)
    lane = iota_f((lookups, BLOCK), 1)
    named = owner_col == lane
    before = ones_where(iota((lookups, lookups), 0) > iota((lookups, lookups), 1))
    earlier = dot(before, ones_where(named))
    rank = jnp.sum(jnp.where(named, earlier, 0.0), axis=1, keepdims=True)
    target_ref[...] = jnp.broadcast_to(owner_col * SLOTS + rank, (lookups, BLOCK))
    placed = jnp.where(rank == lane, offset_col, 0.0)
    sublane = iota_f(square, 0)
    named_t = jnp.concatenate([jnp.where(sublane == row, 1.0, 0.0) for row in rows], axis=1)
    request_ref[...] = dot(named_t, placed, EXACT)


def rows_kernel(asked_ref, table_ref, rows_ref):
    count = rows_ref.shape[0]
    row, lane = iota((count, BLOCK), 0), iota((count, BLOCK), 1)
    spread = dot(jnp.where(row // SLOTS == lane, 1.0, 0.0), asked_ref[...], EXACT)
    wanted = jnp.sum(jnp.where(row % SLOTS == lane, spread, 0.0), axis=1, keepdims=True)
    chosen = ones_where(wanted == iota_f((count, table_ref.shape[0]), 1))
    rows_ref[...] = dot(chosen, table_ref[...].astype(BF16)).astype(BF16)


def masks_kernel(target_ref, hot_ref, cache_ref, asked_ref, take_ref, put_ref, hot_in_ref, hot_put_ref, owned_ref):
    square = (BLOCK, BLOCK)
    eye = iota(square, 0) == iota(square, 1)
    slots, lookups = put_ref.shape
    feats = hot_ref.shape[0]
    samples = hot_ref.shape[1]
    lane = iota_f((samples, BLOCK), 1)
    slot = iota_f((slots, BLOCK), 0)
    for k in range(feats):
        mine = target_ref[pl.ds(k, samples, stride=feats), :]
        for b in range(slots // BLOCK):
            take_ref[k * samples : (k + 1) * samples, b * BLOCK : (b + 1) * BLOCK] = ones_where(
                mine == lane + float(b * BLOCK)
            )
        for h in range(samples // BLOCK):
            at = k * samples + h * BLOCK
            row = jnp.sum(jnp.where(eye, mine[h * BLOCK : (h + 1) * BLOCK, :], 0.0), axis=0, keepdims=True)
            put_ref[:, at : at + BLOCK] = ones_where(slot == row)
    cache = cache_ref[...].astype(BF16)
    hot = hot_ref[...].astype(F32)
    hot_count = cache.shape[0]
    hot_row = iota_f((hot_count, BLOCK), 0)
    hot_lane = iota_f((BLOCK, hot_count), 1)
    for k in range(feats):
        for h in range(samples // BLOCK):
            at = k * samples + h * BLOCK
            row = hot[k : k + 1, h * BLOCK : (h + 1) * BLOCK]
            hot_put_ref[:, at : at + BLOCK] = ones_where(hot_row == row)
            chosen = ones_where(column_of(row, eye) == hot_lane)
            hot_in_ref[h * BLOCK : (h + 1) * BLOCK, k * BLOCK : (k + 1) * BLOCK] = dot(chosen, cache).astype(BF16)
    source, line = iota((BLOCK, slots), 0), iota((BLOCK, slots), 1)
    spread = dot(asked_ref[...], jnp.where(source == line % SLOTS, 1.0, 0.0), EXACT)
    wanted = jnp.sum(jnp.where(source == line // SLOTS, spread, 0.0), axis=0, keepdims=True)
    owned_ref[...] = ones_where(iota_f(owned_ref.shape, 0) == wanted)


def layer_kernel(
    returned_ref, take_ref, put_ref, hot_in_ref, weight_ref, out_weight_ref, labels_ref,
    outgoing_ref, inputs_ref, dhidden_ref, hot_dx_ref, head_ref,
):
    square = (BLOCK, BLOCK)
    eye = iota(square, 0) == iota(square, 1)
    samples = hot_in_ref.shape[0]
    width = BLOCK
    cold = dot(take_ref[...], returned_ref[...]).astype(BF16)
    inputs = jnp.concatenate([hot_in_ref[...], cold[:samples], cold[samples:]], axis=1)
    inputs_ref[...] = inputs
    weight = weight_ref[...]
    out_weight = out_weight_ref[...]
    preact = dot(inputs, weight)
    gates = jax.nn.sigmoid(preact)
    hidden = (preact * gates).astype(BF16).astype(F32)
    logits = jnp.sum(hidden * out_weight, axis=1, keepdims=True)
    labels = labels_ref[...].astype(F32)
    label = jnp.concatenate([column_of(labels[h : h + 1, :], eye) for h in range(samples // BLOCK)], axis=0)
    errors = jax.nn.sigmoid(logits) - label
    slope = gates * (1.0 + preact * (1.0 - gates))
    dhidden = (errors * out_weight * slope).astype(BF16)
    dhidden_ref[...] = dhidden
    dinputs = dot_t(dhidden, weight).astype(BF16)
    cold_dx = jnp.concatenate([dinputs[:, 2 * width : 3 * width], dinputs[:, 3 * width :]], axis=0)
    outgoing_ref[...] = dot(put_ref[...], cold_dx).astype(BF16)
    hot_dx_ref[:samples, :] = dinputs[:, :width]
    hot_dx_ref[samples:, :] = dinputs[:, width : 2 * width]
    head = jnp.sum(errors * hidden, axis=0, keepdims=True)
    for b in range(head_ref.shape[0]):
        head_ref[b : b + 1, :] = head[:, b * BLOCK : (b + 1) * BLOCK]


def half_of_top(core, inputs, dhidden):
    shape = (inputs.shape[1] // 2, inputs.shape[1])
    line = iota(shape, 0)
    row = (line & 15) * 32 + ((line >> 4) & 3) * 8 + core * 4 + (line >> 6)
    ordered = dot_t(ones_where(row == iota(shape, 1)), inputs).astype(BF16)
    return dot(ordered, dhidden)


def send_kernel(
    core_ref, refresh_ref, inputs_ref, dhidden_ref, hot_put_ref, hot_dx_ref, head_ref, pending_ref,
    send_ref, picked_ref, pending_new_ref,
):
    pending_new_ref[...] = pending_ref[...] + dot(hot_put_ref[...], hot_dx_ref[...])
    count = refresh_ref.shape[0]
    blocks = [pl.ds(pl.multiple_of(refresh_ref[i] * BLOCK, BLOCK), BLOCK) for i in range(count)]
    for i, at in enumerate(blocks):
        picked_ref[i * BLOCK : (i + 1) * BLOCK, :] = pending_new_ref[at, :]
    end = count * BLOCK
    picked_ref[end : end + 8, :] = head_ref[...]
    picked_ref[end + 8 :, :] = jnp.zeros((picked_ref.shape[0] - end - 8, BLOCK), F32)
    for at in blocks:
        pending_new_ref[at, :] = jnp.zeros((BLOCK, BLOCK), F32)
    other = 1 - core_ref[0]
    wide = dhidden_ref.shape[1]
    half = send_ref.shape[0]
    send_ref[:, :wide] = half_of_top(other, inputs_ref[...], dhidden_ref[...])
    send_ref[:, wide:] = picked_ref[pl.ds(pl.multiple_of(other * half, half), half), :]


def pair_kernel(core_ref, inputs_ref, dhidden_ref, picked_ref, received_ref, sum_ref):
    mine = core_ref[0]
    wide = dhidden_ref.shape[1]
    half = sum_ref.shape[0]
    sum_ref[:, :wide] = half_of_top(mine, inputs_ref[...], dhidden_ref[...]) + received_ref[:, :wide]
    sum_ref[:, wide:] = picked_ref[pl.ds(pl.multiple_of(mine * half, half), half), :] + received_ref[:, wide:]


def plane_kernel(parts_ref, out_ref):
    total = parts_ref[0]
    for i in range(1, parts_ref.shape[0]):
        total = total + parts_ref[i]
    wide = total.shape[1] - BLOCK
    tall = wide // BLOCK
    for b in range(tall):
        out_ref[:, b, :] = total[:, b * BLOCK : (b + 1) * BLOCK]
    for z in range(out_ref.shape[0]):
        out_ref[z, tall:, :] = total[:, wide:]


def column_kernel(parts_ref, top_ref, copies_ref):
    total = parts_ref[0]
    for i in range(1, parts_ref.shape[0]):
        total = total + parts_ref[i]
    tall = top_ref.shape[0]
    top_ref[...] = total[:tall]
    for i in range(copies_ref.shape[0]):
        copies_ref[i] = total[tall:]


def adagrad(table_rows, accum_rows, gradient):
    accum_next = accum_rows + gradient * gradient
    return (table_rows - step_size * gradient / (jnp.sqrt(accum_next) + epsilon), accum_next)


def hot_kernel(refresh_ref, clock_ref, sums_ref, cache_ref, accum_ref, cache_new_ref, accum_new_ref, out_grad_ref):
    cache_new_ref[...] = cache_ref[...]
    accum_new_ref[...] = accum_ref[...]
    count = refresh_ref.shape[0]
    for i in range(count):
        block = refresh_ref[i]
        at = pl.ds(pl.multiple_of(block * BLOCK, BLOCK), BLOCK)
        flush = sums_ref[i * BLOCK : (i + 1) * BLOCK, :] / (1.0 + clock_ref[block].astype(F32))
        cache_next, accum_next = adagrad(cache_ref[at, :], accum_ref[at, :], flush)
        cache_new_ref[at, :] = cache_next
        accum_new_ref[at, :] = accum_next
    out_grad_ref[...] = sums_ref[count * BLOCK : count * BLOCK + 8, :]


def cold_kernel(owned_ref, incoming_ref, grad_ref):
    grad_ref[...] = dot(owned_ref[...], incoming_ref[...])


def update_kernel(own_ref, one_ref, two_ref, three_ref, table_ref, accum_ref, table_new_ref, accum_new_ref):
    grad = (own_ref[...] + one_ref[...]) + (two_ref[...] + three_ref[...])
    table_next, accum_next = adagrad(table_ref[...], accum_ref[...], grad)
    table_new_ref[...] = table_next
    accum_new_ref[...] = accum_next


def swap(x, axis):
    return lax.all_to_all(x, axis, split_axis=0, concat_axis=0, tiled=True)


def local(
    hot_ids,
    cold_owner,
    cold_offset,
    labels,
    top_weight,
    out_weight,
    cold_table,
    cold_accum,
    hot_cache,
    hot_accum,
    pending,
    refresh_blocks,
    block_clock,
):
    samples, feats = hot_ids.shape
    lookups = cold_offset.shape[0]
    own_rows, width = cold_table.shape
    hot_count = hot_cache.shape[0]
    inputs_width, hidden_width = top_weight.shape
    owners = lax.axis_size(DP)
    slots = owners * SLOTS
    groups = lookups // BLOCK
    core = lax.axis_index("dp_2").astype(jnp.int32).reshape(1)

    request, target = call(
        requests_kernel,
        [((owners, BLOCK), F32), ((lookups, BLOCK), F32)],
        (cold_owner.reshape(groups, BLOCK), cold_offset.reshape(groups, BLOCK)),
    )
    asked = swap(request.reshape(owners, 1, BLOCK), DP).reshape(owners, BLOCK)
    (found,) = call(rows_kernel, [((slots, width), BF16)], (asked, cold_table))
    returned = swap(found.reshape(owners, SLOTS, width), DP).reshape(slots, width)
    take, put, hot_in, hot_put, owned = call(
        masks_kernel,
        [
            ((lookups, slots), BF16),
            ((slots, lookups), BF16),
            ((samples, feats * width), BF16),
            ((hot_count, samples * feats), BF16),
            ((own_rows, slots), BF16),
        ],
        (target, hot_ids.T, hot_cache, asked),
    )
    outgoing, inputs, dhidden, hot_dx, head = call(
        layer_kernel,
        [
            ((slots, width), BF16),
            ((samples, inputs_width), BF16),
            ((samples, hidden_width), BF16),
            ((samples * feats, width), BF16),
            ((8, BLOCK), F32),
        ],
        (returned, take, put, hot_in, top_weight, out_weight.reshape(1, hidden_width), labels.reshape(2, BLOCK)),
    )
    incoming = swap(outgoing.reshape(owners, SLOTS, width), DP).reshape(slots, width)

    half = inputs_width // 2
    broad = hidden_width + BLOCK
    send, picked, pending_new = call(
        send_kernel,
        [((half, broad), F32), ((inputs_width, BLOCK), F32), ((hot_count, width), F32)],
        (core, refresh_blocks, inputs, dhidden, hot_put, hot_dx, head, pending),
        smem=2,
    )
    received = lax.ppermute(send, "dp_2", [(0, 1), (1, 0)])
    (paired,) = call(pair_kernel, [((half, broad), F32)], (core, inputs, dhidden, picked, received), smem=1)
    near = lax.axis_size(("rep", "dp_1"))
    far = lax.axis_size("dp_0")
    plane = swap(paired.reshape(near, far, broad), ("rep", "dp_1"))
    tall = hidden_width // BLOCK
    (columns,) = call(plane_kernel, [((far, tall + far, BLOCK), F32)], (plane,))
    columns = swap(columns, "dp_0")
    top, copies = call(
        column_kernel, [((tall, BLOCK), F32), ((2 * near, far, BLOCK), F32)], (columns,)
    )
    sums = swap(copies, PLANE).reshape(2 * near * far, BLOCK)

    (grad,) = call(cold_kernel, [((own_rows, width), F32)], (owned, incoming))
    others = [lax.ppermute(grad, "rep", [(i, i ^ d) for i in range(4)]) for d in (1, 2, 3)]
    cold_table_new, cold_accum_new = call(
        update_kernel, [((own_rows, width), F32)] * 2, (grad, *others, cold_table, cold_accum)
    )
    hot_cache_new, hot_accum_new, out_grad = call(
        hot_kernel,
        [((hot_count, width), F32)] * 2 + [((8, BLOCK), F32)],
        (refresh_blocks, block_clock, sums, hot_cache, hot_accum),
        smem=2,
    )
    return (
        cold_table_new,
        cold_accum_new,
        hot_cache_new,
        hot_accum_new,
        pending_new,
        top.reshape(1, hidden_width),
        out_grad.reshape(hidden_width),
    )


def solution(mesh):
    split = Mesh(mesh.devices.reshape(16, 4, 2, mesh.shape["rep"]), ("dp_0", "dp_1", "dp_2", "rep"))
    in_specs = (
        P(DP_REP, None),
        P(DP_REP, None),
        P(DP_REP),
        P(DP_REP),
        P(),
        P(),
        P(DP, None),
        P(DP, None),
        P(),
        P(),
        P(DP_REP, None),
        P(),
        P(),
    )
    out_specs = (P(DP, None), P(DP, None), P(), P(), P(DP_REP, None), P(DP_REP, None), P())
    return jax.shard_map(local, mesh=split, in_specs=in_specs, out_specs=out_specs, check_vma=False)
```

time: 249 us -> 170 us (0.68)
  blocking collectives: 96.3 us -> 60.9 us
  local copies, waits for them, and re-layouts: 40.3 us -> 7.24 us
  other arithmetic: 17.4 us -> 0 us
  Pallas kernels: 0 us -> 14.9 us
  waiting for transfers between devices: 54.4 us -> 47.2 us
  starting transfers between devices: 32.8 us -> 38.5 us
  matrix products: 3.97 us -> 0 us
    all_to_all x4 -> x2, blocking collectives: 84.4 us -> 60.9 us  [swap(): return lax.all_to_all(x, axis, split_axis=0, concat_axis=0, tiled=True)]
    pallas_call x0 -> x11, Pallas kernels: none -> 14.9 us  [call(): pl.pallas_call(kernel, out_shape=shapes, in_specs=[SMEM] * smem + [VMEM]...]
    gather x7 -> x0, local copies, waits for them, and re-layouts: 12.2 us -> none  [the longest x1 4.08 us: local(): found = cold_table[asked].astype(jnp.bfloat16)]
    ppermute x0 -> x4, starting transfers between devices: none -> 12 us  [the longest x3 9.72 us: local(): lax.ppermute(grad, 'rep', [(i, i ^ d) for i in range(4)])]
    all_gather x1 -> x0, blocking collectives: 12 us -> none  [in_one_piece(): result = lax.all_gather(both, axis, axis=dim, tiled=True)]
    scatter-add x2 -> x0, other arithmetic: 10.6 us -> none  [the longest x1 7.08 us: local(): cold_grad = jnp.zeros((own_rows, width), jnp.float32).at[asked.reshape(-1...]
    all_to_all x6 -> x4, waiting for transfers between devices: 54.4 us -> 44.7 us  [swap(): return lax.all_to_all(x, axis, split_axis=0, concat_axis=0, tiled=True)]
    scatter x5 -> x0, local copies, waits for them, and re-layouts: 8.64 us -> none  [the longest x1 2.6 us: local(): jnp.zeros((owners_count * capacity,), jnp.int32).at[targets]]
  transfers between devices with their start and end apart: 6 -> 8, of which waited for: 5 -> 5; matrix products, arithmetic and copies ran while one was open for 16% -> 0% of each run, Pallas kernels for 0% -> 3%
where the time goes in v1:
time: 170 us
  blocking collectives  60.9 us (36%)
  waiting for transfers between devices  47.2 us (28%)
  starting transfers between devices  38.5 us (23%)
  Pallas kernels  14.9 us (9%)
  local copies, waits for them, and re-layouts  7.24 us (4%)
    all_to_all x2, blocking collectives, swap(): return lax.all_to_all(x, axis, split_axis=0, concat_axis=0, tiled=True)  60.9 us
    all_to_all x4, waiting for transfers between devices, swap(): return lax.all_to_all(x, axis, split_axis=0, concat_axis=0, tiled=True)  44.7 us
    all_to_all x4, starting transfers between devices, swap(): return lax.all_to_all(x, axis, split_axis=0, concat_axis=0, tiled=True)  26.5 us
    pallas_call x11, Pallas kernels, call(): pl.pallas_call(kernel, out_shape=shapes, in_specs=[SMEM] * smem + [VMEM]...  14.9 us
    ppermute x3, starting transfers between devices, local(): lax.ppermute(grad, 'rep', [(i, i ^ d) for i in range(4)])  9.72 us
    unnamed x40, local copies, waits for them, and re-layouts  7.24 us
  transfers between devices with their start and end apart: 8, of which 5 were waited for; matrix products, arithmetic and copies ran while one was open for 0% of the time, Pallas kernels for 3%

profile of v1, /device:TPU:1, one launch (start us, length us, event | category | flops | bytes accessed | tf_op | source)
XLA Modules:
  0.0 169.7 jit_solution(4736242367512768429)
XLA Ops:
  0.7 0.7 copy-done.18
  1.4 0.7 copy-done.19
  2.1 1.1 shard_map.180
  3.2 35.1 %all_to_all.30 = f32[128,1,128]{2,1,0:T(1,128)S(1)} all-to-all(f32[128,1,128]{2,1,0:T(1,128)S(1)} %bitcast.24), channel_id=1, replica_groups=mesh['dp_0'=16,'dp_1'=4,'dp_2'=2,'rep'=4] {'dp_0','dp_1','dp_2'}, dimensions={0} | all-to-all | bytes 131072 | tf_op jit(solution)/shard_map/all_to_all | solution.py:252
  38.3 0.9 copy-done.8
  39.2 2.1 %shard_map.182 = bf16[1024,128]{1,0:T(8,128)(2,1)} custom-call(f32[128,128]{1,0:T(8,128)S(1)} %bitcast.22, f32[512,128]{1,0:T(8,128)S(1)} %copy-done.8), custom_call_target="tpu_custom_call" | custom-call | flops 100000000 | bytes 1000000 | tf_op jit(solution)/shard_map/pallas_call | solution.py:27
  41.3 5.7 %all-to-all-start.1 = ((bf16[128,8,128]{2,1,0:T(8,128)(2,1)}), bf16[128,8,128]{2,1,0:T(8,128)(2,1)S(1)}, u32[]{:S(2)}, u32[]{:S(2)}) async-start(bf16[128,8,128]{2,1,0:T(8,128)(2,1)} %bitcast.6), calls=%async_computation.1 | async-start | bytes 524288 | tf_op jit(solution)/shard_map/all_to_all | solution.py:252
  47.1 0.7 copy-done.14
  47.7 1.7 shard_map.181
  49.4 1.0 copy-done.2
  50.4 1.0 copy-done.4
  51.4 1.0 copy-done.6
  52.4 15.3 %all-to-all-done.1 = bf16[128,8,128]{2,1,0:T(8,128)(2,1)S(1)} async-done(((bf16[128,8,128]{2,1,0:T(8,128)(2,1)}), bf16[128,8,128]{2,1,0:T(8,128)(2,1)S(1)}, u32[]{:S(2)}, u32[]{:S(2)}) %all-to-all-start.1) | async-done | bytes 262176 | tf_op jit(solution)/shard_map/all_to_all | solution.py:252
  67.7 1.2 copy-done.3
  68.9 3.0 %shard_map.183 = (bf16[1024,128]{1,0:T(8,128)(2,1)}, bf16[256,512]{1,0:T(8,128)(2,1)S(1)}, bf16[256,1024]{1,0:T(8,128)(2,1)S(1)}, bf16[512,128]{1,0:T(8,128)(2,1)S(1)}, f32[8,128]{1,0:T(8,128)S(1)}) custom-call(bf16[1024,128]{1,0:T(8,128)(2,1)S(1)} %bitcast.19, bf16[512,1024]{1,0:T(8,128)(2,1)S(1)} %get-tuple-element.32.take_ref, ...), custom_call_target="tpu_custom_call" | custom-call | flops 100000000 | bytes 1000000 | tf_op jit(solution)/shard_map/pallas_call | solution.py:27
  71.9 1.8 %shard_map.186 = (f32[256,1152]{1,0:T(8,128)S(1)}, f32[512,128]{1,0:T(8,128)S(1)}, f32[1024,128]{1,0:T(8,128)}) custom-call(s32[1]{0:T(128)} %bitcast.12.core_ref, s32[3]{0:T(128)S(1)} %copy-done.15, bf16[256,512]{1,0:T(8,128)(2,1)S(1)} %get-tuple-element.38.inputs_ref, bf16[256,1024]{1,0:T(8,128)(2,1)S(1)} %get-tuple-element.39.dhidden_ref, ...), custom_call_target="tpu_custom_call" | custom-call | flops 100000000 | bytes 1000000 | tf_op jit(solution)/shard_map/pallas_call | solution.py:27
  73.7 2.3 %collective-permute-start.3 = (f32[256,1152]{1,0:T(8,128)S(1)}, f32[256,1152]{1,0:T(8,128)S(1)}, u32[]{:S(2)}, u32[]{:S(2)}) collective-permute-start(f32[256,1152]{1,0:T(8,128)S(1)} %get-tuple-element.44), channel_id=1, source_target_pairs={{0,4},{4,0},{1,5},{5,1},{2,6},{6,2},{3,7},{7,3},{8,12},{12,8},{9,1... | collective-permute-start | bytes 3538952 | tf_op jit(solution)/shard_map/ppermute | solution.py:320
  76.1 2.5 %collective-permute-done.3.received_ref = f32[256,1152]{1,0:T(8,128)S(1)} collective-permute-done((f32[256,1152]{1,0:T(8,128)S(1)}, f32[256,1152]{1,0:T(8,128)S(1)}, u32[]{:S(2)}, u32[]{:S(2)}) %collective-permute-start.3) | collective-permute-done | bytes 1179680 | tf_op jit(solution)/shard_map/ppermute | solution.py:320
  79.1 25.8 %all_to_all.31.parts_ref = f32[16,16,1152]{2,1,0:T(8,128)S(1)} all-to-all(f32[16,16,1152]{2,1,0:T(8,128)S(1)} %bitcast.18), channel_id=1, replica_groups=mesh['dp_0'=16,'dp_1'=4,'dp_2'=2,'rep'=4] {'rep','dp_1'}, dimensions={0} | all-to-all | bytes 2359296 | tf_op jit(solution)/shard_map/all_to_all | solution.py:252
  105.0 6.9 %all-to-all-start.2 = ((bf16[128,8,128]{2,1,0:T(8,128)(2,1)}), bf16[128,8,128]{2,1,0:T(8,128)(2,1)S(1)}, u32[]{:S(2)}, u32[]{:S(2)}) async-start(bf16[128,8,128]{2,1,0:T(8,128)(2,1)} %bitcast.10), calls=%async_computation.2 | async-start | bytes 524288 | tf_op jit(solution)/shard_map/all_to_all | solution.py:252
  111.9 0.8 shard_map.188
  112.6 19.8 %all-to-all-done.2 = bf16[128,8,128]{2,1,0:T(8,128)(2,1)S(1)} async-done(((bf16[128,8,128]{2,1,0:T(8,128)(2,1)}), bf16[128,8,128]{2,1,0:T(8,128)(2,1)S(1)}, u32[]{:S(2)}, u32[]{:S(2)}) %all-to-all-start.2) | async-done | bytes 262176 | tf_op jit(solution)/shard_map/all_to_all | solution.py:252
  132.5 5.5 %all-to-all-start.4 = ((f32[16,24,128]{2,1,0:T(8,128)}), f32[16,24,128]{2,1,0:T(8,128)S(1)}, u32[]{:S(2)}, u32[]{:S(2)}) async-start(f32[16,24,128]{2,1,0:T(8,128)} %shard_map.188), calls=%async_computation.4 | async-start | bytes 393216 | tf_op jit(solution)/shard_map/all_to_all | solution.py:252
  138.5 2.1 %collective-permute-start = (f32[512,128]{1,0:T(8,128)S(1)}, f32[512,128]{1,0:T(8,128)S(1)}, u32[]{:S(2)}, u32[]{:S(2)}) collective-permute-start(f32[512,128]{1,0:T(8,128)S(1)} %shard_map.184.own_ref), channel_id=1, source_target_pairs={{0,1},{1,0},{2,3},{3,2},{4,5},{5,4},{6,7},{7,6},{8,9},{9,8},{10,11... | collective-permute-start | bytes 786440 | tf_op jit(solution)/shard_map/ppermute | solution.py:334
  140.5 3.7 %collective-permute-start.1 = (f32[512,128]{1,0:T(8,128)S(1)}, f32[512,128]{1,0:T(8,128)S(1)}, u32[]{:S(2)}, u32[]{:S(2)}) collective-permute-start(f32[512,128]{1,0:T(8,128)S(1)} %shard_map.184.own_ref), channel_id=1, source_target_pairs={{0,2},{1,3},{2,0},{3,1},{4,6},{5,7},{6,4},{7,5},{8,10},{9,11},{10,... | collective-permute-start | bytes 786440 | tf_op jit(solution)/shard_map/ppermute | solution.py:334
  144.2 4.0 %collective-permute-start.2 = (f32[512,128]{1,0:T(8,128)S(1)}, f32[512,128]{1,0:T(8,128)S(1)}, u32[]{:S(2)}, u32[]{:S(2)}) collective-permute-start(f32[512,128]{1,0:T(8,128)S(1)} %shard_map.184.own_ref), channel_id=1, source_target_pairs={{0,3},{1,2},{2,1},{3,0},{4,7},{5,6},{6,5},{7,4},{8,11},{9,10},{10,... | collective-permute-start | bytes 786440 | tf_op jit(solution)/shard_map/ppermute | solution.py:334
  148.2 2.3 %all-to-all-done.4.parts_ref = f32[16,24,128]{2,1,0:T(8,128)S(1)} async-done(((f32[16,24,128]{2,1,0:T(8,128)}), f32[16,24,128]{2,1,0:T(8,128)S(1)}, u32[]{:S(2)}, u32[]{:S(2)}) %all-to-all-start.4) | async-done | bytes 196640 | tf_op jit(solution)/shard_map/all_to_all | solution.py:252
  150.5 0.7 shard_map.189
  151.3 8.5 %all-to-all-start.5 = ((f32[32,16,128]{2,1,0:T(8,128)}), f32[32,16,128]{2,1,0:T(8,128)S(1)}, u32[]{:S(2)}, u32[]{:S(2)}) async-start(f32[32,16,128]{2,1,0:T(8,128)} %get-tuple-element.45), calls=%async_computation.5 | async-start | bytes 524288 | tf_op jit(solution)/shard_map/all_to_all | solution.py:252
  159.8 0.9 shard_map.185
  160.7 7.3 %all-to-all-done.5 = f32[32,16,128]{2,1,0:T(8,128)S(1)} async-done(((f32[32,16,128]{2,1,0:T(8,128)}), f32[32,16,128]{2,1,0:T(8,128)S(1)}, u32[]{:S(2)}, u32[]{:S(2)}) %all-to-all-start.5) | async-done | bytes 262176 | tf_op jit(solution)/shard_map/all_to_all | solution.py:252
  168.0 1.7 shard_map.190
  (37 shorter events, 1.1 us)
Async XLA Ops:
  0.6 46.4 %copy-start = (f32[1024,128]{1,0:T(8,128)S(1)}, f32[1024,128]{1,0:T(8,128)}, u32[]{:S(2)}) copy-start(f32[1024,128]{1,0:T(8,128)} %cache_ref.3) | copy-start | bytes 1572868
  0.6 0.7 copy-start.18
  1.4 0.7 copy-start.19
  2.1 65.6 %copy-start.1 = (bf16[512,1024]{1,0:T(8,128)(2,1)S(1)}, bf16[512,1024]{1,0:T(8,128)(2,1)}, u32[]{:S(2)}) copy-start(bf16[512,1024]{1,0:T(8,128)(2,1)} %weight_ref.1) | copy-start | bytes 3145732
  38.3 1.0 copy-start.8
  39.2 28.4 %copy-start.13 = (f32[1024]{0:T(1024)S(1)}, f32[1024]{0:T(1024)}, u32[]{:S(2)}) copy-start(f32[1024]{0:T(1024)} %param.18) | copy-start | bytes 12292
  39.2 28.4 %copy-start.16 = (s32[256]{0:T(256)S(1)}, s32[256]{0:T(256)}, u32[]{:S(2)}) copy-start(s32[256]{0:T(256)} %param.16) | copy-start | bytes 3076
  41.3 26.3 %all-to-all-start.1 = ((bf16[128,8,128]{2,1,0:T(8,128)(2,1)}), bf16[128,8,128]{2,1,0:T(8,128)(2,1)S(1)}, u32[]{:S(2)}, u32[]{:S(2)}) async-start(bf16[128,8,128]{2,1,0:T(8,128)(2,1)} %bitcast.6), calls=%async_computation.1 | async-start | bytes 524288 | tf_op jit(solution)/shard_map/all_to_all | solution.py:252
  47.0 0.7 copy-start.14
  49.4 1.0 copy-start.2
  50.4 1.0 copy-start.4
  51.4 1.0 copy-start.6
  67.6 1.2 copy-start.3
  68.9 3.0 %copy-start.7 = (bf16[1024,512]{1,0:T(8,128)(2,1)S(1)}, bf16[1024,512]{1,0:T(8,128)(2,1)}, u32[]{:S(2)}) copy-start(bf16[1024,512]{1,0:T(8,128)(2,1)} %copy-done.6) | copy-start | bytes 3145732
  68.9 3.0 %copy-start.11 = (f32[1024,128]{1,0:T(8,128)S(1)}, f32[1024,128]{1,0:T(8,128)}, u32[]{:S(2)}) copy-start(f32[1024,128]{1,0:T(8,128)} %pending_ref.1) | copy-start | bytes 1572868
  68.9 3.0 %copy-start.15 = (s32[3]{0:T(128)S(1)}, s32[3]{0:T(128)}, u32[]{:S(2)}) copy-start(s32[3]{0:T(128)} %refresh_ref.3) | copy-start | bytes 40
  73.7 4.8 %collective-permute-start.3 = (f32[256,1152]{1,0:T(8,128)S(1)}, f32[256,1152]{1,0:T(8,128)S(1)}, u32[]{:S(2)}, u32[]{:S(2)}) collective-permute-start(f32[256,1152]{1,0:T(8,128)S(1)} %get-tuple-element.44), channel_id=1, source_target_pairs={{0,4},{4,0},{1,5},{5,1},{2,6},{6,2},{3,7},{7,3},{8,12},{12,8},{9,1... | collective-permute-start | bytes 3538952 | tf_op jit(solution)/shard_map/ppermute | solution.py:320
  105.0 33.0 %copy-start.5 = (bf16[512,1024]{1,0:T(8,128)(2,1)S(1)}, bf16[512,1024]{1,0:T(8,128)(2,1)}, u32[]{:S(2)}) copy-start(bf16[512,1024]{1,0:T(8,128)(2,1)} %copy-done.4) | copy-start | bytes 3145732
  105.0 27.5 %all-to-all-start.2 = ((bf16[128,8,128]{2,1,0:T(8,128)(2,1)}), bf16[128,8,128]{2,1,0:T(8,128)(2,1)S(1)}, u32[]{:S(2)}, u32[]{:S(2)}) async-start(bf16[128,8,128]{2,1,0:T(8,128)(2,1)} %bitcast.10), calls=%async_computation.2 | async-start | bytes 524288 | tf_op jit(solution)/shard_map/all_to_all | solution.py:252
  132.5 18.1 %all-to-all-start.4 = ((f32[16,24,128]{2,1,0:T(8,128)}), f32[16,24,128]{2,1,0:T(8,128)S(1)}, u32[]{:S(2)}, u32[]{:S(2)}) async-start(f32[16,24,128]{2,1,0:T(8,128)} %shard_map.188), calls=%async_computation.4 | async-start | bytes 393216 | tf_op jit(solution)/shard_map/all_to_all | solution.py:252
  138.0 21.8 %copy-start.9 = (f32[512,128]{1,0:T(8,128)S(1)}, f32[512,128]{1,0:T(8,128)}, u32[]{:S(2)}) copy-start(f32[512,128]{1,0:T(8,128)} %table_ref.3) | copy-start | bytes 786436
  138.0 21.8 %copy-start.12 = (f32[512,128]{1,0:T(8,128)S(1)}, f32[512,128]{1,0:T(8,128)}, u32[]{:S(2)}) copy-start(f32[512,128]{1,0:T(8,128)} %accum_ref.2) | copy-start | bytes 786436
  138.4 29.6 %copy-start.10 = (f32[1024,128]{1,0:T(8,128)S(1)}, f32[1024,128]{1,0:T(8,128)}, u32[]{:S(2)}) copy-start(f32[1024,128]{1,0:T(8,128)} %accum_ref.3) | copy-start | bytes 1572868
  138.5 29.6 %copy-start.17 = (s32[8]{0:T(128)S(1)}, s32[8]{0:T(128)}, u32[]{:S(2)}) copy-start(s32[8]{0:T(128)} %clock_ref.1) | copy-start | bytes 100
  138.5 21.3 %collective-permute-start = (f32[512,128]{1,0:T(8,128)S(1)}, f32[512,128]{1,0:T(8,128)S(1)}, u32[]{:S(2)}, u32[]{:S(2)}) collective-permute-start(f32[512,128]{1,0:T(8,128)S(1)} %shard_map.184.own_ref), channel_id=1, source_target_pairs={{0,1},{1,0},{2,3},{3,2},{4,5},{5,4},{6,7},{7,6},{8,9},{9,8},{10,11... | collective-permute-start | bytes 786440 | tf_op jit(solution)/shard_map/ppermute | solution.py:334
  140.5 19.2 %collective-permute-start.1 = (f32[512,128]{1,0:T(8,128)S(1)}, f32[512,128]{1,0:T(8,128)S(1)}, u32[]{:S(2)}, u32[]{:S(2)}) collective-permute-start(f32[512,128]{1,0:T(8,128)S(1)} %shard_map.184.own_ref), channel_id=1, source_target_pairs={{0,2},{1,3},{2,0},{3,1},{4,6},{5,7},{6,4},{7,5},{8,10},{9,11},{10,... | collective-permute-start | bytes 786440 | tf_op jit(solution)/shard_map/ppermute | solution.py:334
  144.2 15.6 %collective-permute-start.2 = (f32[512,128]{1,0:T(8,128)S(1)}, f32[512,128]{1,0:T(8,128)S(1)}, u32[]{:S(2)}, u32[]{:S(2)}) collective-permute-start(f32[512,128]{1,0:T(8,128)S(1)} %shard_map.184.own_ref), channel_id=1, source_target_pairs={{0,3},{1,2},{2,1},{3,0},{4,7},{5,6},{6,5},{7,4},{8,11},{9,10},{10,... | collective-permute-start | bytes 786440 | tf_op jit(solution)/shard_map/ppermute | solution.py:334
  151.3 16.7 %all-to-all-start.5 = ((f32[32,16,128]{2,1,0:T(8,128)}), f32[32,16,128]{2,1,0:T(8,128)S(1)}, u32[]{:S(2)}, u32[]{:S(2)}) async-start(f32[32,16,128]{2,1,0:T(8,128)} %get-tuple-element.45), calls=%async_computation.5 | async-start | bytes 524288 | tf_op jit(solution)/shard_map/all_to_all | solution.py:252

commit v2 on v1

--- a/solution.py
+++ b/solution.py
@@ -30,7 +30,7 @@
         in_specs=[SMEM] * smem + [VMEM] * (len(args) - smem),
         out_specs=[VMEM] * len(outs),
         scratch_shapes=[pltpu.VMEM(s, d) for s, d in scratch],
-        compiler_params=pltpu.CompilerParams(vmem_limit_bytes=40 * 2**20),
+        compiler_params=pltpu.CompilerParams(vmem_limit_bytes=16 * 2**20),
         cost_estimate=pl.CostEstimate(flops=flops, bytes_accessed=moved, transcendentals=0),
     )(*args)
 
@@ -81,16 +81,26 @@
     request_ref[...] = dot(named_t, placed, EXACT)
 
 
-def rows_kernel(asked_ref, table_ref, rows_ref):
-    count = rows_ref.shape[0]
-    row, lane = iota((count, BLOCK), 0), iota((count, BLOCK), 1)
-    spread = dot(jnp.where(row // SLOTS == lane, 1.0, 0.0), asked_ref[...], EXACT)
-    wanted = jnp.sum(jnp.where(row % SLOTS == lane, spread, 0.0), axis=1, keepdims=True)
-    chosen = ones_where(wanted == iota_f((count, table_ref.shape[0]), 1))
-    rows_ref[...] = dot(chosen, table_ref[...].astype(BF16)).astype(BF16)
-
-
-def masks_kernel(target_ref, hot_ref, cache_ref, asked_ref, take_ref, put_ref, hot_in_ref, hot_put_ref, owned_ref):
+def rows_kernel(asked_ref, table_ref, rows_ref, wide_ref):
+    asked = asked_ref[...]
+    table = table_ref[...]
+    sources = asked.shape[0]
+    line = iota_f((sources, table.shape[0]), 1)
+    for slot in range(SLOTS):
+        chosen = ones_where(asked[:, slot : slot + 1] == line)
+        wide_ref[pl.ds(slot, sources, stride=SLOTS), :] = dot(chosen, table)
+    rows_ref[...] = wide_ref[...].astype(BF16)
+
+
+def owned_kernel(asked_ref, owned_ref):
+    slots = owned_ref.shape[1]
+    source, line = iota((BLOCK, slots), 0), iota((BLOCK, slots), 1)
+    spread = dot(asked_ref[...], jnp.where(source == line % SLOTS, 1.0, 0.0), EXACT)
+    wanted = jnp.sum(jnp.where(source == line // SLOTS, spread, 0.0), axis=0, keepdims=True)
+    owned_ref[...] = ones_where(iota_f(owned_ref.shape, 0) == wanted)
+
+
+def masks_kernel(target_ref, hot_ref, cache_ref, table_ref, take_ref, put_ref, hot_in_ref, hot_put_ref, narrow_ref):
     square = (BLOCK, BLOCK)
     eye = iota(square, 0) == iota(square, 1)
     slots, lookups = put_ref.shape
@@ -120,10 +130,7 @@
             hot_put_ref[:, at : at + BLOCK] = ones_where(hot_row == row)
             chosen = ones_where(column_of(row, eye) == hot_lane)
             hot_in_ref[h * BLOCK : (h + 1) * BLOCK, k * BLOCK : (k + 1) * BLOCK] = dot(chosen, cache).astype(BF16)
-    source, line = iota((BLOCK, slots), 0), iota((BLOCK, slots), 1)
-    spread = dot(asked_ref[...], jnp.where(source == line % SLOTS, 1.0, 0.0), EXACT)
-    wanted = jnp.sum(jnp.where(source == line // SLOTS, spread, 0.0), axis=0, keepdims=True)
-    owned_ref[...] = ones_where(iota_f(owned_ref.shape, 0) == wanted)
+    narrow_ref[...] = table_ref[...].astype(BF16)
 
 
 def layer_kernel(
@@ -159,16 +166,21 @@
         head_ref[b : b + 1, :] = head[:, b * BLOCK : (b + 1) * BLOCK]
 
 
-def half_of_top(core, inputs, dhidden):
+def half_of_top(core, rep, inputs, dhidden):
     shape = (inputs.shape[1] // 2, inputs.shape[1])
     line = iota(shape, 0)
-    row = (line & 15) * 32 + ((line >> 4) & 3) * 8 + core * 4 + (line >> 6)
+    row = (line & 15) * 32 + ((line >> 4) & 3) * 8 + core * 4 + ((line >> 6) ^ rep)
     ordered = dot_t(ones_where(row == iota(shape, 1)), inputs).astype(BF16)
     return dot(ordered, dhidden)
 
 
+def hot_rows(picked_ref, core, rep, piece):
+    count = picked_ref.shape[0] // 8
+    return picked_ref[pl.ds(pl.multiple_of((core * 4 + (rep ^ piece)) * count, count), count), :]
+
+
 def send_kernel(
-    core_ref, refresh_ref, inputs_ref, dhidden_ref, hot_put_ref, hot_dx_ref, head_ref, pending_ref,
+    place_ref, refresh_ref, inputs_ref, dhidden_ref, hot_put_ref, hot_dx_ref, head_ref, pending_ref,
     send_ref, picked_ref, pending_new_ref,
 ):
     pending_new_ref[...] = pending_ref[...] + dot(hot_put_ref[...], hot_dx_ref[...])
@@ -181,19 +193,27 @@
     picked_ref[end + 8 :, :] = jnp.zeros((picked_ref.shape[0] - end - 8, BLOCK), F32)
     for at in blocks:
         pending_new_ref[at, :] = jnp.zeros((BLOCK, BLOCK), F32)
-    other = 1 - core_ref[0]
+    core, rep = 1 - place_ref[0], place_ref[1]
     wide = dhidden_ref.shape[1]
-    half = send_ref.shape[0]
-    send_ref[:, :wide] = half_of_top(other, inputs_ref[...], dhidden_ref[...])
-    send_ref[:, wide:] = picked_ref[pl.ds(pl.multiple_of(other * half, half), half), :]
-
-
-def pair_kernel(core_ref, inputs_ref, dhidden_ref, picked_ref, received_ref, sum_ref):
-    mine = core_ref[0]
+    tall = send_ref.shape[0] // 4
+    send_ref[:, :wide] = half_of_top(core, rep, inputs_ref[...], dhidden_ref[...])
+    for d in range(4):
+        send_ref[d * tall : (d + 1) * tall, wide:] = hot_rows(picked_ref, core, rep, d)
+
+
+def pair_kernel(place_ref, inputs_ref, dhidden_ref, picked_ref, received_ref, *pieces):
+    core, rep = place_ref[0], place_ref[1]
     wide = dhidden_ref.shape[1]
-    half = sum_ref.shape[0]
-    sum_ref[:, :wide] = half_of_top(mine, inputs_ref[...], dhidden_ref[...]) + received_ref[:, :wide]
-    sum_ref[:, wide:] = picked_ref[pl.ds(pl.multiple_of(mine * half, half), half), :] + received_ref[:, wide:]
+    top = half_of_top(core, rep, inputs_ref[...], dhidden_ref[...])
+    tall = pieces[0].shape[0]
+    for d, piece in enumerate(pieces):
+        rows = slice(d * tall, (d + 1) * tall)
+        piece[:, :wide] = top[rows] + received_ref[rows, :wide]
+        piece[:, wide:] = hot_rows(picked_ref, core, rep, d) + received_ref[rows, wide:]
+
+
+def four_kernel(own_ref, one_ref, two_ref, three_ref, sum_ref):
+    sum_ref[...] = (own_ref[...] + one_ref[...]) + (two_ref[...] + three_ref[...])
 
 
 def plane_kernel(parts_ref, out_ref):
@@ -250,6 +270,10 @@
 
 def swap(x, axis):
     return lax.all_to_all(x, axis, split_axis=0, concat_axis=0, tiled=True)
+
+
+def from_others(pieces):
+    return [lax.ppermute(p, "rep", [(i, i ^ d) for i in range(4)]) for d, p in enumerate(pieces, 1)]
 
 
 def local(
@@ -275,7 +299,7 @@
     owners = lax.axis_size(DP)
     slots = owners * SLOTS
     groups = lookups // BLOCK
-    core = lax.axis_index("dp_2").astype(jnp.int32).reshape(1)
+    place = jnp.stack([lax.axis_index("dp_2"), lax.axis_index("rep")]).astype(jnp.int32)
 
     request, target = call(
         requests_kernel,
@@ -283,19 +307,20 @@
         (cold_owner.reshape(groups, BLOCK), cold_offset.reshape(groups, BLOCK)),
     )
     asked = swap(request.reshape(owners, 1, BLOCK), DP).reshape(owners, BLOCK)
-    (found,) = call(rows_kernel, [((slots, width), BF16)], (asked, cold_table))
-    returned = swap(found.reshape(owners, SLOTS, width), DP).reshape(slots, width)
-    take, put, hot_in, hot_put, owned = call(
+    take, put, hot_in, hot_put, narrow = call(
         masks_kernel,
         [
             ((lookups, slots), BF16),
             ((slots, lookups), BF16),
             ((samples, feats * width), BF16),
             ((hot_count, samples * feats), BF16),
-            ((own_rows, slots), BF16),
+            ((own_rows, width), BF16),
         ],
-        (target, hot_ids.T, hot_cache, asked),
-    )
+        (target, hot_ids.T, hot_cache, cold_table),
+    )
+    (found,) = call(rows_kernel, [((slots, width), BF16)], (asked, narrow), scratch=[((slots, width), F32)])
+    returned = swap(found.reshape(owners, SLOTS, width), DP).reshape(slots, width)
+    (owned,) = call(owned_kernel, [((own_rows, slots), BF16)], (asked,))
     outgoing, inputs, dhidden, hot_dx, head = call(
         layer_kernel,
         [
@@ -314,24 +339,29 @@
     send, picked, pending_new = call(
         send_kernel,
         [((half, broad), F32), ((inputs_width, BLOCK), F32), ((hot_count, width), F32)],
-        (core, refresh_blocks, inputs, dhidden, hot_put, hot_dx, head, pending),
+        (place, refresh_blocks, inputs, dhidden, hot_put, hot_dx, head, pending),
         smem=2,
     )
     received = lax.ppermute(send, "dp_2", [(0, 1), (1, 0)])
-    (paired,) = call(pair_kernel, [((half, broad), F32)], (core, inputs, dhidden, picked, received), smem=1)
-    near = lax.axis_size(("rep", "dp_1"))
+    pieces = call(
+        pair_kernel, [((half // 4, broad), F32)] * 4, (place, inputs, dhidden, picked, received), smem=1
+    )
+    (paired,) = call(four_kernel, [((half // 4, broad), F32)], (pieces[0], *from_others(pieces[1:])))
+    paired, incoming = lax.optimization_barrier((paired, incoming))
+    near = lax.axis_size("dp_1")
     far = lax.axis_size("dp_0")
-    plane = swap(paired.reshape(near, far, broad), ("rep", "dp_1"))
+    plane_size = lax.axis_size(PLANE)
+    plane = swap(paired.reshape(near, far, broad), "dp_1")
     tall = hidden_width // BLOCK
     (columns,) = call(plane_kernel, [((far, tall + far, BLOCK), F32)], (plane,))
     columns = swap(columns, "dp_0")
     top, copies = call(
-        column_kernel, [((tall, BLOCK), F32), ((2 * near, far, BLOCK), F32)], (columns,)
-    )
-    sums = swap(copies, PLANE).reshape(2 * near * far, BLOCK)
+        column_kernel, [((tall, BLOCK), F32), ((plane_size, far, BLOCK), F32)], (columns,)
+    )
+    sums = swap(copies, PLANE).reshape(plane_size * far, BLOCK)
 
     (grad,) = call(cold_kernel, [((own_rows, width), F32)], (owned, incoming))
-    others = [lax.ppermute(grad, "rep", [(i, i ^ d) for i in range(4)]) for d in (1, 2, 3)]
+    others = from_others([grad] * 3)
     cold_table_new, cold_accum_new = call(
         update_kernel, [((own_rows, width), F32)] * 2, (grad, *others, cold_table, cold_accum)
     )

time: 170 us -> 167 us (0.982)
  blocking collectives: 60.9 us -> 10.3 us
  starting transfers between devices: 38.5 us -> 78.3 us
  waiting for transfers between devices: 47.2 us -> 52.7 us
    all_to_all x2 -> x1, blocking collectives: 60.9 us -> 10.3 us  [swap(): return lax.all_to_all(x, axis, split_axis=0, concat_axis=0, tiled=True)]
    all_to_all x4 -> x5, starting transfers between devices: 26.5 us -> 56.3 us  [swap(): return lax.all_to_all(x, axis, split_axis=0, concat_axis=0, tiled=True)]
    ppermute x3 -> x6, waiting for transfers between devices: 0.01 us -> 14.8 us  [from_others(): lax.ppermute(p, 'rep', [(i, i ^ d) for i in range(4)])]
    ppermute x3 -> x6, starting transfers between devices: 9.72 us -> 19.5 us  [from_others(): lax.ppermute(p, 'rep', [(i, i ^ d) for i in range(4)])]
    all_to_all x4 -> x5, waiting for transfers between devices: 44.7 us -> 37.9 us  [swap(): return lax.all_to_all(x, axis, split_axis=0, concat_axis=0, tiled=True)]
    ppermute x1, waiting for transfers between devices: 2.45 us -> 0.01 us  [local(): received = lax.ppermute(send, 'dp_2', [(0, 1), (1, 0)])]
    pallas_call x11 -> x13, Pallas kernels: 14.9 us -> 16.1 us  [call(): pl.pallas_call(kernel, out_shape=shapes, in_specs=[SMEM] * smem + [VMEM]...]
    unnamed x40 -> x38, local copies, waits for them, and re-layouts: 7.24 us -> 7.25 us
  transfers between devices with their start and end apart: 8 -> 12, of which waited for: 5 -> 6; matrix products, arithmetic and copies ran while one was open for 0% -> 0% of each run, Pallas kernels for 3% -> 3%
where the time goes in v2:
time: 167 us; the launch traced here: 166 us
  starting transfers between devices  78.3 us (47%)
  waiting for transfers between devices  52.7 us (32%)
  Pallas kernels  16.1 us (10%)
  blocking collectives  10.3 us (6%)
  local copies, waits for them, and re-layouts  7.25 us (4%)
    all_to_all x5, starting transfers between devices, swap(): return lax.all_to_all(x, axis, split_axis=0, concat_axis=0, tiled=True)  56.3 us
    all_to_all x5, waiting for transfers between devices, swap(): return lax.all_to_all(x, axis, split_axis=0, concat_axis=0, tiled=True)  37.9 us
    ppermute x6, starting transfers between devices, from_others(): lax.ppermute(p, 'rep', [(i, i ^ d) for i in range(4)])  19.5 us
    pallas_call x13, Pallas kernels, call(): pl.pallas_call(kernel, out_shape=shapes, in_specs=[SMEM] * smem + [VMEM]...  16.1 us
    ppermute x6, waiting for transfers between devices, from_others(): lax.ppermute(p, 'rep', [(i, i ^ d) for i in range(4)])  14.8 us
    all_to_all x1, blocking collectives, swap(): return lax.all_to_all(x, axis, split_axis=0, concat_axis=0, tiled=True)  10.3 us
    unnamed x38, local copies, waits for them, and re-layouts  7.25 us
  transfers between devices with their start and end apart: 12, of which 6 were waited for; matrix products, arithmetic and copies ran while one was open for 0% of the time, Pallas kernels for 3%

profile of v2, /device:TPU:1, one launch (start us, length us, event | category | flops | bytes accessed | tf_op | source)
XLA Modules:
  0.0 165.7 jit_solution(5017102527812178826)
XLA Ops:
  2.0 1.7 %shard_map.180 = (f32[128,128]{1,0:T(8,128)}, f32[512,128]{1,0:T(8,128)S(1)}) custom-call(s32[4,128]{1,0:T(4,128)S(1)} %bitcast.28, s32[4,128]{1,0:T(4,128)S(1)} %bitcast.29), custom_call_target="tpu_custom_call" | custom-call | flops 100000000 | bytes 1000000 | tf_op jit(solution)/shard_map/pallas_call | solution.py:27
  3.7 20.5 %all-to-all-start = ((f32[128,1,128]{2,1,0:T(1,128)}), f32[128,1,128]{2,1,0:T(1,128)S(1)}, u32[]{:S(2)}, u32[]{:S(2)}) async-start(f32[128,1,128]{2,1,0:T(1,128)} %bitcast.3), calls=%async_computation | async-start | bytes 131072 | tf_op jit(solution)/shard_map/all_to_all | solution.py:272
  24.3 1.0 copy-done
  25.3 0.9 copy-done.7
  26.9 1.3 shard_map.182
  28.2 1.0 copy-done.3
  29.2 1.0 copy-done.5
  30.2 8.9 %all-to-all-done = f32[128,1,128]{2,1,0:T(1,128)S(1)} async-done(((f32[128,1,128]{2,1,0:T(1,128)}), f32[128,1,128]{2,1,0:T(1,128)S(1)}, u32[]{:S(2)}, u32[]{:S(2)}) %all-to-all-start) | async-done | bytes 65568 | tf_op jit(solution)/shard_map/all_to_all | solution.py:272
  39.1 1.2 shard_map.183
  40.3 7.2 %all-to-all-start.1 = ((bf16[128,8,128]{2,1,0:T(8,128)(2,1)}), bf16[128,8,128]{2,1,0:T(8,128)(2,1)S(1)}, u32[]{:S(2)}, u32[]{:S(2)}) async-start(bf16[128,8,128]{2,1,0:T(8,128)(2,1)} %bitcast.8), calls=%async_computation.1 | async-start | bytes 524288 | tf_op jit(solution)/shard_map/all_to_all | solution.py:272
  47.6 20.4 %all-to-all-done.1 = bf16[128,8,128]{2,1,0:T(8,128)(2,1)S(1)} async-done(((bf16[128,8,128]{2,1,0:T(8,128)(2,1)}), bf16[128,8,128]{2,1,0:T(8,128)(2,1)S(1)}, u32[]{:S(2)}, u32[]{:S(2)}) %all-to-all-start.1) | async-done | bytes 262176 | tf_op jit(solution)/shard_map/all_to_all | solution.py:272
  68.0 1.2 copy-done.4
  69.2 3.0 %shard_map.184 = (bf16[1024,128]{1,0:T(8,128)(2,1)}, bf16[256,512]{1,0:T(8,128)(2,1)S(1)}, bf16[256,1024]{1,0:T(8,128)(2,1)S(1)}, bf16[512,128]{1,0:T(8,128)(2,1)S(1)}, f32[8,128]{1,0:T(8,128)S(1)}) custom-call(bf16[1024,128]{1,0:T(8,128)(2,1)S(1)} %bitcast.20, bf16[512,1024]{1,0:T(8,128)(2,1)S(1)} %get-tuple-element.38.take_ref, ...), custom_call_target="tpu_custom_call" | custom-call | flops 100000000 | bytes 1000000 | tf_op jit(solution)/shard_map/pallas_call | solution.py:27
  72.3 2.4 %shard_map.185 = (f32[256,1152]{1,0:T(8,128)}, f32[512,128]{1,0:T(8,128)S(1)}, f32[1024,128]{1,0:T(8,128)}) custom-call(s32[2]{0:T(128)S(1)} %pad_add_fusion.place_ref, s32[3]{0:T(128)S(1)} %copy-done.14, bf16[256,512]{1,0:T(8,128)(2,1)S(1)} %get-tuple-element.41.inputs_ref, bf16[256,1024]{1,0:T(8,128)(2,1)S(1)} %get-tuple-element.42.dhidden_ref, ...), custom_call_target="tpu_custom_call" | custom-call | flops 100000000 | bytes 1000000 | tf_op jit(solution)/shard_map/pallas_call | solution.py:27
  74.7 2.5 %collective-permute-start = (f32[256,1152]{1,0:T(8,128)}, f32[256,1152]{1,0:T(8,128)S(1)}, u32[]{:S(2)}, u32[]{:S(2)}) collective-permute-start(f32[256,1152]{1,0:T(8,128)} %get-tuple-element.47), channel_id=1, source_target_pairs={{0,4},{4,0},{1,5},{5,1},{2,6},{6,2},{3,7},{7,3},{8,12},{12,8},{9,1... | collective-permute-start | bytes 3538952 | tf_op jit(solution)/shard_map/ppermute | solution.py:345
  77.2 7.9 %all-to-all-start.2 = ((bf16[128,8,128]{2,1,0:T(8,128)(2,1)}), bf16[128,8,128]{2,1,0:T(8,128)(2,1)S(1)}, u32[]{:S(2)}, u32[]{:S(2)}) async-start(bf16[128,8,128]{2,1,0:T(8,128)(2,1)} %bitcast.12), calls=%async_computation.2 | async-start | bytes 524288 | tf_op jit(solution)/shard_map/all_to_all | solution.py:272
  85.1 1.1 shard_map.186
  86.2 3.2 %collective-permute-start.1 = (f32[64,1152]{1,0:T(8,128)S(1)}, f32[64,1152]{1,0:T(8,128)S(1)}, u32[]{:S(2)}, u32[]{:S(2)}) collective-permute-start(f32[64,1152]{1,0:T(8,128)S(1)} %get-tuple-element.49), channel_id=1, source_target_pairs={{0,1},{1,0},{2,3},{3,2},{4,5},{5,4},{6,7},{7,6},{8,9},{9,8},{10,11... | collective-permute-start | bytes 884744 | tf_op jit(solution)/shard_map/ppermute | solution.py:276
  89.4 4.5 %collective-permute-start.2 = (f32[64,1152]{1,0:T(8,128)S(1)}, f32[64,1152]{1,0:T(8,128)S(1)}, u32[]{:S(2)}, u32[]{:S(2)}) collective-permute-start(f32[64,1152]{1,0:T(8,128)S(1)} %get-tuple-element.50), channel_id=1, source_target_pairs={{0,2},{1,3},{2,0},{3,1},{4,6},{5,7},{6,4},{7,5},{8,10},{9,11},{10,... | collective-permute-start | bytes 884744 | tf_op jit(solution)/shard_map/ppermute | solution.py:276
  94.0 2.1 %collective-permute-start.3 = (f32[64,1152]{1,0:T(8,128)S(1)}, f32[64,1152]{1,0:T(8,128)S(1)}, u32[]{:S(2)}, u32[]{:S(2)}) collective-permute-start(f32[64,1152]{1,0:T(8,128)S(1)} %get-tuple-element.51), channel_id=1, source_target_pairs={{0,3},{1,2},{2,1},{3,0},{4,7},{5,6},{6,5},{7,4},{8,11},{9,10},{10,... | collective-permute-start | bytes 884744 | tf_op jit(solution)/shard_map/ppermute | solution.py:276
  96.1 8.5 %collective-permute-done.2.two_ref = f32[64,1152]{1,0:T(8,128)S(1)} collective-permute-done((f32[64,1152]{1,0:T(8,128)S(1)}, f32[64,1152]{1,0:T(8,128)S(1)}, u32[]{:S(2)}, u32[]{:S(2)}) %collective-permute-start.2) | collective-permute-done | bytes 294944 | tf_op jit(solution)/shard_map/ppermute | solution.py:276
  104.6 6.3 %collective-permute-done.3.three_ref = f32[64,1152]{1,0:T(8,128)S(1)} collective-permute-done((f32[64,1152]{1,0:T(8,128)S(1)}, f32[64,1152]{1,0:T(8,128)S(1)}, u32[]{:S(2)}, u32[]{:S(2)}) %collective-permute-start.3) | collective-permute-done | bytes 294944 | tf_op jit(solution)/shard_map/ppermute | solution.py:276
  110.9 10.3 %all_to_all.30.parts_ref = f32[4,16,1152]{2,1,0:T(8,128)S(1)} all-to-all(f32[4,16,1152]{2,1,0:T(8,128)S(1)} %bitcast.19), channel_id=1, replica_groups=mesh['dp_0'=16,'dp_1'=4,'dp_2'=2,'rep'=4] {'dp_1'}, dimensions={0} | all-to-all | bytes 589824 | tf_op jit(solution)/shard_map/all_to_all | solution.py:272
  122.0 11.6 %all-to-all-start.4 = ((f32[16,24,128]{2,1,0:T(8,128)}), f32[16,24,128]{2,1,0:T(8,128)S(1)}, u32[]{:S(2)}, u32[]{:S(2)}) async-start(f32[16,24,128]{2,1,0:T(8,128)} %shard_map.190), calls=%async_computation.4 | async-start | bytes 393216 | tf_op jit(solution)/shard_map/all_to_all | solution.py:272
  134.9 2.1 %collective-permute-start.4 = (f32[512,128]{1,0:T(8,128)S(1)}, f32[512,128]{1,0:T(8,128)S(1)}, u32[]{:S(2)}, u32[]{:S(2)}) collective-permute-start(f32[512,128]{1,0:T(8,128)S(1)} %shard_map.188.own_ref), channel_id=1, source_target_pairs={{0,1},{1,0},{2,3},{3,2},{4,5},{5,4},{6,7},{7,6},{8,9},{9,8},{10,11... | collective-permute-start | bytes 786440 | tf_op jit(solution)/shard_map/ppermute | solution.py:276
  136.9 3.1 %collective-permute-start.5 = (f32[512,128]{1,0:T(8,128)S(1)}, f32[512,128]{1,0:T(8,128)S(1)}, u32[]{:S(2)}, u32[]{:S(2)}) collective-permute-start(f32[512,128]{1,0:T(8,128)S(1)} %shard_map.188.own_ref), channel_id=1, source_target_pairs={{0,2},{1,3},{2,0},{3,1},{4,6},{5,7},{6,4},{7,5},{8,10},{9,11},{10,... | collective-permute-start | bytes 786440 | tf_op jit(solution)/shard_map/ppermute | solution.py:276
  140.0 4.6 %collective-permute-start.6 = (f32[512,128]{1,0:T(8,128)S(1)}, f32[512,128]{1,0:T(8,128)S(1)}, u32[]{:S(2)}, u32[]{:S(2)}) collective-permute-start(f32[512,128]{1,0:T(8,128)S(1)} %shard_map.188.own_ref), channel_id=1, source_target_pairs={{0,3},{1,2},{2,1},{3,0},{4,7},{5,6},{6,5},{7,4},{8,11},{9,10},{10,... | collective-permute-start | bytes 786440 | tf_op jit(solution)/shard_map/ppermute | solution.py:276
  144.6 1.4 all-to-all-done.4.parts_ref
  146.7 9.1 %all-to-all-start.5 = ((f32[32,16,128]{2,1,0:T(8,128)}), f32[32,16,128]{2,1,0:T(8,128)S(1)}, u32[]{:S(2)}, u32[]{:S(2)}) async-start(f32[32,16,128]{2,1,0:T(8,128)} %get-tuple-element.57), calls=%async_computation.5 | async-start | bytes 524288 | tf_op jit(solution)/shard_map/all_to_all | solution.py:272
  155.8 0.9 shard_map.189
  156.7 7.3 %all-to-all-done.5 = f32[32,16,128]{2,1,0:T(8,128)S(1)} async-done(((f32[32,16,128]{2,1,0:T(8,128)}), f32[32,16,128]{2,1,0:T(8,128)S(1)}, u32[]{:S(2)}, u32[]{:S(2)}) %all-to-all-start.5) | async-done | bytes 262176 | tf_op jit(solution)/shard_map/all_to_all | solution.py:272
  164.0 1.7 %shard_map.192 = (f32[1024,128]{1,0:T(8,128)}, f32[1024,128]{1,0:T(8,128)}, f32[8,128]{1,0:T(8,128)}) custom-call(s32[3]{0:T(128)S(1)} %copy-done.14, s32[8]{0:T(128)S(1)} %copy-done.16, f32[512,128]{1,0:T(8,128)S(1)} %bitcast.22, f32[1024,128]{1,0:T(8,128)S(1)} %copy-done.1, f32[1024,128]{1,0:T(8,128)S(1)} %copy-done.9), custom_call_target="tpu_custom_call" | custom-call | flops 100000000 | bytes 1000000 | tf_op jit(solution)/shard_map/pallas_call | solution.py:27
  (45 shorter events, 4.9 us)
Async XLA Ops:
  0.6 0.7 copy-start.17
  1.3 0.7 copy-start.18
  3.7 64.3 %copy-start.12 = (f32[1024]{0:T(1024)S(1)}, f32[1024]{0:T(1024)}, u32[]{:S(2)}) copy-start(f32[1024]{0:T(1024)} %param.18) | copy-start | bytes 12292
  3.7 64.3 %copy-start.15 = (s32[256]{0:T(256)S(1)}, s32[256]{0:T(256)}, u32[]{:S(2)}) copy-start(s32[256]{0:T(256)} %param.16) | copy-start | bytes 3076
  3.7 35.4 %all-to-all-start = ((f32[128,1,128]{2,1,0:T(1,128)}), f32[128,1,128]{2,1,0:T(1,128)S(1)}, u32[]{:S(2)}, u32[]{:S(2)}) async-start(f32[128,1,128]{2,1,0:T(1,128)} %bitcast.3), calls=%async_computation | async-start | bytes 131072 | tf_op jit(solution)/shard_map/all_to_all | solution.py:272
  24.3 1.0 copy-start
  25.3 0.9 copy-start.7
  26.3 0.7 copy-start.13
  26.9 41.1 %copy-start.2 = (bf16[512,1024]{1,0:T(8,128)(2,1)S(1)}, bf16[512,1024]{1,0:T(8,128)(2,1)}, u32[]{:S(2)}) copy-start(bf16[512,1024]{1,0:T(8,128)(2,1)} %weight_ref.1) | copy-start | bytes 3145732
  28.2 1.0 copy-start.3
  29.2 1.0 copy-start.5
  40.3 27.7 %all-to-all-start.1 = ((bf16[128,8,128]{2,1,0:T(8,128)(2,1)}), bf16[128,8,128]{2,1,0:T(8,128)(2,1)S(1)}, u32[]{:S(2)}, u32[]{:S(2)}) async-start(bf16[128,8,128]{2,1,0:T(8,128)(2,1)} %bitcast.8), calls=%async_computation.1 | async-start | bytes 524288 | tf_op jit(solution)/shard_map/all_to_all | solution.py:272
  68.0 1.2 copy-start.4
  69.2 3.0 %copy-start.6 = (bf16[1024,512]{1,0:T(8,128)(2,1)S(1)}, bf16[1024,512]{1,0:T(8,128)(2,1)}, u32[]{:S(2)}) copy-start(bf16[1024,512]{1,0:T(8,128)(2,1)} %copy-done.5) | copy-start | bytes 3145732
  69.2 3.0 %copy-start.10 = (f32[1024,128]{1,0:T(8,128)S(1)}, f32[1024,128]{1,0:T(8,128)}, u32[]{:S(2)}) copy-start(f32[1024,128]{1,0:T(8,128)} %pending_ref.1) | copy-start | bytes 1572868
  69.2 3.0 %copy-start.14 = (s32[3]{0:T(128)S(1)}, s32[3]{0:T(128)}, u32[]{:S(2)}) copy-start(s32[3]{0:T(128)} %refresh_ref.3) | copy-start | bytes 40
  74.7 10.4 %collective-permute-start = (f32[256,1152]{1,0:T(8,128)}, f32[256,1152]{1,0:T(8,128)S(1)}, u32[]{:S(2)}, u32[]{:S(2)}) collective-permute-start(f32[256,1152]{1,0:T(8,128)} %get-tuple-element.47), channel_id=1, source_target_pairs={{0,4},{4,0},{1,5},{5,1},{2,6},{6,2},{3,7},{7,3},{8,12},{12,8},{9,1... | collective-permute-start | bytes 3538952 | tf_op jit(solution)/shard_map/ppermute | solution.py:345
  77.2 33.8 %all-to-all-start.2 = ((bf16[128,8,128]{2,1,0:T(8,128)(2,1)}), bf16[128,8,128]{2,1,0:T(8,128)(2,1)S(1)}, u32[]{:S(2)}, u32[]{:S(2)}) async-start(bf16[128,8,128]{2,1,0:T(8,128)(2,1)} %bitcast.12), calls=%async_computation.2 | async-start | bytes 524288 | tf_op jit(solution)/shard_map/all_to_all | solution.py:272
  86.2 9.9 %collective-permute-start.1 = (f32[64,1152]{1,0:T(8,128)S(1)}, f32[64,1152]{1,0:T(8,128)S(1)}, u32[]{:S(2)}, u32[]{:S(2)}) collective-permute-start(f32[64,1152]{1,0:T(8,128)S(1)} %get-tuple-element.49), channel_id=1, source_target_pairs={{0,1},{1,0},{2,3},{3,2},{4,5},{5,4},{6,7},{7,6},{8,9},{9,8},{10,11... | collective-permute-start | bytes 884744 | tf_op jit(solution)/shard_map/ppermute | solution.py:276
  89.4 15.1 %collective-permute-start.2 = (f32[64,1152]{1,0:T(8,128)S(1)}, f32[64,1152]{1,0:T(8,128)S(1)}, u32[]{:S(2)}, u32[]{:S(2)}) collective-permute-start(f32[64,1152]{1,0:T(8,128)S(1)} %get-tuple-element.50), channel_id=1, source_target_pairs={{0,2},{1,3},{2,0},{3,1},{4,6},{5,7},{6,4},{7,5},{8,10},{9,11},{10,... | collective-permute-start | bytes 884744 | tf_op jit(solution)/shard_map/ppermute | solution.py:276
  94.0 16.9 %collective-permute-start.3 = (f32[64,1152]{1,0:T(8,128)S(1)}, f32[64,1152]{1,0:T(8,128)S(1)}, u32[]{:S(2)}, u32[]{:S(2)}) collective-permute-start(f32[64,1152]{1,0:T(8,128)S(1)} %get-tuple-element.51), channel_id=1, source_target_pairs={{0,3},{1,2},{2,1},{3,0},{4,7},{5,6},{6,5},{7,4},{8,11},{9,10},{10,... | collective-permute-start | bytes 884744 | tf_op jit(solution)/shard_map/ppermute | solution.py:276
  122.0 24.0 %all-to-all-start.4 = ((f32[16,24,128]{2,1,0:T(8,128)}), f32[16,24,128]{2,1,0:T(8,128)S(1)}, u32[]{:S(2)}, u32[]{:S(2)}) async-start(f32[16,24,128]{2,1,0:T(8,128)} %shard_map.190), calls=%async_computation.4 | async-start | bytes 393216 | tf_op jit(solution)/shard_map/all_to_all | solution.py:272
  134.4 21.4 %copy-start.8 = (f32[512,128]{1,0:T(8,128)S(1)}, f32[512,128]{1,0:T(8,128)}, u32[]{:S(2)}) copy-start(f32[512,128]{1,0:T(8,128)} %table_ref.3) | copy-start | bytes 786436
  134.4 21.4 %copy-start.11 = (f32[512,128]{1,0:T(8,128)S(1)}, f32[512,128]{1,0:T(8,128)}, u32[]{:S(2)}) copy-start(f32[512,128]{1,0:T(8,128)} %accum_ref.2) | copy-start | bytes 786436
  134.8 29.2 %copy-start.1 = (f32[1024,128]{1,0:T(8,128)S(1)}, f32[1024,128]{1,0:T(8,128)}, u32[]{:S(2)}) copy-start(f32[1024,128]{1,0:T(8,128)} %cache_ref.3) | copy-start | bytes 1572868
  134.8 29.2 %copy-start.9 = (f32[1024,128]{1,0:T(8,128)S(1)}, f32[1024,128]{1,0:T(8,128)}, u32[]{:S(2)}) copy-start(f32[1024,128]{1,0:T(8,128)} %accum_ref.3) | copy-start | bytes 1572868
  134.9 29.2 %copy-start.16 = (s32[8]{0:T(128)S(1)}, s32[8]{0:T(128)}, u32[]{:S(2)}) copy-start(s32[8]{0:T(128)} %clock_ref.1) | copy-start | bytes 100
  134.9 20.9 %collective-permute-start.4 = (f32[512,128]{1,0:T(8,128)S(1)}, f32[512,128]{1,0:T(8,128)S(1)}, u32[]{:S(2)}, u32[]{:S(2)}) collective-permute-start(f32[512,128]{1,0:T(8,128)S(1)} %shard_map.188.own_ref), channel_id=1, source_target_pairs={{0,1},{1,0},{2,3},{3,2},{4,5},{5,4},{6,7},{7,6},{8,9},{9,8},{10,11... | collective-permute-start | bytes 786440 | tf_op jit(solution)/shard_map/ppermute | solution.py:276
  136.9 18.8 %collective-permute-start.5 = (f32[512,128]{1,0:T(8,128)S(1)}, f32[512,128]{1,0:T(8,128)S(1)}, u32[]{:S(2)}, u32[]{:S(2)}) collective-permute-start(f32[512,128]{1,0:T(8,128)S(1)} %shard_map.188.own_ref), channel_id=1, source_target_pairs={{0,2},{1,3},{2,0},{3,1},{4,6},{5,7},{6,4},{7,5},{8,10},{9,11},{10,... | collective-permute-start | bytes 786440 | tf_op jit(solution)/shard_map/ppermute | solution.py:276
  140.0 15.8 %collective-permute-start.6 = (f32[512,128]{1,0:T(8,128)S(1)}, f32[512,128]{1,0:T(8,128)S(1)}, u32[]{:S(2)}, u32[]{:S(2)}) collective-permute-start(f32[512,128]{1,0:T(8,128)S(1)} %shard_map.188.own_ref), channel_id=1, source_target_pairs={{0,3},{1,2},{2,1},{3,0},{4,7},{5,6},{6,5},{7,4},{8,11},{9,10},{10,... | collective-permute-start | bytes 786440 | tf_op jit(solution)/shard_map/ppermute | solution.py:276
  146.7 17.3 %all-to-all-start.5 = ((f32[32,16,128]{2,1,0:T(8,128)}), f32[32,16,128]{2,1,0:T(8,128)S(1)}, u32[]{:S(2)}, u32[]{:S(2)}) async-start(f32[32,16,128]{2,1,0:T(8,128)} %get-tuple-element.57), calls=%async_computation.5 | async-start | bytes 524288 | tf_op jit(solution)/shard_map/all_to_all | solution.py:272

commit v3 on v2

--- a/solution.py
+++ b/solution.py
@@ -17,6 +17,9 @@
 
 F32 = jnp.float32
 BF16 = jnp.bfloat16
+I16 = jnp.int16
+LN2 = 0.6931471805599453
+FINE = 65534.0
 EXACT = lax.Precision.HIGHEST
 VMEM = pl.BlockSpec(memory_space=pltpu.VMEM)
 SMEM = pl.BlockSpec(memory_space=pltpu.SMEM)
@@ -57,6 +60,42 @@
 
 def dot_t(a, b):
     return lax.dot_general(a, b, (((1,), (1,)), ((), ())), preferred_element_type=F32)
+
+
+def power(exponent):
+    return jnp.exp(exponent * LN2)
+
+
+def exponent_of(top):
+    return jnp.ceil(jnp.log(jnp.maximum(top, 1e-30)) * (1.0 / LN2) + 0.01) - 15.0
+
+
+def pack(values, packed_ref):
+    wide = values.shape[1] - BLOCK
+    top, hot = values[:, :wide], values[:, wide:]
+    top_exponent = exponent_of(jnp.max(jnp.abs(top), axis=1, keepdims=True))
+    hot_exponent = exponent_of(jnp.max(jnp.abs(hot), axis=1, keepdims=True))
+    lane = iota((values.shape[0], BLOCK), 1)
+    hot = hot * power(-hot_exponent)
+    coarse = jnp.round(hot)
+    at = 0
+    for part in (
+        jnp.round(top * power(-top_exponent)),
+        coarse,
+        jnp.round((hot - coarse) * FINE),
+        jnp.where(lane < BLOCK // 2, top_exponent, hot_exponent),
+    ):
+        packed_ref[:, at : at + part.shape[1]] = part.astype(jnp.int32).astype(I16)
+        at += part.shape[1]
+
+
+def unpack(packed):
+    values = packed.astype(jnp.int32).astype(F32)
+    wide = values.shape[1] - 3 * BLOCK
+    coarse, fine, exponents = (values[:, wide + i * BLOCK : wide + (i + 1) * BLOCK] for i in range(3))
+    top = values[:, :wide] * power(exponents[:, :1])
+    hot = (coarse + fine * (1.0 / FINE)) * power(exponents[:, BLOCK - 1 :])
+    return jnp.concatenate([top, hot], axis=1)
 
 
 def requests_kernel(owner_ref, offset_ref, request_ref, target_ref):
@@ -100,24 +139,17 @@
     owned_ref[...] = ones_where(iota_f(owned_ref.shape, 0) == wanted)
 
 
-def masks_kernel(target_ref, hot_ref, cache_ref, table_ref, take_ref, put_ref, hot_in_ref, hot_put_ref, narrow_ref):
+def masks_kernel(target_ref, hot_ref, cache_ref, table_ref, rows_ref, hot_in_ref, hot_put_ref, narrow_ref):
     square = (BLOCK, BLOCK)
     eye = iota(square, 0) == iota(square, 1)
-    slots, lookups = put_ref.shape
     feats = hot_ref.shape[0]
     samples = hot_ref.shape[1]
-    lane = iota_f((samples, BLOCK), 1)
-    slot = iota_f((slots, BLOCK), 0)
     for k in range(feats):
         mine = target_ref[pl.ds(k, samples, stride=feats), :]
-        for b in range(slots // BLOCK):
-            take_ref[k * samples : (k + 1) * samples, b * BLOCK : (b + 1) * BLOCK] = ones_where(
-                mine == lane + float(b * BLOCK)
-            )
         for h in range(samples // BLOCK):
             at = k * samples + h * BLOCK
             row = jnp.sum(jnp.where(eye, mine[h * BLOCK : (h + 1) * BLOCK, :], 0.0), axis=0, keepdims=True)
-            put_ref[:, at : at + BLOCK] = ones_where(slot == row)
+            rows_ref[:, at : at + BLOCK] = jnp.broadcast_to(row, (8, BLOCK))
     cache = cache_ref[...].astype(BF16)
     hot = hot_ref[...].astype(F32)
     hot_count = cache.shape[0]
@@ -134,14 +166,20 @@
 
 
 def layer_kernel(
-    returned_ref, take_ref, put_ref, hot_in_ref, weight_ref, out_weight_ref, labels_ref,
+    returned_ref, target_ref, rows_ref, hot_in_ref, weight_ref, out_weight_ref, labels_ref,
     outgoing_ref, inputs_ref, dhidden_ref, hot_dx_ref, head_ref,
 ):
     square = (BLOCK, BLOCK)
     eye = iota(square, 0) == iota(square, 1)
     samples = hot_in_ref.shape[0]
     width = BLOCK
-    cold = dot(take_ref[...], returned_ref[...]).astype(BF16)
+    lane = iota_f((samples, BLOCK), 1)
+    slots = returned_ref.shape[0]
+    mine = [target_ref[pl.ds(k, samples, stride=2), :] for k in range(2)]
+    take = [
+        jnp.concatenate([ones_where(t == lane + float(b)) for b in range(0, slots, BLOCK)], axis=1) for t in mine
+    ]
+    cold = dot(jnp.concatenate(take, axis=0), returned_ref[...]).astype(BF16)
     inputs = jnp.concatenate([hot_in_ref[...], cold[:samples], cold[samples:]], axis=1)
     inputs_ref[...] = inputs
     weight = weight_ref[...]
@@ -158,7 +196,8 @@
     dhidden_ref[...] = dhidden
     dinputs = dot_t(dhidden, weight).astype(BF16)
     cold_dx = jnp.concatenate([dinputs[:, 2 * width : 3 * width], dinputs[:, 3 * width :]], axis=0)
-    outgoing_ref[...] = dot(put_ref[...], cold_dx).astype(BF16)
+    put = ones_where(iota_f((outgoing_ref.shape[0], rows_ref.shape[1]), 0) == rows_ref[:1, :])
+    outgoing_ref[...] = dot(put, cold_dx).astype(BF16)
     hot_dx_ref[:samples, :] = dinputs[:, :width]
     hot_dx_ref[samples:, :] = dinputs[:, width : 2 * width]
     head = jnp.sum(errors * hidden, axis=0, keepdims=True)
@@ -194,32 +233,34 @@
     for at in blocks:
         pending_new_ref[at, :] = jnp.zeros((BLOCK, BLOCK), F32)
     core, rep = 1 - place_ref[0], place_ref[1]
-    wide = dhidden_ref.shape[1]
-    tall = send_ref.shape[0] // 4
-    send_ref[:, :wide] = half_of_top(core, rep, inputs_ref[...], dhidden_ref[...])
-    for d in range(4):
-        send_ref[d * tall : (d + 1) * tall, wide:] = hot_rows(picked_ref, core, rep, d)
-
-
-def pair_kernel(place_ref, inputs_ref, dhidden_ref, picked_ref, received_ref, *pieces):
+    top = half_of_top(core, rep, inputs_ref[...], dhidden_ref[...])
+    hot = jnp.concatenate([hot_rows(picked_ref, core, rep, d) for d in range(4)], axis=0)
+    pack(jnp.concatenate([top, hot], axis=1), send_ref)
+
+
+def pair_kernel(place_ref, inputs_ref, dhidden_ref, picked_ref, received_ref, own_ref, *pieces):
     core, rep = place_ref[0], place_ref[1]
-    wide = dhidden_ref.shape[1]
     top = half_of_top(core, rep, inputs_ref[...], dhidden_ref[...])
-    tall = pieces[0].shape[0]
-    for d, piece in enumerate(pieces):
+    tall = own_ref.shape[0]
+    for d, piece in enumerate((own_ref, *pieces)):
         rows = slice(d * tall, (d + 1) * tall)
-        piece[:, :wide] = top[rows] + received_ref[rows, :wide]
-        piece[:, wide:] = hot_rows(picked_ref, core, rep, d) + received_ref[rows, wide:]
+        mine = jnp.concatenate([top[rows], hot_rows(picked_ref, core, rep, d)], axis=1)
+        both = mine + unpack(received_ref[rows, :])
+        if d:
+            pack(both, piece)
+        else:
+            piece[...] = both
 
 
 def four_kernel(own_ref, one_ref, two_ref, three_ref, sum_ref):
-    sum_ref[...] = (own_ref[...] + one_ref[...]) + (two_ref[...] + three_ref[...])
+    total = (own_ref[...] + unpack(one_ref[...])) + (unpack(two_ref[...]) + unpack(three_ref[...]))
+    pack(total, sum_ref)
 
 
 def plane_kernel(parts_ref, out_ref):
-    total = parts_ref[0]
+    total = unpack(parts_ref[0])
     for i in range(1, parts_ref.shape[0]):
-        total = total + parts_ref[i]
+        total = total + unpack(parts_ref[i])
     wide = total.shape[1] - BLOCK
     tall = wide // BLOCK
     for b in range(tall):
@@ -307,11 +348,10 @@
         (cold_owner.reshape(groups, BLOCK), cold_offset.reshape(groups, BLOCK)),
     )
     asked = swap(request.reshape(owners, 1, BLOCK), DP).reshape(owners, BLOCK)
-    take, put, hot_in, hot_put, narrow = call(
+    target_rows, hot_in, hot_put, narrow = call(
         masks_kernel,
         [
-            ((lookups, slots), BF16),
-            ((slots, lookups), BF16),
+            ((8, lookups), F32),
             ((samples, feats * width), BF16),
             ((hot_count, samples * feats), BF16),
             ((own_rows, width), BF16),
@@ -330,34 +370,36 @@
             ((samples * feats, width), BF16),
             ((8, BLOCK), F32),
         ],
-        (returned, take, put, hot_in, top_weight, out_weight.reshape(1, hidden_width), labels.reshape(2, BLOCK)),
+        (returned, target, target_rows, hot_in, top_weight, out_weight.reshape(1, hidden_width), labels.reshape(2, BLOCK)),
     )
     incoming = swap(outgoing.reshape(owners, SLOTS, width), DP).reshape(slots, width)
 
     half = inputs_width // 2
     broad = hidden_width + BLOCK
-    send, picked, pending_new = call(
-        send_kernel,
-        [((half, broad), F32), ((inputs_width, BLOCK), F32), ((hot_count, width), F32)],
-        (place, refresh_blocks, inputs, dhidden, hot_put, hot_dx, head, pending),
-        smem=2,
-    )
-    received = lax.ppermute(send, "dp_2", [(0, 1), (1, 0)])
-    pieces = call(
-        pair_kernel, [((half // 4, broad), F32)] * 4, (place, inputs, dhidden, picked, received), smem=1
-    )
-    (paired,) = call(four_kernel, [((half // 4, broad), F32)], (pieces[0], *from_others(pieces[1:])))
-    paired, incoming = lax.optimization_barrier((paired, incoming))
+    packed = broad + 2 * BLOCK
     near = lax.axis_size("dp_1")
     far = lax.axis_size("dp_0")
     plane_size = lax.axis_size(PLANE)
-    plane = swap(paired.reshape(near, far, broad), "dp_1")
+    send, picked, pending_new = call(
+        send_kernel,
+        [((half, packed), I16), ((plane_size * far, BLOCK), F32), ((hot_count, width), F32)],
+        (place, refresh_blocks, inputs, dhidden, hot_put, hot_dx, head, pending),
+        smem=2,
+    )
+    received = lax.ppermute(send, "dp_2", [(0, 1), (1, 0)])
+    pieces = call(
+        pair_kernel,
+        [((half // 4, broad), F32)] + [((half // 4, packed), I16)] * 3,
+        (place, inputs, dhidden, picked, received),
+        smem=1,
+    )
+    (paired,) = call(four_kernel, [((half // 4, packed), I16)], (pieces[0], *from_others(pieces[1:])))
+    paired, incoming = lax.optimization_barrier((paired, incoming))
+    plane = swap(paired.reshape(near, far, packed), "dp_1")
     tall = hidden_width // BLOCK
     (columns,) = call(plane_kernel, [((far, tall + far, BLOCK), F32)], (plane,))
     columns = swap(columns, "dp_0")
-    top, copies = call(
-        column_kernel, [((tall, BLOCK), F32), ((plane_size, far, BLOCK), F32)], (columns,)
-    )
+    top, copies = call(column_kernel, [((tall, BLOCK), F32), ((plane_size, far, BLOCK), F32)], (columns,))
     sums = swap(copies, PLANE).reshape(plane_size * far, BLOCK)
 
     (grad,) = call(cold_kernel, [((own_rows, width), F32)], (owned, incoming))

time: 167 us -> 163 us (0.976)
  local copies, waits for them, and re-layouts: 7.25 us -> 9.19 us
  blocking collectives: 10.3 us -> 8.6 us
    ppermute x6, waiting for transfers between devices: 14.8 us -> 8.36 us  [from_others(): lax.ppermute(p, 'rep', [(i, i ^ d) for i in range(4)])]
    all_to_all x5, waiting for transfers between devices: 37.9 us -> 41 us  [swap(): return lax.all_to_all(x, axis, split_axis=0, concat_axis=0, tiled=True)]
    unnamed x38 -> x42, local copies, waits for them, and re-layouts: 7.25 us -> 9.19 us
    ppermute x1, waiting for transfers between devices: 0.01 us -> 1.8 us  [local(): received = lax.ppermute(send, 'dp_2', [(0, 1), (1, 0)])]
    all_to_all x1, blocking collectives: 10.3 us -> 8.6 us  [swap(): return lax.all_to_all(x, axis, split_axis=0, concat_axis=0, tiled=True)]
  transfers between devices with their start and end apart: 12 -> 12, of which waited for: 6 -> 7; matrix products, arithmetic and copies ran while one was open for 0% -> 0% of each run, Pallas kernels for 3% -> 4%
where the time goes in v3:
time: 163 us
  starting transfers between devices  77.8 us (48%)
  waiting for transfers between devices  51.2 us (31%)
  Pallas kernels  14.8 us (9%)
  local copies, waits for them, and re-layouts  9.19 us (6%)
  blocking collectives  8.6 us (5%)
    all_to_all x5, starting transfers between devices, swap(): return lax.all_to_all(x, axis, split_axis=0, concat_axis=0, tiled=True)  55.5 us
    all_to_all x5, waiting for transfers between devices, swap(): return lax.all_to_all(x, axis, split_axis=0, concat_axis=0, tiled=True)  41 us
    ppermute x6, starting transfers between devices, from_others(): lax.ppermute(p, 'rep', [(i, i ^ d) for i in range(4)])  19.4 us
    pallas_call x13, Pallas kernels, call(): pl.pallas_call(kernel, out_shape=shapes, in_specs=[SMEM] * smem + [VMEM]...  14.8 us
    unnamed x42, local copies, waits for them, and re-layouts  9.19 us
    all_to_all x1, blocking collectives, swap(): return lax.all_to_all(x, axis, split_axis=0, concat_axis=0, tiled=True)  8.6 us
    ppermute x6, waiting for transfers between devices, from_others(): lax.ppermute(p, 'rep', [(i, i ^ d) for i in range(4)])  8.36 us
  transfers between devices with their start and end apart: 12, of which 7 were waited for; matrix products, arithmetic and copies ran while one was open for 0% of the time, Pallas kernels for 4%

profile of v3, /device:TPU:1, one launch (start us, length us, event | category | flops | bytes accessed | tf_op | source)
XLA Modules:
  0.0 162.5 jit_solution(17252053572728955496)
XLA Ops:
  2.0 1.7 %shard_map.180 = (f32[128,128]{1,0:T(8,128)}, f32[512,128]{1,0:T(8,128)S(1)}) custom-call(s32[4,128]{1,0:T(4,128)S(1)} %bitcast.29, s32[4,128]{1,0:T(4,128)S(1)} %bitcast.30), custom_call_target="tpu_custom_call" | custom-call | flops 100000000 | bytes 1000000 | tf_op jit(solution)/shard_map/pallas_call | solution.py:30
  3.7 20.4 %all-to-all-start = ((f32[128,1,128]{2,1,0:T(1,128)}), f32[128,1,128]{2,1,0:T(1,128)S(1)}, u32[]{:S(2)}, u32[]{:S(2)}) async-start(f32[128,1,128]{2,1,0:T(1,128)} %bitcast.3), calls=%async_computation | async-start | bytes 131072 | tf_op jit(solution)/shard_map/all_to_all | solution.py:313
  24.8 1.0 copy-done
  27.3 11.6 %all-to-all-done = f32[128,1,128]{2,1,0:T(1,128)S(1)} async-done(((f32[128,1,128]{2,1,0:T(1,128)}), f32[128,1,128]{2,1,0:T(1,128)S(1)}, u32[]{:S(2)}, u32[]{:S(2)}) %all-to-all-start) | async-done | bytes 65568 | tf_op jit(solution)/shard_map/all_to_all | solution.py:313
  39.0 1.2 shard_map.183
  40.2 5.7 %all-to-all-start.1 = ((bf16[128,8,128]{2,1,0:T(8,128)(2,1)}), bf16[128,8,128]{2,1,0:T(8,128)(2,1)S(1)}, u32[]{:S(2)}, u32[]{:S(2)}) async-start(bf16[128,8,128]{2,1,0:T(8,128)(2,1)} %bitcast.8), calls=%async_computation.1 | async-start | bytes 524288 | tf_op jit(solution)/shard_map/all_to_all | solution.py:313
  45.8 20.6 %all-to-all-done.1 = bf16[128,8,128]{2,1,0:T(8,128)(2,1)S(1)} async-done(((bf16[128,8,128]{2,1,0:T(8,128)(2,1)}), bf16[128,8,128]{2,1,0:T(8,128)(2,1)S(1)}, u32[]{:S(2)}, u32[]{:S(2)}) %all-to-all-start.1) | async-done | bytes 262176 | tf_op jit(solution)/shard_map/all_to_all | solution.py:313
  67.1 0.9 copy-done.5
  68.1 0.9 copy-done.11
  69.0 2.3 %shard_map.184 = (bf16[1024,128]{1,0:T(8,128)(2,1)S(1)}, bf16[256,512]{1,0:T(8,128)(2,1)S(1)}, bf16[256,1024]{1,0:T(8,128)(2,1)S(1)}, bf16[512,128]{1,0:T(8,128)(2,1)S(1)}, f32[8,128]{1,0:T(8,128)S(1)}) custom-call(bf16[1024,128]{1,0:T(8,128)(2,1)S(1)} %bitcast.20, f32[512,128]{1,0:T(8,128)S(1)} %copy-done.5, f32[8,512]{1,0:T(8,128)S(1)} %get-tuple-element.37.rows_ref, ...), custom_call_target="tpu_custom_call" | custom-call | flops 100000000 | bytes 1000000 | tf_op jit(solution)/shard_map/pallas_call | solution.py:30
  72.7 8.5 %all-to-all-start.2 = ((bf16[128,8,128]{2,1,0:T(8,128)(2,1)}), bf16[128,8,128]{2,1,0:T(8,128)(2,1)S(1)}, u32[]{:S(2)}, u32[]{:S(2)}) async-start(bf16[128,8,128]{2,1,0:T(8,128)(2,1)} %bitcast.25), calls=%async_computation.2 | async-start | bytes 524288 | tf_op jit(solution)/shard_map/all_to_all | solution.py:313
  82.0 0.9 copy-done.13
  82.9 1.8 %shard_map.185 = (s16[256,1408]{1,0:T(8,128)(2,1)S(1)}, f32[512,128]{1,0:T(8,128)S(1)}, f32[1024,128]{1,0:T(8,128)}) custom-call(s32[2]{0:T(128)S(1)} %pad_add_fusion.place_ref, s32[3]{0:T(128)S(1)} %copy-done.16, bf16[256,512]{1,0:T(8,128)(2,1)S(1)} %get-tuple-element.39.inputs_ref, bf16[256,1024]{1,0:T(8,128)(2,1)S(1)} %get-tuple-element.40.dhidden_ref, ...), custom_call_target="tpu_custom_call" | custom-call | flops 100000000 | bytes 1000000 | tf_op jit(solution)/shard_map/pallas_call | solution.py:30
  84.7 2.8 %collective-permute-start = (s16[256,1408]{1,0:T(8,128)(2,1)S(1)}, s16[256,1408]{1,0:T(8,128)(2,1)S(1)}, u32[]{:S(2)}, u32[]{:S(2)}) collective-permute-start(s16[256,1408]{1,0:T(8,128)(2,1)S(1)} %get-tuple-element.45), channel_id=1, source_target_pairs={{0,4},{4,0},{1,5},{5,1},{2,6},{6,2},{3,7},{7,3},{8,12},{12,8},{9,1... | collective-permute-start | bytes 2162696 | tf_op jit(solution)/shard_map/ppermute | solution.py:389
  87.5 1.8 %collective-permute-done.received_ref = s16[256,1408]{1,0:T(8,128)(2,1)S(1)} collective-permute-done((s16[256,1408]{1,0:T(8,128)(2,1)S(1)}, s16[256,1408]{1,0:T(8,128)(2,1)S(1)}, u32[]{:S(2)}, u32[]{:S(2)}) %collective-permute-start) | collective-permute-done | bytes 720928 | tf_op jit(solution)/shard_map/ppermute | solution.py:389
  89.3 1.3 shard_map.186
  90.6 3.2 %collective-permute-start.1 = (s16[64,1408]{1,0:T(8,128)(2,1)S(1)}, s16[64,1408]{1,0:T(8,128)(2,1)S(1)}, u32[]{:S(2)}, u32[]{:S(2)}) collective-permute-start(s16[64,1408]{1,0:T(8,128)(2,1)S(1)} %get-tuple-element.47), channel_id=1, source_target_pairs={{0,1},{1,0},{2,3},{3,2},{4,5},{5,4},{6,7},{7,6},{8,9},{9,8},{10,11... | collective-permute-start | bytes 540680 | tf_op jit(solution)/shard_map/ppermute | solution.py:317
  93.8 4.7 %collective-permute-start.2 = (s16[64,1408]{1,0:T(8,128)(2,1)S(1)}, s16[64,1408]{1,0:T(8,128)(2,1)S(1)}, u32[]{:S(2)}, u32[]{:S(2)}) collective-permute-start(s16[64,1408]{1,0:T(8,128)(2,1)S(1)} %get-tuple-element.48), channel_id=1, source_target_pairs={{0,2},{1,3},{2,0},{3,1},{4,6},{5,7},{6,4},{7,5},{8,10},{9,11},{10,... | collective-permute-start | bytes 540680 | tf_op jit(solution)/shard_map/ppermute | solution.py:317
  98.5 1.9 %collective-permute-start.3 = (s16[64,1408]{1,0:T(8,128)(2,1)S(1)}, s16[64,1408]{1,0:T(8,128)(2,1)S(1)}, u32[]{:S(2)}, u32[]{:S(2)}) collective-permute-start(s16[64,1408]{1,0:T(8,128)(2,1)S(1)} %get-tuple-element.49), channel_id=1, source_target_pairs={{0,3},{1,2},{2,1},{3,0},{4,7},{5,6},{6,5},{7,4},{8,11},{9,10},{10,... | collective-permute-start | bytes 540680 | tf_op jit(solution)/shard_map/ppermute | solution.py:317
  100.5 4.1 %collective-permute-done.2.two_ref = s16[64,1408]{1,0:T(8,128)(2,1)S(1)} collective-permute-done((s16[64,1408]{1,0:T(8,128)(2,1)S(1)}, s16[64,1408]{1,0:T(8,128)(2,1)S(1)}, u32[]{:S(2)}, u32[]{:S(2)}) %collective-permute-start.2) | collective-permute-done | bytes 180256 | tf_op jit(solution)/shard_map/ppermute | solution.py:317
  104.6 4.3 %collective-permute-done.3.three_ref = s16[64,1408]{1,0:T(8,128)(2,1)S(1)} collective-permute-done((s16[64,1408]{1,0:T(8,128)(2,1)S(1)}, s16[64,1408]{1,0:T(8,128)(2,1)S(1)}, u32[]{:S(2)}, u32[]{:S(2)}) %collective-permute-start.3) | collective-permute-done | bytes 180256 | tf_op jit(solution)/shard_map/ppermute | solution.py:317
  109.1 8.6 %all_to_all.30.parts_ref = s16[4,16,1408]{2,1,0:T(8,128)(2,1)S(1)} all-to-all(s16[4,16,1408]{2,1,0:T(8,128)(2,1)S(1)} %bitcast.22), channel_id=1, replica_groups=mesh['dp_0'=16,'dp_1'=4,'dp_2'=2,'rep'=4] {'dp_1'}, dimensions={0} | all-to-all | bytes 360448 | tf_op jit(solution)/shard_map/all_to_all | solution.py:313
  117.7 0.8 shard_map.190
  118.5 11.6 %all-to-all-start.4 = ((f32[16,24,128]{2,1,0:T(8,128)}), f32[16,24,128]{2,1,0:T(8,128)S(1)}, u32[]{:S(2)}, u32[]{:S(2)}) async-start(f32[16,24,128]{2,1,0:T(8,128)} %shard_map.190), calls=%async_computation.4 | async-start | bytes 393216 | tf_op jit(solution)/shard_map/all_to_all | solution.py:313
  131.3 2.1 %collective-permute-start.4 = (f32[512,128]{1,0:T(8,128)S(1)}, f32[512,128]{1,0:T(8,128)S(1)}, u32[]{:S(2)}, u32[]{:S(2)}) collective-permute-start(f32[512,128]{1,0:T(8,128)S(1)} %shard_map.188.own_ref), channel_id=1, source_target_pairs={{0,1},{1,0},{2,3},{3,2},{4,5},{5,4},{6,7},{7,6},{8,9},{9,8},{10,11... | collective-permute-start | bytes 786440 | tf_op jit(solution)/shard_map/ppermute | solution.py:317
  133.4 3.5 %collective-permute-start.5 = (f32[512,128]{1,0:T(8,128)S(1)}, f32[512,128]{1,0:T(8,128)S(1)}, u32[]{:S(2)}, u32[]{:S(2)}) collective-permute-start(f32[512,128]{1,0:T(8,128)S(1)} %shard_map.188.own_ref), channel_id=1, source_target_pairs={{0,2},{1,3},{2,0},{3,1},{4,6},{5,7},{6,4},{7,5},{8,10},{9,11},{10,... | collective-permute-start | bytes 786440 | tf_op jit(solution)/shard_map/ppermute | solution.py:317
  136.9 4.0 %collective-permute-start.6 = (f32[512,128]{1,0:T(8,128)S(1)}, f32[512,128]{1,0:T(8,128)S(1)}, u32[]{:S(2)}, u32[]{:S(2)}) collective-permute-start(f32[512,128]{1,0:T(8,128)S(1)} %shard_map.188.own_ref), channel_id=1, source_target_pairs={{0,3},{1,2},{2,1},{3,0},{4,7},{5,6},{6,5},{7,4},{8,11},{9,10},{10,... | collective-permute-start | bytes 786440 | tf_op jit(solution)/shard_map/ppermute | solution.py:317
  140.9 1.5 all-to-all-done.4.parts_ref
  143.2 9.4 %all-to-all-start.5 = ((f32[32,16,128]{2,1,0:T(8,128)}), f32[32,16,128]{2,1,0:T(8,128)S(1)}, u32[]{:S(2)}, u32[]{:S(2)}) async-start(f32[32,16,128]{2,1,0:T(8,128)} %get-tuple-element.55), calls=%async_computation.5 | async-start | bytes 524288 | tf_op jit(solution)/shard_map/all_to_all | solution.py:313
  152.6 0.9 shard_map.189
  153.6 7.3 %all-to-all-done.5 = f32[32,16,128]{2,1,0:T(8,128)S(1)} async-done(((f32[32,16,128]{2,1,0:T(8,128)}), f32[32,16,128]{2,1,0:T(8,128)S(1)}, u32[]{:S(2)}, u32[]{:S(2)}) %all-to-all-start.5) | async-done | bytes 262176 | tf_op jit(solution)/shard_map/all_to_all | solution.py:313
  160.9 1.7 %shard_map.192 = (f32[1024,128]{1,0:T(8,128)}, f32[1024,128]{1,0:T(8,128)}, f32[8,128]{1,0:T(8,128)}) custom-call(s32[3]{0:T(128)S(1)} %copy-done.16, s32[8]{0:T(128)S(1)} %copy-done.18, f32[512,128]{1,0:T(8,128)S(1)} %bitcast.21, f32[1024,128]{1,0:T(8,128)S(1)} %copy-done.1, f32[1024,128]{1,0:T(8,128)S(1)} %copy-done.6), custom_call_target="tpu_custom_call" | custom-call | flops 100000000 | bytes 1000000 | tf_op jit(solution)/shard_map/pallas_call | solution.py:30
  (49 shorter events, 8.5 us)
Async XLA Ops:
  0.6 0.7 copy-start.19
  0.6 23.5 %copy-start.3 = (f32[512,128]{1,0:T(8,128)S(1)}, f32[512,128]{1,0:T(8,128)}, u32[]{:S(2)}) copy-start(f32[512,128]{1,0:T(8,128)} %table_ref.3) | copy-start | bytes 786436
  1.3 0.7 copy-start.20
  3.7 22.9 %copy-start.4 = (f32[512,128]{1,0:T(8,128)}, f32[512,128]{1,0:T(8,128)S(1)}, u32[]{:S(2)}) copy-start(f32[512,128]{1,0:T(8,128)S(1)} %get-tuple-element.35.target_ref) | copy-start | bytes 786436
  3.7 35.2 %all-to-all-start = ((f32[128,1,128]{2,1,0:T(1,128)}), f32[128,1,128]{2,1,0:T(1,128)S(1)}, u32[]{:S(2)}, u32[]{:S(2)}) async-start(f32[128,1,128]{2,1,0:T(1,128)} %bitcast.3), calls=%async_computation | async-start | bytes 131072 | tf_op jit(solution)/shard_map/all_to_all | solution.py:313
  24.1 0.7 copy-start.15
  24.8 1.0 copy-start
  25.9 40.6 %copy-start.2 = (bf16[512,1024]{1,0:T(8,128)(2,1)S(1)}, bf16[512,1024]{1,0:T(8,128)(2,1)}, u32[]{:S(2)}) copy-start(bf16[512,1024]{1,0:T(8,128)(2,1)} %weight_ref.1) | copy-start | bytes 3145732
  26.7 0.7 copy-start.10
  40.2 26.3 %all-to-all-start.1 = ((bf16[128,8,128]{2,1,0:T(8,128)(2,1)}), bf16[128,8,128]{2,1,0:T(8,128)(2,1)S(1)}, u32[]{:S(2)}, u32[]{:S(2)}) async-start(bf16[128,8,128]{2,1,0:T(8,128)(2,1)} %bitcast.8), calls=%async_computation.1 | async-start | bytes 524288 | tf_op jit(solution)/shard_map/all_to_all | solution.py:313
  66.4 0.7 copy-start.14
  66.4 0.7 copy-start.17
  67.1 0.9 copy-start.5
  68.1 0.9 copy-start.11
  71.3 0.7 copy-start.8
  72.7 8.6 %copy-start.7 = (f32[1024,128]{1,0:T(8,128)S(1)}, f32[1024,128]{1,0:T(8,128)}, u32[]{:S(2)}) copy-start(f32[1024,128]{1,0:T(8,128)} %pending_ref.1) | copy-start | bytes 1572868
  72.7 36.4 %all-to-all-start.2 = ((bf16[128,8,128]{2,1,0:T(8,128)(2,1)}), bf16[128,8,128]{2,1,0:T(8,128)(2,1)S(1)}, u32[]{:S(2)}, u32[]{:S(2)}) async-start(bf16[128,8,128]{2,1,0:T(8,128)(2,1)} %bitcast.25), calls=%async_computation.2 | async-start | bytes 524288 | tf_op jit(solution)/shard_map/all_to_all | solution.py:313
  81.3 0.7 copy-start.16
  82.0 0.9 copy-start.13
  84.7 4.6 %collective-permute-start = (s16[256,1408]{1,0:T(8,128)(2,1)S(1)}, s16[256,1408]{1,0:T(8,128)(2,1)S(1)}, u32[]{:S(2)}, u32[]{:S(2)}) collective-permute-start(s16[256,1408]{1,0:T(8,128)(2,1)S(1)} %get-tuple-element.45), channel_id=1, source_target_pairs={{0,4},{4,0},{1,5},{5,1},{2,6},{6,2},{3,7},{7,3},{8,12},{12,8},{9,1... | collective-permute-start | bytes 2162696 | tf_op jit(solution)/shard_map/ppermute | solution.py:389
  90.6 9.9 %collective-permute-start.1 = (s16[64,1408]{1,0:T(8,128)(2,1)S(1)}, s16[64,1408]{1,0:T(8,128)(2,1)S(1)}, u32[]{:S(2)}, u32[]{:S(2)}) collective-permute-start(s16[64,1408]{1,0:T(8,128)(2,1)S(1)} %get-tuple-element.47), channel_id=1, source_target_pairs={{0,1},{1,0},{2,3},{3,2},{4,5},{5,4},{6,7},{7,6},{8,9},{9,8},{10,11... | collective-permute-start | bytes 540680 | tf_op jit(solution)/shard_map/ppermute | solution.py:317
  93.8 10.8 %collective-permute-start.2 = (s16[64,1408]{1,0:T(8,128)(2,1)S(1)}, s16[64,1408]{1,0:T(8,128)(2,1)S(1)}, u32[]{:S(2)}, u32[]{:S(2)}) collective-permute-start(s16[64,1408]{1,0:T(8,128)(2,1)S(1)} %get-tuple-element.48), channel_id=1, source_target_pairs={{0,2},{1,3},{2,0},{3,1},{4,6},{5,7},{6,4},{7,5},{8,10},{9,11},{10,... | collective-permute-start | bytes 540680 | tf_op jit(solution)/shard_map/ppermute | solution.py:317
  98.5 10.3 %collective-permute-start.3 = (s16[64,1408]{1,0:T(8,128)(2,1)S(1)}, s16[64,1408]{1,0:T(8,128)(2,1)S(1)}, u32[]{:S(2)}, u32[]{:S(2)}) collective-permute-start(s16[64,1408]{1,0:T(8,128)(2,1)S(1)} %get-tuple-element.49), channel_id=1, source_target_pairs={{0,3},{1,2},{2,1},{3,0},{4,7},{5,6},{6,5},{7,4},{8,11},{9,10},{10,... | collective-permute-start | bytes 540680 | tf_op jit(solution)/shard_map/ppermute | solution.py:317
  118.5 23.9 %all-to-all-start.4 = ((f32[16,24,128]{2,1,0:T(8,128)}), f32[16,24,128]{2,1,0:T(8,128)S(1)}, u32[]{:S(2)}, u32[]{:S(2)}) async-start(f32[16,24,128]{2,1,0:T(8,128)} %shard_map.190), calls=%async_computation.4 | async-start | bytes 393216 | tf_op jit(solution)/shard_map/all_to_all | solution.py:313
  131.3 21.3 %collective-permute-start.4 = (f32[512,128]{1,0:T(8,128)S(1)}, f32[512,128]{1,0:T(8,128)S(1)}, u32[]{:S(2)}, u32[]{:S(2)}) collective-permute-start(f32[512,128]{1,0:T(8,128)S(1)} %shard_map.188.own_ref), channel_id=1, source_target_pairs={{0,1},{1,0},{2,3},{3,2},{4,5},{5,4},{6,7},{7,6},{8,9},{9,8},{10,11... | collective-permute-start | bytes 786440 | tf_op jit(solution)/shard_map/ppermute | solution.py:317
  133.4 19.2 %collective-permute-start.5 = (f32[512,128]{1,0:T(8,128)S(1)}, f32[512,128]{1,0:T(8,128)S(1)}, u32[]{:S(2)}, u32[]{:S(2)}) collective-permute-start(f32[512,128]{1,0:T(8,128)S(1)} %shard_map.188.own_ref), channel_id=1, source_target_pairs={{0,2},{1,3},{2,0},{3,1},{4,6},{5,7},{6,4},{7,5},{8,10},{9,11},{10,... | collective-permute-start | bytes 786440 | tf_op jit(solution)/shard_map/ppermute | solution.py:317
  136.9 15.7 %collective-permute-start.6 = (f32[512,128]{1,0:T(8,128)S(1)}, f32[512,128]{1,0:T(8,128)S(1)}, u32[]{:S(2)}, u32[]{:S(2)}) collective-permute-start(f32[512,128]{1,0:T(8,128)S(1)} %shard_map.188.own_ref), channel_id=1, source_target_pairs={{0,3},{1,2},{2,1},{3,0},{4,7},{5,6},{6,5},{7,4},{8,11},{9,10},{10,... | collective-permute-start | bytes 786440 | tf_op jit(solution)/shard_map/ppermute | solution.py:317
  143.2 9.5 %copy-start.9 = (f32[512,128]{1,0:T(8,128)S(1)}, f32[512,128]{1,0:T(8,128)}, u32[]{:S(2)}) copy-start(f32[512,128]{1,0:T(8,128)} %accum_ref.2) | copy-start | bytes 786436
  143.2 17.7 %all-to-all-start.5 = ((f32[32,16,128]{2,1,0:T(8,128)}), f32[32,16,128]{2,1,0:T(8,128)S(1)}, u32[]{:S(2)}, u32[]{:S(2)}) async-start(f32[32,16,128]{2,1,0:T(8,128)} %get-tuple-element.55), calls=%async_computation.5 | async-start | bytes 524288 | tf_op jit(solution)/shard_map/all_to_all | solution.py:313
  152.6 8.3 %copy-start.1 = (f32[1024,128]{1,0:T(8,128)S(1)}, f32[1024,128]{1,0:T(8,128)}, u32[]{:S(2)}) copy-start(f32[1024,128]{1,0:T(8,128)} %cache_ref.3) | copy-start | bytes 1572868
  152.6 8.3 %copy-start.6 = (f32[1024,128]{1,0:T(8,128)S(1)}, f32[1024,128]{1,0:T(8,128)}, u32[]{:S(2)}) copy-start(f32[1024,128]{1,0:T(8,128)} %accum_ref.3) | copy-start | bytes 1572868
  153.6 7.3 %copy-start.18 = (s32[8]{0:T(128)S(1)}, s32[8]{0:T(128)}, u32[]{:S(2)}) copy-start(s32[8]{0:T(128)} %clock_ref.1) | copy-start | bytes 100
  (1 other events, 0.7 us)

commit v4 on v3

--- a/solution.py
+++ b/solution.py
@@ -22,19 +22,49 @@
 FINE = 65534.0
 EXACT = lax.Precision.HIGHEST
 VMEM = pl.BlockSpec(memory_space=pltpu.VMEM)
+HBM = pl.BlockSpec(memory_space=pltpu.HBM)
 SMEM = pl.BlockSpec(memory_space=pltpu.SMEM)
 
 
-def call(kernel, outs, args, smem=0, scratch=(), flops=10**8, moved=10**6):
-    shapes = [jax.ShapeDtypeStruct(s, d) for s, d in outs]
+class Loaded:
+    def __init__(self, source, held, sem):
+        self.copy = pltpu.make_async_copy(source, held, sem)
+        self.held = held
+        self.copy.start()
+
+    def wait(self):
+        self.copy.wait()
+        return self.held
+
+
+def call(kernel, outs, args, smem=0, scratch=(), loads=(), held=(), kept=()):
+    own = len(scratch)
+    ins = len(args)
+
+    def body(*refs):
+        given = list(refs[:ins])
+        rest = refs[ins + len(outs) :]
+        for j, i in enumerate(loads):
+            given[i] = Loaded(given[i], rest[own + j], rest[own + len(loads) + j])
+        kernel(*given, *refs[ins : ins + len(outs)], *rest[:own])
+
+    specs = [SMEM] * smem + [VMEM] * (ins - smem)
+    args = list(args)
+    for i in loads:
+        specs[i] = HBM
+        args[i] = pltpu.with_memory_space_constraint(args[i], pltpu.HBM)
+    for i in held:
+        args[i] = pltpu.with_memory_space_constraint(args[i], pltpu.VMEM)
     return pl.pallas_call(
-        kernel,
-        out_shape=shapes,
-        in_specs=[SMEM] * smem + [VMEM] * (len(args) - smem),
+        body,
+        out_shape=[(pltpu.VMEM if i in kept else jax.ShapeDtypeStruct)(s, d) for i, (s, d) in enumerate(outs)],
+        in_specs=specs,
         out_specs=[VMEM] * len(outs),
-        scratch_shapes=[pltpu.VMEM(s, d) for s, d in scratch],
+        scratch_shapes=[pltpu.VMEM(s, d) for s, d in scratch]
+        + [pltpu.VMEM(args[i].shape, args[i].dtype) for i in loads]
+        + [pltpu.SemaphoreType.DMA for _ in loads],
         compiler_params=pltpu.CompilerParams(vmem_limit_bytes=16 * 2**20),
-        cost_estimate=pl.CostEstimate(flops=flops, bytes_accessed=moved, transcendentals=0),
+        cost_estimate=pl.CostEstimate(flops=10**9, bytes_accessed=10**7, transcendentals=0),
     )(*args)
 
 
@@ -101,10 +131,10 @@
 def requests_kernel(owner_ref, offset_ref, request_ref, target_ref):
     square = (BLOCK, BLOCK)
     eye = iota(square, 0) == iota(square, 1)
-    groups = owner_ref.shape[0]
+    owner = owner_ref.wait()[...].astype(F32)
+    offset = offset_ref.wait()[...].astype(F32)
+    groups = owner.shape[0]
     lookups = groups * BLOCK
-    owner = owner_ref[...].astype(F32)
-    offset = offset_ref[...].astype(F32)
     rows = [owner[s : s + 1, :] for s in range(groups)]
     owner_col = jnp.concatenate([column_of(row, eye) for row in rows], axis=0)
     offset_col = jnp.concatenate([column_of(offset[s : s + 1, :], eye) for s in range(groups)], axis=0)
@@ -142,16 +172,15 @@
 def masks_kernel(target_ref, hot_ref, cache_ref, table_ref, rows_ref, hot_in_ref, hot_put_ref, narrow_ref):
     square = (BLOCK, BLOCK)
     eye = iota(square, 0) == iota(square, 1)
-    feats = hot_ref.shape[0]
-    samples = hot_ref.shape[1]
+    hot = hot_ref.wait()[...].astype(F32)
+    feats, samples = hot.shape
     for k in range(feats):
         mine = target_ref[pl.ds(k, samples, stride=feats), :]
         for h in range(samples // BLOCK):
             at = k * samples + h * BLOCK
             row = jnp.sum(jnp.where(eye, mine[h * BLOCK : (h + 1) * BLOCK, :], 0.0), axis=0, keepdims=True)
             rows_ref[:, at : at + BLOCK] = jnp.broadcast_to(row, (8, BLOCK))
-    cache = cache_ref[...].astype(BF16)
-    hot = hot_ref[...].astype(F32)
+    cache = cache_ref.wait()[...].astype(BF16)
     hot_count = cache.shape[0]
     hot_row = iota_f((hot_count, BLOCK), 0)
     hot_lane = iota_f((BLOCK, hot_count), 1)
@@ -162,7 +191,7 @@
             hot_put_ref[:, at : at + BLOCK] = ones_where(hot_row == row)
             chosen = ones_where(column_of(row, eye) == hot_lane)
             hot_in_ref[h * BLOCK : (h + 1) * BLOCK, k * BLOCK : (k + 1) * BLOCK] = dot(chosen, cache).astype(BF16)
-    narrow_ref[...] = table_ref[...].astype(BF16)
+    narrow_ref[...] = table_ref.wait()[...].astype(BF16)
 
 
 def layer_kernel(
@@ -171,8 +200,8 @@
 ):
     square = (BLOCK, BLOCK)
     eye = iota(square, 0) == iota(square, 1)
-    samples = hot_in_ref.shape[0]
     width = BLOCK
+    samples = target_ref.shape[0] // 2
     lane = iota_f((samples, BLOCK), 1)
     slots = returned_ref.shape[0]
     mine = [target_ref[pl.ds(k, samples, stride=2), :] for k in range(2)]
@@ -182,13 +211,13 @@
     cold = dot(jnp.concatenate(take, axis=0), returned_ref[...]).astype(BF16)
     inputs = jnp.concatenate([hot_in_ref[...], cold[:samples], cold[samples:]], axis=1)
     inputs_ref[...] = inputs
-    weight = weight_ref[...]
-    out_weight = out_weight_ref[...]
+    weight = weight_ref.wait()[...]
+    out_weight = out_weight_ref.wait()[...]
     preact = dot(inputs, weight)
     gates = jax.nn.sigmoid(preact)
     hidden = (preact * gates).astype(BF16).astype(F32)
     logits = jnp.sum(hidden * out_weight, axis=1, keepdims=True)
-    labels = labels_ref[...].astype(F32)
+    labels = labels_ref.wait()[...].astype(F32)
     label = jnp.concatenate([column_of(labels[h : h + 1, :], eye) for h in range(samples // BLOCK)], axis=0)
     errors = jax.nn.sigmoid(logits) - label
     slope = gates * (1.0 + preact * (1.0 - gates))
@@ -222,7 +251,7 @@
     place_ref, refresh_ref, inputs_ref, dhidden_ref, hot_put_ref, hot_dx_ref, head_ref, pending_ref,
     send_ref, picked_ref, pending_new_ref,
 ):
-    pending_new_ref[...] = pending_ref[...] + dot(hot_put_ref[...], hot_dx_ref[...])
+    pending_new_ref[...] = dot(hot_put_ref[...], hot_dx_ref[...]) + pending_ref.wait()[...]
     count = refresh_ref.shape[0]
     blocks = [pl.ds(pl.multiple_of(refresh_ref[i] * BLOCK, BLOCK), BLOCK) for i in range(count)]
     for i, at in enumerate(blocks):
@@ -302,9 +331,12 @@
     grad_ref[...] = dot(owned_ref[...], incoming_ref[...])
 
 
-def update_kernel(own_ref, one_ref, two_ref, three_ref, table_ref, accum_ref, table_new_ref, accum_new_ref):
-    grad = (own_ref[...] + one_ref[...]) + (two_ref[...] + three_ref[...])
-    table_next, accum_next = adagrad(table_ref[...], accum_ref[...], grad)
+def two_kernel(own_ref, other_ref, sum_ref):
+    sum_ref[...] = own_ref[...] + other_ref[...]
+
+
+def update_kernel(own_ref, other_ref, table_ref, accum_ref, table_new_ref, accum_new_ref):
+    table_next, accum_next = adagrad(table_ref[...], accum_ref[...], own_ref[...] + other_ref[...])
     table_new_ref[...] = table_next
     accum_new_ref[...] = accum_next
 
@@ -313,8 +345,8 @@
     return lax.all_to_all(x, axis, split_axis=0, concat_axis=0, tiled=True)
 
 
-def from_others(pieces):
-    return [lax.ppermute(p, "rep", [(i, i ^ d) for i in range(4)]) for d, p in enumerate(pieces, 1)]
+def from_rep(piece, distance):
+    return lax.ppermute(piece, "rep", [(i, i ^ distance) for i in range(4)])
 
 
 def local(
@@ -346,6 +378,8 @@
         requests_kernel,
         [((owners, BLOCK), F32), ((lookups, BLOCK), F32)],
         (cold_owner.reshape(groups, BLOCK), cold_offset.reshape(groups, BLOCK)),
+        loads=(0, 1),
+        kept=(1,),
     )
     asked = swap(request.reshape(owners, 1, BLOCK), DP).reshape(owners, BLOCK)
     target_rows, hot_in, hot_put, narrow = call(
@@ -357,8 +391,11 @@
             ((own_rows, width), BF16),
         ],
         (target, hot_ids.T, hot_cache, cold_table),
-    )
-    (found,) = call(rows_kernel, [((slots, width), BF16)], (asked, narrow), scratch=[((slots, width), F32)])
+        loads=(1, 2, 3),
+        held=(0,),
+        kept=(0, 1, 2, 3),
+    )
+    (found,) = call(rows_kernel, [((slots, width), BF16)], (asked, narrow), held=(1,), scratch=[((slots, width), F32)])
     returned = swap(found.reshape(owners, SLOTS, width), DP).reshape(slots, width)
     (owned,) = call(owned_kernel, [((own_rows, slots), BF16)], (asked,))
     outgoing, inputs, dhidden, hot_dx, head = call(
@@ -371,9 +408,10 @@
             ((8, BLOCK), F32),
         ],
         (returned, target, target_rows, hot_in, top_weight, out_weight.reshape(1, hidden_width), labels.reshape(2, BLOCK)),
-    )
-    incoming = swap(outgoing.reshape(owners, SLOTS, width), DP).reshape(slots, width)
-
+        loads=(4, 5, 6),
+        held=(1, 2, 3),
+        kept=(1, 2, 3, 4),
+    )
     half = inputs_width // 2
     broad = hidden_width + BLOCK
     packed = broad + 2 * BLOCK
@@ -385,15 +423,22 @@
         [((half, packed), I16), ((plane_size * far, BLOCK), F32), ((hot_count, width), F32)],
         (place, refresh_blocks, inputs, dhidden, hot_put, hot_dx, head, pending),
         smem=2,
-    )
+        loads=(7,),
+        held=(2, 3, 4, 5, 6),
+        kept=(1,),
+    )
+    send, outgoing = lax.optimization_barrier((send, outgoing))
     received = lax.ppermute(send, "dp_2", [(0, 1), (1, 0)])
+    incoming = swap(outgoing.reshape(owners, SLOTS, width), DP).reshape(slots, width)
     pieces = call(
         pair_kernel,
         [((half // 4, broad), F32)] + [((half // 4, packed), I16)] * 3,
         (place, inputs, dhidden, picked, received),
         smem=1,
-    )
-    (paired,) = call(four_kernel, [((half // 4, packed), I16)], (pieces[0], *from_others(pieces[1:])))
+        held=(1, 2, 3),
+    )
+    two, one, three = (from_rep(pieces[d], d) for d in (2, 1, 3))
+    (paired,) = call(four_kernel, [((half // 4, packed), I16)], (pieces[0], one, two, three))
     paired, incoming = lax.optimization_barrier((paired, incoming))
     plane = swap(paired.reshape(near, far, packed), "dp_1")
     tall = hidden_width // BLOCK
@@ -403,9 +448,9 @@
     sums = swap(copies, PLANE).reshape(plane_size * far, BLOCK)
 
     (grad,) = call(cold_kernel, [((own_rows, width), F32)], (owned, incoming))
-    others = from_others([grad] * 3)
+    (grad,) = call(two_kernel, [((own_rows, width), F32)], (grad, from_rep(grad, 1)))
     cold_table_new, cold_accum_new = call(
-        update_kernel, [((own_rows, width), F32)] * 2, (grad, *others, cold_table, cold_accum)
+        update_kernel, [((own_rows, width), F32)] * 2, (grad, from_rep(grad, 3), cold_table, cold_accum)
     )
     hot_cache_new, hot_accum_new, out_grad = call(
         hot_kernel,

time: 163 us -> 161 us (0.988)
  local copies, waits for them, and re-layouts: 9.19 us -> 2.35 us
  starting transfers between devices: 77.8 us -> 71.3 us
  Pallas kernels: 14.8 us -> 20.1 us
  waiting for transfers between devices: 51.2 us -> 55.4 us
    unnamed x42 -> x20, local copies, waits for them, and re-layouts: 9.19 us -> 2.35 us
    pallas_call x13 -> x14, Pallas kernels: 14.8 us -> 20.1 us  [call(): pl.pallas_call(body, out_shape=[(pltpu.VMEM if i in kept else jax.ShapeDt...]
    ppermute x6 -> x5, starting transfers between devices: 19.4 us -> 14.4 us  [from_rep(): return lax.ppermute(piece, 'rep', [(i, i ^ distance) for i in range(4)])]
    ppermute x6 -> x5, waiting for transfers between devices: 8.36 us -> 13.2 us  [from_rep(): return lax.ppermute(piece, 'rep', [(i, i ^ distance) for i in range(4)])]
    ppermute x1, waiting for transfers between devices: 1.8 us -> 0.01 us  [local(): received = lax.ppermute(send, 'dp_2', [(0, 1), (1, 0)])]
  transfers between devices with their start and end apart: 12 -> 11, of which waited for: 7 -> 8; matrix products, arithmetic and copies ran while one was open for 0% -> 0% of each run, Pallas kernels for 4% -> 4%
where the time goes in v4:
time: 161 us; the launch traced here: 160 us
  starting transfers between devices  71.3 us (44%)
  waiting for transfers between devices  55.4 us (34%)
  Pallas kernels  20.1 us (12%)
  blocking collectives  10.2 us (6%)
  local copies, waits for them, and re-layouts  2.35 us (1%)
    all_to_all x5, starting transfers between devices, swap(): return lax.all_to_all(x, axis, split_axis=0, concat_axis=0, tiled=True)  54.4 us
    all_to_all x5, waiting for transfers between devices, swap(): return lax.all_to_all(x, axis, split_axis=0, concat_axis=0, tiled=True)  42.1 us
    pallas_call x14, Pallas kernels, call(): pl.pallas_call(body, out_shape=[(pltpu.VMEM if i in kept else jax.ShapeDt...  20.1 us
    ppermute x5, starting transfers between devices, from_rep(): return lax.ppermute(piece, 'rep', [(i, i ^ distance) for i in range(4)])  14.4 us
    ppermute x5, waiting for transfers between devices, from_rep(): return lax.ppermute(piece, 'rep', [(i, i ^ distance) for i in range(4)])  13.2 us
    all_to_all x1, blocking collectives, swap(): return lax.all_to_all(x, axis, split_axis=0, concat_axis=0, tiled=True)  10.2 us
  transfers between devices with their start and end apart: 11, of which 8 were waited for; matrix products, arithmetic and copies ran while one was open for 0% of the time, Pallas kernels for 4%

profile of v4, /device:TPU:1, one launch (start us, length us, event | category | flops | bytes accessed | tf_op | source)
XLA Modules:
  0.0 160.2 jit_solution(222981418097084634)
XLA Ops:
  0.6 2.4 %shard_map.180 = (f32[128,128]{1,0:T(8,128)}, f32[512,128]{1,0:T(8,128)S(1)}) custom-call(s32[4,128]{1,0:T(4,128)} %bitcast.26, s32[4,128]{1,0:T(4,128)} %bitcast.27), custom_call_target="tpu_custom_call" | custom-call | flops 1000000000 | bytes 10000000 | tf_op jit(solution)/shard_map/pallas_call | solution.py:58
  3.1 20.4 %all-to-all-start = ((f32[128,1,128]{2,1,0:T(1,128)}), f32[128,1,128]{2,1,0:T(1,128)S(1)}, u32[]{:S(2)}, u32[]{:S(2)}) async-start(f32[128,1,128]{2,1,0:T(1,128)} %bitcast.3), calls=%async_computation | async-start | bytes 131072 | tf_op jit(solution)/shard_map/all_to_all | solution.py:345
  23.5 1.9 %shard_map.182 = (f32[8,512]{1,0:T(8,128)S(1)}, bf16[256,256]{1,0:T(8,128)(2,1)S(1)}, bf16[1024,512]{1,0:T(8,128)(2,1)S(1)}, bf16[512,128]{1,0:T(8,128)(2,1)S(1)}) custom-call(f32[512,128]{1,0:T(8,128)S(1)} %get-tuple-element.37.refs_0_.refs_1_, s32[2,256]{1,0:T(2,128)} %bitcast.28, f32[1024,128]{1,0:T(8,128)} %refs_3_.5, f32[512,128]{1,0:T(8,128)} %refs_2_.3), custom_call_target="tpu_custom_call" | custom-call | flops 1000000000 | bytes 10000000 | tf_op jit(solution)/shard_map/pallas_call | solution.py:58
  25.3 13.0 %all-to-all-done = f32[128,1,128]{2,1,0:T(1,128)S(1)} async-done(((f32[128,1,128]{2,1,0:T(1,128)}), f32[128,1,128]{2,1,0:T(1,128)S(1)}, u32[]{:S(2)}, u32[]{:S(2)}) %all-to-all-start) | async-done | bytes 65568 | tf_op jit(solution)/shard_map/all_to_all | solution.py:345
  38.3 1.2 shard_map.183
  39.5 5.7 %all-to-all-start.1 = ((bf16[128,8,128]{2,1,0:T(8,128)(2,1)}), bf16[128,8,128]{2,1,0:T(8,128)(2,1)S(1)}, u32[]{:S(2)}, u32[]{:S(2)}) async-start(bf16[128,8,128]{2,1,0:T(8,128)(2,1)} %bitcast.8), calls=%async_computation.1 | async-start | bytes 524288 | tf_op jit(solution)/shard_map/all_to_all | solution.py:345
  45.3 20.5 %all-to-all-done.1 = bf16[128,8,128]{2,1,0:T(8,128)(2,1)S(1)} async-done(((bf16[128,8,128]{2,1,0:T(8,128)(2,1)}), bf16[128,8,128]{2,1,0:T(8,128)(2,1)S(1)}, u32[]{:S(2)}, u32[]{:S(2)}) %all-to-all-start.1) | async-done | bytes 262176 | tf_op jit(solution)/shard_map/all_to_all | solution.py:345
  65.8 4.4 %shard_map.184 = (bf16[1024,128]{1,0:T(8,128)(2,1)}, bf16[256,512]{1,0:T(8,128)(2,1)S(1)}, bf16[256,1024]{1,0:T(8,128)(2,1)S(1)}, bf16[512,128]{1,0:T(8,128)(2,1)S(1)}, f32[8,128]{1,0:T(8,128)S(1)}) custom-call(bf16[1024,128]{1,0:T(8,128)(2,1)S(1)} %bitcast.20, f32[512,128]{1,0:T(8,128)S(1)} %get-tuple-element.37.refs_0_.refs_1_, ...), custom_call_target="tpu_custom_call" | custom-call | flops 1000000000 | bytes 10000000 | tf_op jit(solution)/shard_map/pallas_call | solution.py:58
  70.9 3.3 %shard_map.185 = (s16[256,1408]{1,0:T(8,128)(2,1)S(1)}, f32[512,128]{1,0:T(8,128)S(1)}, f32[1024,128]{1,0:T(8,128)}) custom-call(s32[2]{0:T(128)S(1)} %pad_add_fusion.refs_0_, s32[3]{0:T(128)S(1)} %copy-done.4, bf16[256,512]{1,0:T(8,128)(2,1)S(1)} %get-tuple-element.41.refs_2_.refs_1_, bf16[256,1024]{1,0:T(8,128)(2,1)S(1)} %get-tuple-element.42.refs_3_.refs_2_, ...), custom_call_target="tpu_custom_call" | custom-call | flops 1000000000 | bytes 10000000 | tf_op jit(solution)/shard_map/pallas_call | solution.py:58
  74.2 0.7 copy-done.8
  74.9 2.4 %collective-permute-start = (s16[256,1408]{1,0:T(8,128)(2,1)S(1)}, s16[256,1408]{1,0:T(8,128)(2,1)S(1)}, u32[]{:S(2)}, u32[]{:S(2)}) collective-permute-start(s16[256,1408]{1,0:T(8,128)(2,1)S(1)} %get-tuple-element.49), channel_id=1, source_target_pairs={{0,4},{4,0},{1,5},{5,1},{2,6},{6,2},{3,7},{7,3},{8,12},{12,8},{9,1... | collective-permute-start | bytes 2162696 | tf_op jit(solution)/shard_map/ppermute | solution.py:431
  77.3 8.1 %all-to-all-start.2 = ((bf16[128,8,128]{2,1,0:T(8,128)(2,1)}), bf16[128,8,128]{2,1,0:T(8,128)(2,1)S(1)}, u32[]{:S(2)}, u32[]{:S(2)}) async-start(bf16[128,8,128]{2,1,0:T(8,128)(2,1)} %bitcast.12), calls=%async_computation.2 | async-start | bytes 524288 | tf_op jit(solution)/shard_map/all_to_all | solution.py:345
  85.5 0.9 copy-done.9
  86.4 1.3 shard_map.186
  87.7 3.2 %collective-permute-start.1 = (s16[64,1408]{1,0:T(8,128)(2,1)S(1)}, s16[64,1408]{1,0:T(8,128)(2,1)S(1)}, u32[]{:S(2)}, u32[]{:S(2)}) collective-permute-start(s16[64,1408]{1,0:T(8,128)(2,1)S(1)} %get-tuple-element.51), channel_id=1, source_target_pairs={{0,1},{1,0},{2,3},{3,2},{4,5},{5,4},{6,7},{7,6},{8,9},{9,8},{10,11... | collective-permute-start | bytes 540680 | tf_op jit(solution)/shard_map/ppermute | solution.py:349
  90.9 4.5 %collective-permute-start.2 = (s16[64,1408]{1,0:T(8,128)(2,1)S(1)}, s16[64,1408]{1,0:T(8,128)(2,1)S(1)}, u32[]{:S(2)}, u32[]{:S(2)}) collective-permute-start(s16[64,1408]{1,0:T(8,128)(2,1)S(1)} %get-tuple-element.52), channel_id=1, source_target_pairs={{0,2},{1,3},{2,0},{3,1},{4,6},{5,7},{6,4},{7,5},{8,10},{9,11},{10,... | collective-permute-start | bytes 540680 | tf_op jit(solution)/shard_map/ppermute | solution.py:349
  95.5 2.1 %collective-permute-start.3 = (s16[64,1408]{1,0:T(8,128)(2,1)S(1)}, s16[64,1408]{1,0:T(8,128)(2,1)S(1)}, u32[]{:S(2)}, u32[]{:S(2)}) collective-permute-start(s16[64,1408]{1,0:T(8,128)(2,1)S(1)} %get-tuple-element.53), channel_id=1, source_target_pairs={{0,3},{1,2},{2,1},{3,0},{4,7},{5,6},{6,5},{7,4},{8,11},{9,10},{10,... | collective-permute-start | bytes 540680 | tf_op jit(solution)/shard_map/ppermute | solution.py:349
  97.6 3.5 %collective-permute-done.2.refs_2_ = s16[64,1408]{1,0:T(8,128)(2,1)S(1)} collective-permute-done((s16[64,1408]{1,0:T(8,128)(2,1)S(1)}, s16[64,1408]{1,0:T(8,128)(2,1)S(1)}, u32[]{:S(2)}, u32[]{:S(2)}) %collective-permute-start.2) | collective-permute-done | bytes 180256 | tf_op jit(solution)/shard_map/ppermute | solution.py:349
  101.1 4.3 %collective-permute-done.3.refs_3_ = s16[64,1408]{1,0:T(8,128)(2,1)S(1)} collective-permute-done((s16[64,1408]{1,0:T(8,128)(2,1)S(1)}, s16[64,1408]{1,0:T(8,128)(2,1)S(1)}, u32[]{:S(2)}, u32[]{:S(2)}) %collective-permute-start.3) | collective-permute-done | bytes 180256 | tf_op jit(solution)/shard_map/ppermute | solution.py:349
  105.9 10.2 %all_to_all.30.refs_0_ = s16[4,16,1408]{2,1,0:T(8,128)(2,1)S(1)} all-to-all(s16[4,16,1408]{2,1,0:T(8,128)(2,1)S(1)} %bitcast.22), channel_id=1, replica_groups=mesh['dp_0'=16,'dp_1'=4,'dp_2'=2,'rep'=4] {'dp_1'}, dimensions={0} | all-to-all | bytes 360448 | tf_op jit(solution)/shard_map/all_to_all | solution.py:345
  116.1 0.8 shard_map.191
  116.9 10.9 %all-to-all-start.4 = ((f32[16,24,128]{2,1,0:T(8,128)}), f32[16,24,128]{2,1,0:T(8,128)S(1)}, u32[]{:S(2)}, u32[]{:S(2)}) async-start(f32[16,24,128]{2,1,0:T(8,128)} %shard_map.191), calls=%async_computation.4 | async-start | bytes 393216 | tf_op jit(solution)/shard_map/all_to_all | solution.py:345
  127.8 0.8 shard_map.181.refs_0_
  129.0 2.0 %collective-permute-start.4 = (f32[512,128]{1,0:T(8,128)S(1)}, f32[512,128]{1,0:T(8,128)S(1)}, u32[]{:S(2)}, u32[]{:S(2)}) collective-permute-start(f32[512,128]{1,0:T(8,128)S(1)} %shard_map.188.refs_0_), channel_id=1, source_target_pairs={{0,1},{1,0},{2,3},{3,2},{4,5},{5,4},{6,7},{7,6},{8,9},{9,8},{10,11... | collective-permute-start | bytes 786440 | tf_op jit(solution)/shard_map/ppermute | solution.py:349
  131.0 5.4 %collective-permute-done.4.refs_1_ = f32[512,128]{1,0:T(8,128)S(1)} collective-permute-done((f32[512,128]{1,0:T(8,128)S(1)}, f32[512,128]{1,0:T(8,128)S(1)}, u32[]{:S(2)}, u32[]{:S(2)}) %collective-permute-start.4) | collective-permute-done | bytes 262176 | tf_op jit(solution)/shard_map/ppermute | solution.py:349
  136.5 2.5 %collective-permute-start.5 = (f32[512,128]{1,0:T(8,128)S(1)}, f32[512,128]{1,0:T(8,128)S(1)}, u32[]{:S(2)}, u32[]{:S(2)}) collective-permute-start(f32[512,128]{1,0:T(8,128)S(1)} %shard_map.189.refs_0_), channel_id=1, source_target_pairs={{0,3},{1,2},{2,1},{3,0},{4,7},{5,6},{6,5},{7,4},{8,11},{9,10},{10,... | collective-permute-start | bytes 786440 | tf_op jit(solution)/shard_map/ppermute | solution.py:349
  139.0 1.1 all-to-all-done.4.refs_0_
  140.1 0.7 shard_map.192
  140.9 9.3 %all-to-all-start.5 = ((f32[32,16,128]{2,1,0:T(8,128)}), f32[32,16,128]{2,1,0:T(8,128)S(1)}, u32[]{:S(2)}, u32[]{:S(2)}) async-start(f32[32,16,128]{2,1,0:T(8,128)} %get-tuple-element.59), calls=%async_computation.5 | async-start | bytes 524288 | tf_op jit(solution)/shard_map/all_to_all | solution.py:345
  150.3 0.9 shard_map.190
  151.2 7.3 %all-to-all-done.5 = f32[32,16,128]{2,1,0:T(8,128)S(1)} async-done(((f32[32,16,128]{2,1,0:T(8,128)}), f32[32,16,128]{2,1,0:T(8,128)S(1)}, u32[]{:S(2)}, u32[]{:S(2)}) %all-to-all-start.5) | async-done | bytes 262176 | tf_op jit(solution)/shard_map/all_to_all | solution.py:345
  158.5 1.7 %shard_map.193 = (f32[1024,128]{1,0:T(8,128)}, f32[1024,128]{1,0:T(8,128)}, f32[8,128]{1,0:T(8,128)}) custom-call(s32[3]{0:T(128)S(1)} %copy-done.4, s32[8]{0:T(128)S(1)} %copy-done.5, f32[512,128]{1,0:T(8,128)S(1)} %bitcast.21, f32[1024,128]{1,0:T(8,128)S(1)} %copy-done, f32[1024,128]{1,0:T(8,128)S(1)} %copy-done.1), custom_call_target="tpu_custom_call" | custom-call | flops 1000000000 | bytes 10000000 | tf_op jit(solution)/shard_map/pallas_call | solution.py:58
  (26 shorter events, 1.8 us)
Async XLA Ops:
  3.1 35.2 %all-to-all-start = ((f32[128,1,128]{2,1,0:T(1,128)}), f32[128,1,128]{2,1,0:T(1,128)S(1)}, u32[]{:S(2)}, u32[]{:S(2)}) async-start(f32[128,1,128]{2,1,0:T(1,128)} %bitcast.3), calls=%async_computation | async-start | bytes 131072 | tf_op jit(solution)/shard_map/all_to_all | solution.py:345
  39.5 26.3 %all-to-all-start.1 = ((bf16[128,8,128]{2,1,0:T(8,128)(2,1)}), bf16[128,8,128]{2,1,0:T(8,128)(2,1)S(1)}, u32[]{:S(2)}, u32[]{:S(2)}) async-start(bf16[128,8,128]{2,1,0:T(8,128)(2,1)} %bitcast.8), calls=%async_computation.1 | async-start | bytes 524288 | tf_op jit(solution)/shard_map/all_to_all | solution.py:345
  70.2 4.0 %copy-start.6 = (bf16[256,1024]{1,0:T(8,128)(2,1)}, bf16[256,1024]{1,0:T(8,128)(2,1)S(1)}, u32[]{:S(2)}) copy-start(bf16[256,1024]{1,0:T(8,128)(2,1)S(1)} %get-tuple-element.42.refs_3_.refs_2_) | copy-start | bytes 1572868
  70.2 0.7 copy-start.4
  74.2 0.7 copy-start.8
  74.9 10.6 %copy-start.7 = (bf16[256,1024]{1,0:T(8,128)(2,1)S(1)}, bf16[256,1024]{1,0:T(8,128)(2,1)}, u32[]{:S(2)}) copy-start(bf16[256,1024]{1,0:T(8,128)(2,1)} %copy-done.6) | copy-start | bytes 1572868
  74.9 10.6 %collective-permute-start = (s16[256,1408]{1,0:T(8,128)(2,1)S(1)}, s16[256,1408]{1,0:T(8,128)(2,1)S(1)}, u32[]{:S(2)}, u32[]{:S(2)}) collective-permute-start(s16[256,1408]{1,0:T(8,128)(2,1)S(1)} %get-tuple-element.49), channel_id=1, source_target_pairs={{0,4},{4,0},{1,5},{5,1},{2,6},{6,2},{3,7},{7,3},{8,12},{12,8},{9,1... | collective-permute-start | bytes 2162696 | tf_op jit(solution)/shard_map/ppermute | solution.py:431
  77.3 28.6 %all-to-all-start.2 = ((bf16[128,8,128]{2,1,0:T(8,128)(2,1)}), bf16[128,8,128]{2,1,0:T(8,128)(2,1)S(1)}, u32[]{:S(2)}, u32[]{:S(2)}) async-start(bf16[128,8,128]{2,1,0:T(8,128)(2,1)} %bitcast.12), calls=%async_computation.2 | async-start | bytes 524288 | tf_op jit(solution)/shard_map/all_to_all | solution.py:345
  85.4 1.0 copy-start.9
  87.7 9.9 %collective-permute-start.1 = (s16[64,1408]{1,0:T(8,128)(2,1)S(1)}, s16[64,1408]{1,0:T(8,128)(2,1)S(1)}, u32[]{:S(2)}, u32[]{:S(2)}) collective-permute-start(s16[64,1408]{1,0:T(8,128)(2,1)S(1)} %get-tuple-element.51), channel_id=1, source_target_pairs={{0,1},{1,0},{2,3},{3,2},{4,5},{5,4},{6,7},{7,6},{8,9},{9,8},{10,11... | collective-permute-start | bytes 540680 | tf_op jit(solution)/shard_map/ppermute | solution.py:349
  90.9 10.2 %collective-permute-start.2 = (s16[64,1408]{1,0:T(8,128)(2,1)S(1)}, s16[64,1408]{1,0:T(8,128)(2,1)S(1)}, u32[]{:S(2)}, u32[]{:S(2)}) collective-permute-start(s16[64,1408]{1,0:T(8,128)(2,1)S(1)} %get-tuple-element.52), channel_id=1, source_target_pairs={{0,2},{1,3},{2,0},{3,1},{4,6},{5,7},{6,4},{7,5},{8,10},{9,11},{10,... | collective-permute-start | bytes 540680 | tf_op jit(solution)/shard_map/ppermute | solution.py:349
  95.5 9.9 %collective-permute-start.3 = (s16[64,1408]{1,0:T(8,128)(2,1)S(1)}, s16[64,1408]{1,0:T(8,128)(2,1)S(1)}, u32[]{:S(2)}, u32[]{:S(2)}) collective-permute-start(s16[64,1408]{1,0:T(8,128)(2,1)S(1)} %get-tuple-element.53), channel_id=1, source_target_pairs={{0,3},{1,2},{2,1},{3,0},{4,7},{5,6},{6,5},{7,4},{8,11},{9,10},{10,... | collective-permute-start | bytes 540680 | tf_op jit(solution)/shard_map/ppermute | solution.py:349
  116.9 23.3 %all-to-all-start.4 = ((f32[16,24,128]{2,1,0:T(8,128)}), f32[16,24,128]{2,1,0:T(8,128)S(1)}, u32[]{:S(2)}, u32[]{:S(2)}) async-start(f32[16,24,128]{2,1,0:T(8,128)} %shard_map.191), calls=%async_computation.4 | async-start | bytes 393216 | tf_op jit(solution)/shard_map/all_to_all | solution.py:345
  129.0 7.4 %collective-permute-start.4 = (f32[512,128]{1,0:T(8,128)S(1)}, f32[512,128]{1,0:T(8,128)S(1)}, u32[]{:S(2)}, u32[]{:S(2)}) collective-permute-start(f32[512,128]{1,0:T(8,128)S(1)} %shard_map.188.refs_0_), channel_id=1, source_target_pairs={{0,1},{1,0},{2,3},{3,2},{4,5},{5,4},{6,7},{7,6},{8,9},{9,8},{10,11... | collective-permute-start | bytes 786440 | tf_op jit(solution)/shard_map/ppermute | solution.py:349
  136.5 13.8 %collective-permute-start.5 = (f32[512,128]{1,0:T(8,128)S(1)}, f32[512,128]{1,0:T(8,128)S(1)}, u32[]{:S(2)}, u32[]{:S(2)}) collective-permute-start(f32[512,128]{1,0:T(8,128)S(1)} %shard_map.189.refs_0_), channel_id=1, source_target_pairs={{0,3},{1,2},{2,1},{3,0},{4,7},{5,6},{6,5},{7,4},{8,11},{9,10},{10,... | collective-permute-start | bytes 786440 | tf_op jit(solution)/shard_map/ppermute | solution.py:349
  140.9 9.4 %copy-start.2 = (f32[512,128]{1,0:T(8,128)S(1)}, f32[512,128]{1,0:T(8,128)}, u32[]{:S(2)}) copy-start(f32[512,128]{1,0:T(8,128)} %refs_2_.3) | copy-start | bytes 786436
  140.9 9.4 %copy-start.3 = (f32[512,128]{1,0:T(8,128)S(1)}, f32[512,128]{1,0:T(8,128)}, u32[]{:S(2)}) copy-start(f32[512,128]{1,0:T(8,128)} %refs_3_.4) | copy-start | bytes 786436
  140.9 17.6 %all-to-all-start.5 = ((f32[32,16,128]{2,1,0:T(8,128)}), f32[32,16,128]{2,1,0:T(8,128)S(1)}, u32[]{:S(2)}, u32[]{:S(2)}) async-start(f32[32,16,128]{2,1,0:T(8,128)} %get-tuple-element.59), calls=%async_computation.5 | async-start | bytes 524288 | tf_op jit(solution)/shard_map/all_to_all | solution.py:345
  150.2 8.3 %copy-start = (f32[1024,128]{1,0:T(8,128)S(1)}, f32[1024,128]{1,0:T(8,128)}, u32[]{:S(2)}) copy-start(f32[1024,128]{1,0:T(8,128)} %refs_3_.5) | copy-start | bytes 1572868
  150.2 8.3 %copy-start.1 = (f32[1024,128]{1,0:T(8,128)S(1)}, f32[1024,128]{1,0:T(8,128)}, u32[]{:S(2)}) copy-start(f32[1024,128]{1,0:T(8,128)} %refs_4_.3) | copy-start | bytes 1572868
  151.2 7.3 %copy-start.5 = (s32[8]{0:T(128)S(1)}, s32[8]{0:T(128)}, u32[]{:S(2)}) copy-start(s32[8]{0:T(128)} %refs_1_.3) | copy-start | bytes 100

commit v5 on v4

--- a/solution.py
+++ b/solution.py
@@ -8,6 +8,7 @@
 
 BLOCK = 128
 SLOTS = 8
+REFRESHED = 3
 DP = ("dp_0", "dp_1", "dp_2")
 DP_REP = ("dp_0", "dp_1", "dp_2", "rep")
 PLANE = ("dp_2", "rep", "dp_1")
@@ -37,7 +38,7 @@
         return self.held
 
 
-def call(kernel, outs, args, smem=0, scratch=(), loads=(), held=(), kept=()):
+def call(kernel, outs, args, smem=0, scratch=(), loads=(), held=(), kept=(), flops=10**9):
     own = len(scratch)
     ins = len(args)
 
@@ -64,7 +65,7 @@
         + [pltpu.VMEM(args[i].shape, args[i].dtype) for i in loads]
         + [pltpu.SemaphoreType.DMA for _ in loads],
         compiler_params=pltpu.CompilerParams(vmem_limit_bytes=16 * 2**20),
-        cost_estimate=pl.CostEstimate(flops=10**9, bytes_accessed=10**7, transcendentals=0),
+        cost_estimate=pl.CostEstimate(flops=flops, bytes_accessed=flops // 100, transcendentals=0),
     )(*args)
 
 
@@ -169,7 +170,7 @@
     owned_ref[...] = ones_where(iota_f(owned_ref.shape, 0) == wanted)
 
 
-def masks_kernel(target_ref, hot_ref, cache_ref, table_ref, rows_ref, hot_in_ref, hot_put_ref, narrow_ref):
+def masks_kernel(target_ref, hot_ref, cache_ref, table_ref, rows_ref, hot_in_ref, hot_rows_ref, narrow_ref):
     square = (BLOCK, BLOCK)
     eye = iota(square, 0) == iota(square, 1)
     hot = hot_ref.wait()[...].astype(F32)
@@ -182,13 +183,12 @@
             rows_ref[:, at : at + BLOCK] = jnp.broadcast_to(row, (8, BLOCK))
     cache = cache_ref.wait()[...].astype(BF16)
     hot_count = cache.shape[0]
-    hot_row = iota_f((hot_count, BLOCK), 0)
     hot_lane = iota_f((BLOCK, hot_count), 1)
     for k in range(feats):
         for h in range(samples // BLOCK):
             at = k * samples + h * BLOCK
             row = hot[k : k + 1, h * BLOCK : (h + 1) * BLOCK]
-            hot_put_ref[:, at : at + BLOCK] = ones_where(hot_row == row)
+            hot_rows_ref[:, at : at + BLOCK] = jnp.broadcast_to(row, (8, BLOCK))
             chosen = ones_where(column_of(row, eye) == hot_lane)
             hot_in_ref[h * BLOCK : (h + 1) * BLOCK, k * BLOCK : (k + 1) * BLOCK] = dot(chosen, cache).astype(BF16)
     narrow_ref[...] = table_ref.wait()[...].astype(BF16)
@@ -211,7 +211,7 @@
     cold = dot(jnp.concatenate(take, axis=0), returned_ref[...]).astype(BF16)
     inputs = jnp.concatenate([hot_in_ref[...], cold[:samples], cold[samples:]], axis=1)
     inputs_ref[...] = inputs
-    weight = weight_ref.wait()[...]
+    weight = weight_ref[...]
     out_weight = out_weight_ref.wait()[...]
     preact = dot(inputs, weight)
     gates = jax.nn.sigmoid(preact)
@@ -248,12 +248,13 @@
 
 
 def send_kernel(
-    place_ref, refresh_ref, inputs_ref, dhidden_ref, hot_put_ref, hot_dx_ref, head_ref, pending_ref,
+    control_ref, inputs_ref, dhidden_ref, hot_rows_ref, hot_dx_ref, head_ref, pending_ref,
     send_ref, picked_ref, pending_new_ref,
 ):
-    pending_new_ref[...] = dot(hot_put_ref[...], hot_dx_ref[...]) + pending_ref.wait()[...]
-    count = refresh_ref.shape[0]
-    blocks = [pl.ds(pl.multiple_of(refresh_ref[i] * BLOCK, BLOCK), BLOCK) for i in range(count)]
+    put = ones_where(iota_f((pending_ref.shape[0], hot_rows_ref.shape[1]), 0) == hot_rows_ref[:1, :])
+    pending_new_ref[...] = dot(put, hot_dx_ref[...]) + pending_ref[...]
+    count = REFRESHED
+    blocks = [pl.ds(pl.multiple_of(control_ref[2 + i] * BLOCK, BLOCK), BLOCK) for i in range(count)]
     for i, at in enumerate(blocks):
         picked_ref[i * BLOCK : (i + 1) * BLOCK, :] = pending_new_ref[at, :]
     end = count * BLOCK
@@ -261,14 +262,14 @@
     picked_ref[end + 8 :, :] = jnp.zeros((picked_ref.shape[0] - end - 8, BLOCK), F32)
     for at in blocks:
         pending_new_ref[at, :] = jnp.zeros((BLOCK, BLOCK), F32)
-    core, rep = 1 - place_ref[0], place_ref[1]
+    core, rep = 1 - control_ref[0], control_ref[1]
     top = half_of_top(core, rep, inputs_ref[...], dhidden_ref[...])
     hot = jnp.concatenate([hot_rows(picked_ref, core, rep, d) for d in range(4)], axis=0)
     pack(jnp.concatenate([top, hot], axis=1), send_ref)
 
 
-def pair_kernel(place_ref, inputs_ref, dhidden_ref, picked_ref, received_ref, own_ref, *pieces):
-    core, rep = place_ref[0], place_ref[1]
+def pair_kernel(control_ref, inputs_ref, dhidden_ref, picked_ref, received_ref, own_ref, *pieces):
+    core, rep = control_ref[0], control_ref[1]
     top = half_of_top(core, rep, inputs_ref[...], dhidden_ref[...])
     tall = own_ref.shape[0]
     for d, piece in enumerate((own_ref, *pieces)):
@@ -313,14 +314,14 @@
     return (table_rows - step_size * gradient / (jnp.sqrt(accum_next) + epsilon), accum_next)
 
 
-def hot_kernel(refresh_ref, clock_ref, sums_ref, cache_ref, accum_ref, cache_new_ref, accum_new_ref, out_grad_ref):
+def hot_kernel(control_ref, sums_ref, cache_ref, accum_ref, cache_new_ref, accum_new_ref, out_grad_ref):
     cache_new_ref[...] = cache_ref[...]
     accum_new_ref[...] = accum_ref[...]
-    count = refresh_ref.shape[0]
+    count = REFRESHED
     for i in range(count):
-        block = refresh_ref[i]
+        block = control_ref[2 + i]
         at = pl.ds(pl.multiple_of(block * BLOCK, BLOCK), BLOCK)
-        flush = sums_ref[i * BLOCK : (i + 1) * BLOCK, :] / (1.0 + clock_ref[block].astype(F32))
+        flush = sums_ref[i * BLOCK : (i + 1) * BLOCK, :] / (1.0 + control_ref[2 + count + block].astype(F32))
         cache_next, accum_next = adagrad(cache_ref[at, :], accum_ref[at, :], flush)
         cache_new_ref[at, :] = cache_next
         accum_new_ref[at, :] = accum_next
@@ -373,6 +374,7 @@
     slots = owners * SLOTS
     groups = lookups // BLOCK
     place = jnp.stack([lax.axis_index("dp_2"), lax.axis_index("rep")]).astype(jnp.int32)
+    control = jnp.concatenate([place, refresh_blocks, block_clock])
 
     request, target = call(
         requests_kernel,
@@ -382,12 +384,12 @@
         kept=(1,),
     )
     asked = swap(request.reshape(owners, 1, BLOCK), DP).reshape(owners, BLOCK)
-    target_rows, hot_in, hot_put, narrow = call(
+    target_rows, hot_in, hot_id_rows, narrow = call(
         masks_kernel,
         [
             ((8, lookups), F32),
             ((samples, feats * width), BF16),
-            ((hot_count, samples * feats), BF16),
+            ((8, samples * feats), F32),
             ((own_rows, width), BF16),
         ],
         (target, hot_ids.T, hot_cache, cold_table),
@@ -408,7 +410,7 @@
             ((8, BLOCK), F32),
         ],
         (returned, target, target_rows, hot_in, top_weight, out_weight.reshape(1, hidden_width), labels.reshape(2, BLOCK)),
-        loads=(4, 5, 6),
+        loads=(5, 6),
         held=(1, 2, 3),
         kept=(1, 2, 3, 4),
     )
@@ -421,11 +423,11 @@
     send, picked, pending_new = call(
         send_kernel,
         [((half, packed), I16), ((plane_size * far, BLOCK), F32), ((hot_count, width), F32)],
-        (place, refresh_blocks, inputs, dhidden, hot_put, hot_dx, head, pending),
-        smem=2,
-        loads=(7,),
-        held=(2, 3, 4, 5, 6),
+        (control, inputs, dhidden, hot_id_rows, hot_dx, head, pending),
+        smem=1,
+        held=(1, 2, 3, 4, 5),
         kept=(1,),
+        flops=10**9,
     )
     send, outgoing = lax.optimization_barrier((send, outgoing))
     received = lax.ppermute(send, "dp_2", [(0, 1), (1, 0)])
@@ -433,7 +435,7 @@
     pieces = call(
         pair_kernel,
         [((half // 4, broad), F32)] + [((half // 4, packed), I16)] * 3,
-        (place, inputs, dhidden, picked, received),
+        (control, inputs, dhidden, picked, received),
         smem=1,
         held=(1, 2, 3),
     )
@@ -455,8 +457,8 @@
     hot_cache_new, hot_accum_new, out_grad = call(
         hot_kernel,
         [((hot_count, width), F32)] * 2 + [((8, BLOCK), F32)],
-        (refresh_blocks, block_clock, sums, hot_cache, hot_accum),
-        smem=2,
+        (control, sums, hot_cache, hot_accum),
+        smem=1,
     )
     return (
         cold_table_new,

time: 161 us -> 157 us (0.975)
  Pallas kernels: 20.1 us -> 18.2 us
  local copies, waits for them, and re-layouts: 2.35 us -> 0.69 us
    pallas_call x14, Pallas kernels: 20.1 us -> 18.2 us  [call(): pl.pallas_call(body, out_shape=[(pltpu.VMEM if i in kept else jax.ShapeDt...]
    unnamed x20 -> x16, local copies, waits for them, and re-layouts: 2.35 us -> 0.69 us
where the time goes in v5:
time: 157 us; the launch traced here: 156 us
  starting transfers between devices  70.2 us (45%)
  waiting for transfers between devices  56.2 us (36%)
  Pallas kernels  18.2 us (12%)
  blocking collectives  10.2 us (6%)
    all_to_all x5, starting transfers between devices, swap(): return lax.all_to_all(x, axis, split_axis=0, concat_axis=0, tiled=True)  53.7 us
    all_to_all x5, waiting for transfers between devices, swap(): return lax.all_to_all(x, axis, split_axis=0, concat_axis=0, tiled=True)  42.7 us
    pallas_call x14, Pallas kernels, call(): pl.pallas_call(body, out_shape=[(pltpu.VMEM if i in kept else jax.ShapeDt...  18.2 us
    ppermute x5, starting transfers between devices, from_rep(): return lax.ppermute(piece, 'rep', [(i, i ^ distance) for i in range(4)])  14.1 us
    ppermute x5, waiting for transfers between devices, from_rep(): return lax.ppermute(piece, 'rep', [(i, i ^ distance) for i in range(4)])  13.5 us
    all_to_all x1, blocking collectives, swap(): return lax.all_to_all(x, axis, split_axis=0, concat_axis=0, tiled=True)  10.2 us
  transfers between devices with their start and end apart: 11, of which 8 were waited for; matrix products, arithmetic and copies ran while one was open for 0% of the time, Pallas kernels for 4%

profile of v5, /device:TPU:1, one launch (start us, length us, event | category | flops | bytes accessed | tf_op | source)
XLA Modules:
  0.0 156.3 jit_solution(16482985874253524886)
XLA Ops:
  0.6 2.4 %shard_map.180 = (f32[128,128]{1,0:T(8,128)}, f32[512,128]{1,0:T(8,128)S(1)}) custom-call(s32[4,128]{1,0:T(4,128)} %bitcast.26, s32[4,128]{1,0:T(4,128)} %bitcast.27), custom_call_target="tpu_custom_call" | custom-call | flops 1000000000 | bytes 10000000 | tf_op jit(solution)/shard_map/pallas_call | solution.py:59
  3.1 20.4 %all-to-all-start = ((f32[128,1,128]{2,1,0:T(1,128)}), f32[128,1,128]{2,1,0:T(1,128)S(1)}, u32[]{:S(2)}, u32[]{:S(2)}) async-start(f32[128,1,128]{2,1,0:T(1,128)} %bitcast.3), calls=%async_computation | async-start | bytes 131072 | tf_op jit(solution)/shard_map/all_to_all | solution.py:346
  23.5 1.6 %shard_map.182 = (f32[8,512]{1,0:T(8,128)S(1)}, bf16[256,256]{1,0:T(8,128)(2,1)S(1)}, f32[8,512]{1,0:T(8,128)S(1)}, bf16[512,128]{1,0:T(8,128)(2,1)S(1)}) custom-call(f32[512,128]{1,0:T(8,128)S(1)} %get-tuple-element.37.refs_0_.refs_1_, s32[2,256]{1,0:T(2,128)} %bitcast.28, f32[1024,128]{1,0:T(8,128)} %refs_2_.5, f32[512,128]{1,0:T(8,128)} %refs_2_.4), custom_call_target="tpu_custom_call" | custom-call | flops 1000000000 | bytes 10000000 | tf_op jit(solution)/shard_map/pallas_call | solution.py:59
  25.1 13.2 %all-to-all-done = f32[128,1,128]{2,1,0:T(1,128)S(1)} async-done(((f32[128,1,128]{2,1,0:T(1,128)}), f32[128,1,128]{2,1,0:T(1,128)S(1)}, u32[]{:S(2)}, u32[]{:S(2)}) %all-to-all-start) | async-done | bytes 65568 | tf_op jit(solution)/shard_map/all_to_all | solution.py:346
  38.3 1.2 shard_map.183
  39.5 5.7 %all-to-all-start.1 = ((bf16[128,8,128]{2,1,0:T(8,128)(2,1)}), bf16[128,8,128]{2,1,0:T(8,128)(2,1)S(1)}, u32[]{:S(2)}, u32[]{:S(2)}) async-start(bf16[128,8,128]{2,1,0:T(8,128)(2,1)} %bitcast.8), calls=%async_computation.1 | async-start | bytes 524288 | tf_op jit(solution)/shard_map/all_to_all | solution.py:346
  45.2 0.6 copy-done.6
  45.9 19.9 %all-to-all-done.1 = bf16[128,8,128]{2,1,0:T(8,128)(2,1)S(1)} async-done(((bf16[128,8,128]{2,1,0:T(8,128)(2,1)}), bf16[128,8,128]{2,1,0:T(8,128)(2,1)S(1)}, u32[]{:S(2)}, u32[]{:S(2)}) %all-to-all-start.1) | async-done | bytes 262176 | tf_op jit(solution)/shard_map/all_to_all | solution.py:346
  65.8 3.8 %shard_map.184 = (bf16[1024,128]{1,0:T(8,128)(2,1)}, bf16[256,512]{1,0:T(8,128)(2,1)S(1)}, bf16[256,1024]{1,0:T(8,128)(2,1)S(1)}, bf16[512,128]{1,0:T(8,128)(2,1)S(1)}, f32[8,128]{1,0:T(8,128)S(1)}) custom-call(bf16[1024,128]{1,0:T(8,128)(2,1)S(1)} %bitcast.20, f32[512,128]{1,0:T(8,128)S(1)} %get-tuple-element.37.refs_0_.refs_1_, ...), custom_call_target="tpu_custom_call" | custom-call | flops 1000000000 | bytes 10000000 | tf_op jit(solution)/shard_map/pallas_call | solution.py:59
  69.6 2.2 %shard_map.185 = (s16[256,1408]{1,0:T(8,128)(2,1)S(1)}, f32[512,128]{1,0:T(8,128)S(1)}, f32[1024,128]{1,0:T(8,128)}) custom-call(s32[13]{0:T(128)S(1)} %pad_add_fusion.refs_0_, bf16[256,512]{1,0:T(8,128)(2,1)S(1)} %get-tuple-element.41.refs_1_, bf16[256,1024]{1,0:T(8,128)(2,1)S(1)} %get-tuple-element.42.refs_2_, f32[8,512]{1,0:T(8,128)S(1)} %get-tuple-element.43.refs_3_, ...), custom_call_target="tpu_custom_call" | custom-call | flops 1000000000 | bytes 10000000 | tf_op jit(solution)/shard_map/pallas_call | solution.py:59
  71.8 2.3 %collective-permute-start = (s16[256,1408]{1,0:T(8,128)(2,1)S(1)}, s16[256,1408]{1,0:T(8,128)(2,1)S(1)}, u32[]{:S(2)}, u32[]{:S(2)}) collective-permute-start(s16[256,1408]{1,0:T(8,128)(2,1)S(1)} %get-tuple-element.49), channel_id=1, source_target_pairs={{0,4},{4,0},{1,5},{5,1},{2,6},{6,2},{3,7},{7,3},{8,12},{12,8},{9,1... | collective-permute-start | bytes 2162696 | tf_op jit(solution)/shard_map/ppermute | solution.py:433
  74.1 8.1 %all-to-all-start.2 = ((bf16[128,8,128]{2,1,0:T(8,128)(2,1)}), bf16[128,8,128]{2,1,0:T(8,128)(2,1)S(1)}, u32[]{:S(2)}, u32[]{:S(2)}) async-start(bf16[128,8,128]{2,1,0:T(8,128)(2,1)} %bitcast.12), calls=%async_computation.2 | async-start | bytes 524288 | tf_op jit(solution)/shard_map/all_to_all | solution.py:346
  82.3 1.3 shard_map.186
  83.6 3.2 %collective-permute-start.1 = (s16[64,1408]{1,0:T(8,128)(2,1)S(1)}, s16[64,1408]{1,0:T(8,128)(2,1)S(1)}, u32[]{:S(2)}, u32[]{:S(2)}) collective-permute-start(s16[64,1408]{1,0:T(8,128)(2,1)S(1)} %get-tuple-element.51), channel_id=1, source_target_pairs={{0,1},{1,0},{2,3},{3,2},{4,5},{5,4},{6,7},{7,6},{8,9},{9,8},{10,11... | collective-permute-start | bytes 540680 | tf_op jit(solution)/shard_map/ppermute | solution.py:350
  86.8 4.5 %collective-permute-start.2 = (s16[64,1408]{1,0:T(8,128)(2,1)S(1)}, s16[64,1408]{1,0:T(8,128)(2,1)S(1)}, u32[]{:S(2)}, u32[]{:S(2)}) collective-permute-start(s16[64,1408]{1,0:T(8,128)(2,1)S(1)} %get-tuple-element.52), channel_id=1, source_target_pairs={{0,2},{1,3},{2,0},{3,1},{4,6},{5,7},{6,4},{7,5},{8,10},{9,11},{10,... | collective-permute-start | bytes 540680 | tf_op jit(solution)/shard_map/ppermute | solution.py:350
  91.3 2.1 %collective-permute-start.3 = (s16[64,1408]{1,0:T(8,128)(2,1)S(1)}, s16[64,1408]{1,0:T(8,128)(2,1)S(1)}, u32[]{:S(2)}, u32[]{:S(2)}) collective-permute-start(s16[64,1408]{1,0:T(8,128)(2,1)S(1)} %get-tuple-element.53), channel_id=1, source_target_pairs={{0,3},{1,2},{2,1},{3,0},{4,7},{5,6},{6,5},{7,4},{8,11},{9,10},{10,... | collective-permute-start | bytes 540680 | tf_op jit(solution)/shard_map/ppermute | solution.py:350
  93.4 3.5 %collective-permute-done.2.refs_2_ = s16[64,1408]{1,0:T(8,128)(2,1)S(1)} collective-permute-done((s16[64,1408]{1,0:T(8,128)(2,1)S(1)}, s16[64,1408]{1,0:T(8,128)(2,1)S(1)}, u32[]{:S(2)}, u32[]{:S(2)}) %collective-permute-start.2) | collective-permute-done | bytes 180256 | tf_op jit(solution)/shard_map/ppermute | solution.py:350
  97.0 4.5 %collective-permute-done.3.refs_3_ = s16[64,1408]{1,0:T(8,128)(2,1)S(1)} collective-permute-done((s16[64,1408]{1,0:T(8,128)(2,1)S(1)}, s16[64,1408]{1,0:T(8,128)(2,1)S(1)}, u32[]{:S(2)}, u32[]{:S(2)}) %collective-permute-start.3) | collective-permute-done | bytes 180256 | tf_op jit(solution)/shard_map/ppermute | solution.py:350
  101.7 1.0 all-to-all-done.2
  102.7 10.2 %all_to_all.30.refs_0_ = s16[4,16,1408]{2,1,0:T(8,128)(2,1)S(1)} all-to-all(s16[4,16,1408]{2,1,0:T(8,128)(2,1)S(1)} %bitcast.22), channel_id=1, replica_groups=mesh['dp_0'=16,'dp_1'=4,'dp_2'=2,'rep'=4] {'dp_1'}, dimensions={0} | all-to-all | bytes 360448 | tf_op jit(solution)/shard_map/all_to_all | solution.py:346
  112.9 0.8 shard_map.191
  113.7 10.2 %all-to-all-start.4 = ((f32[16,24,128]{2,1,0:T(8,128)}), f32[16,24,128]{2,1,0:T(8,128)S(1)}, u32[]{:S(2)}, u32[]{:S(2)}) async-start(f32[16,24,128]{2,1,0:T(8,128)} %shard_map.191), calls=%async_computation.4 | async-start | bytes 393216 | tf_op jit(solution)/shard_map/all_to_all | solution.py:346
  123.8 0.8 shard_map.181.refs_0_
  125.1 1.9 %collective-permute-start.4 = (f32[512,128]{1,0:T(8,128)S(1)}, f32[512,128]{1,0:T(8,128)S(1)}, u32[]{:S(2)}, u32[]{:S(2)}) collective-permute-start(f32[512,128]{1,0:T(8,128)S(1)} %shard_map.188.refs_0_), channel_id=1, source_target_pairs={{0,1},{1,0},{2,3},{3,2},{4,5},{5,4},{6,7},{7,6},{8,9},{9,8},{10,11... | collective-permute-start | bytes 786440 | tf_op jit(solution)/shard_map/ppermute | solution.py:350
  127.0 5.5 %collective-permute-done.4.refs_1_ = f32[512,128]{1,0:T(8,128)S(1)} collective-permute-done((f32[512,128]{1,0:T(8,128)S(1)}, f32[512,128]{1,0:T(8,128)S(1)}, u32[]{:S(2)}, u32[]{:S(2)}) %collective-permute-start.4) | collective-permute-done | bytes 262176 | tf_op jit(solution)/shard_map/ppermute | solution.py:350
  132.5 2.4 %collective-permute-start.5 = (f32[512,128]{1,0:T(8,128)S(1)}, f32[512,128]{1,0:T(8,128)S(1)}, u32[]{:S(2)}, u32[]{:S(2)}) collective-permute-start(f32[512,128]{1,0:T(8,128)S(1)} %shard_map.189.refs_0_), channel_id=1, source_target_pairs={{0,3},{1,2},{2,1},{3,0},{4,7},{5,6},{6,5},{7,4},{8,11},{9,10},{10,... | collective-permute-start | bytes 786440 | tf_op jit(solution)/shard_map/ppermute | solution.py:350
  134.9 1.3 all-to-all-done.4.refs_0_
  136.2 0.7 shard_map.192
  136.9 9.4 %all-to-all-start.5 = ((f32[32,16,128]{2,1,0:T(8,128)}), f32[32,16,128]{2,1,0:T(8,128)S(1)}, u32[]{:S(2)}, u32[]{:S(2)}) async-start(f32[32,16,128]{2,1,0:T(8,128)} %get-tuple-element.59), calls=%async_computation.5 | async-start | bytes 524288 | tf_op jit(solution)/shard_map/all_to_all | solution.py:346
  146.4 0.9 shard_map.190
  147.3 7.3 %all-to-all-done.5 = f32[32,16,128]{2,1,0:T(8,128)S(1)} async-done(((f32[32,16,128]{2,1,0:T(8,128)}), f32[32,16,128]{2,1,0:T(8,128)S(1)}, u32[]{:S(2)}, u32[]{:S(2)}) %all-to-all-start.5) | async-done | bytes 262176 | tf_op jit(solution)/shard_map/all_to_all | solution.py:346
  154.6 1.7 %shard_map.193 = (f32[1024,128]{1,0:T(8,128)}, f32[1024,128]{1,0:T(8,128)}, f32[8,128]{1,0:T(8,128)}) custom-call(s32[13]{0:T(128)S(1)} %pad_add_fusion.refs_0_, f32[512,128]{1,0:T(8,128)S(1)} %bitcast.21, f32[1024,128]{1,0:T(8,128)S(1)} %copy-done.2, f32[1024,128]{1,0:T(8,128)S(1)} %copy-done.3), custom_call_target="tpu_custom_call" | custom-call | flops 1000000000 | bytes 10000000 | tf_op jit(solution)/shard_map/pallas_call | solution.py:59
  (22 shorter events, 0.9 us)
Async XLA Ops:
  3.1 35.2 %all-to-all-start = ((f32[128,1,128]{2,1,0:T(1,128)}), f32[128,1,128]{2,1,0:T(1,128)S(1)}, u32[]{:S(2)}, u32[]{:S(2)}) async-start(f32[128,1,128]{2,1,0:T(1,128)} %bitcast.3), calls=%async_computation | async-start | bytes 131072 | tf_op jit(solution)/shard_map/all_to_all | solution.py:346
  38.3 27.5 %copy-start = (bf16[512,1024]{1,0:T(8,128)(2,1)S(1)}, bf16[512,1024]{1,0:T(8,128)(2,1)}, u32[]{:S(2)}) copy-start(bf16[512,1024]{1,0:T(8,128)(2,1)} %refs_4_.1) | copy-start | bytes 3145732
  39.5 26.3 %all-to-all-start.1 = ((bf16[128,8,128]{2,1,0:T(8,128)(2,1)}), bf16[128,8,128]{2,1,0:T(8,128)(2,1)S(1)}, u32[]{:S(2)}, u32[]{:S(2)}) async-start(bf16[128,8,128]{2,1,0:T(8,128)(2,1)} %bitcast.8), calls=%async_computation.1 | async-start | bytes 524288 | tf_op jit(solution)/shard_map/all_to_all | solution.py:346
  45.2 0.7 copy-start.6
  45.2 0.7 copy-start.7
  65.8 3.8 %copy-start.1 = (f32[1024,128]{1,0:T(8,128)S(1)}, f32[1024,128]{1,0:T(8,128)}, u32[]{:S(2)}) copy-start(f32[1024,128]{1,0:T(8,128)} %refs_6_.1) | copy-start | bytes 1572868
  71.8 10.4 %collective-permute-start = (s16[256,1408]{1,0:T(8,128)(2,1)S(1)}, s16[256,1408]{1,0:T(8,128)(2,1)S(1)}, u32[]{:S(2)}, u32[]{:S(2)}) collective-permute-start(s16[256,1408]{1,0:T(8,128)(2,1)S(1)} %get-tuple-element.49), channel_id=1, source_target_pairs={{0,4},{4,0},{1,5},{5,1},{2,6},{6,2},{3,7},{7,3},{8,12},{12,8},{9,1... | collective-permute-start | bytes 2162696 | tf_op jit(solution)/shard_map/ppermute | solution.py:433
  74.1 28.6 %all-to-all-start.2 = ((bf16[128,8,128]{2,1,0:T(8,128)(2,1)}), bf16[128,8,128]{2,1,0:T(8,128)(2,1)S(1)}, u32[]{:S(2)}, u32[]{:S(2)}) async-start(bf16[128,8,128]{2,1,0:T(8,128)(2,1)} %bitcast.12), calls=%async_computation.2 | async-start | bytes 524288 | tf_op jit(solution)/shard_map/all_to_all | solution.py:346
  83.6 9.9 %collective-permute-start.1 = (s16[64,1408]{1,0:T(8,128)(2,1)S(1)}, s16[64,1408]{1,0:T(8,128)(2,1)S(1)}, u32[]{:S(2)}, u32[]{:S(2)}) collective-permute-start(s16[64,1408]{1,0:T(8,128)(2,1)S(1)} %get-tuple-element.51), channel_id=1, source_target_pairs={{0,1},{1,0},{2,3},{3,2},{4,5},{5,4},{6,7},{7,6},{8,9},{9,8},{10,11... | collective-permute-start | bytes 540680 | tf_op jit(solution)/shard_map/ppermute | solution.py:350
  86.8 10.2 %collective-permute-start.2 = (s16[64,1408]{1,0:T(8,128)(2,1)S(1)}, s16[64,1408]{1,0:T(8,128)(2,1)S(1)}, u32[]{:S(2)}, u32[]{:S(2)}) collective-permute-start(s16[64,1408]{1,0:T(8,128)(2,1)S(1)} %get-tuple-element.52), channel_id=1, source_target_pairs={{0,2},{1,3},{2,0},{3,1},{4,6},{5,7},{6,4},{7,5},{8,10},{9,11},{10,... | collective-permute-start | bytes 540680 | tf_op jit(solution)/shard_map/ppermute | solution.py:350
  91.3 10.1 %collective-permute-start.3 = (s16[64,1408]{1,0:T(8,128)(2,1)S(1)}, s16[64,1408]{1,0:T(8,128)(2,1)S(1)}, u32[]{:S(2)}, u32[]{:S(2)}) collective-permute-start(s16[64,1408]{1,0:T(8,128)(2,1)S(1)} %get-tuple-element.53), channel_id=1, source_target_pairs={{0,3},{1,2},{2,1},{3,0},{4,7},{5,6},{6,5},{7,4},{8,11},{9,10},{10,... | collective-permute-start | bytes 540680 | tf_op jit(solution)/shard_map/ppermute | solution.py:350
  113.7 22.5 %all-to-all-start.4 = ((f32[16,24,128]{2,1,0:T(8,128)}), f32[16,24,128]{2,1,0:T(8,128)S(1)}, u32[]{:S(2)}, u32[]{:S(2)}) async-start(f32[16,24,128]{2,1,0:T(8,128)} %shard_map.191), calls=%async_computation.4 | async-start | bytes 393216 | tf_op jit(solution)/shard_map/all_to_all | solution.py:346
  125.1 7.4 %collective-permute-start.4 = (f32[512,128]{1,0:T(8,128)S(1)}, f32[512,128]{1,0:T(8,128)S(1)}, u32[]{:S(2)}, u32[]{:S(2)}) collective-permute-start(f32[512,128]{1,0:T(8,128)S(1)} %shard_map.188.refs_0_), channel_id=1, source_target_pairs={{0,1},{1,0},{2,3},{3,2},{4,5},{5,4},{6,7},{7,6},{8,9},{9,8},{10,11... | collective-permute-start | bytes 786440 | tf_op jit(solution)/shard_map/ppermute | solution.py:350
  132.5 13.9 %collective-permute-start.5 = (f32[512,128]{1,0:T(8,128)S(1)}, f32[512,128]{1,0:T(8,128)S(1)}, u32[]{:S(2)}, u32[]{:S(2)}) collective-permute-start(f32[512,128]{1,0:T(8,128)S(1)} %shard_map.189.refs_0_), channel_id=1, source_target_pairs={{0,3},{1,2},{2,1},{3,0},{4,7},{5,6},{6,5},{7,4},{8,11},{9,10},{10,... | collective-permute-start | bytes 786440 | tf_op jit(solution)/shard_map/ppermute | solution.py:350
  136.9 9.4 %copy-start.4 = (f32[512,128]{1,0:T(8,128)S(1)}, f32[512,128]{1,0:T(8,128)}, u32[]{:S(2)}) copy-start(f32[512,128]{1,0:T(8,128)} %refs_2_.4) | copy-start | bytes 786436
  136.9 9.5 %copy-start.5 = (f32[512,128]{1,0:T(8,128)S(1)}, f32[512,128]{1,0:T(8,128)}, u32[]{:S(2)}) copy-start(f32[512,128]{1,0:T(8,128)} %refs_3_.4) | copy-start | bytes 786436
  136.9 17.7 %all-to-all-start.5 = ((f32[32,16,128]{2,1,0:T(8,128)}), f32[32,16,128]{2,1,0:T(8,128)S(1)}, u32[]{:S(2)}, u32[]{:S(2)}) async-start(f32[32,16,128]{2,1,0:T(8,128)} %get-tuple-element.59), calls=%async_computation.5 | async-start | bytes 524288 | tf_op jit(solution)/shard_map/all_to_all | solution.py:346
  146.3 8.3 %copy-start.2 = (f32[1024,128]{1,0:T(8,128)S(1)}, f32[1024,128]{1,0:T(8,128)}, u32[]{:S(2)}) copy-start(f32[1024,128]{1,0:T(8,128)} %refs_2_.5) | copy-start | bytes 1572868
  146.3 8.3 %copy-start.3 = (f32[1024,128]{1,0:T(8,128)S(1)}, f32[1024,128]{1,0:T(8,128)}, u32[]{:S(2)}) copy-start(f32[1024,128]{1,0:T(8,128)} %refs_3_.5) | copy-start | bytes 1572868

commit v6 on v5

--- a/solution.py
+++ b/solution.py
@@ -21,6 +21,8 @@
 I16 = jnp.int16
 LN2 = 0.6931471805599453
 FINE = 65534.0
+SENT = 18
+HELD = 13
 EXACT = lax.Precision.HIGHEST
 VMEM = pl.BlockSpec(memory_space=pltpu.VMEM)
 HBM = pl.BlockSpec(memory_space=pltpu.HBM)
@@ -170,7 +172,10 @@
     owned_ref[...] = ones_where(iota_f(owned_ref.shape, 0) == wanted)
 
 
-def masks_kernel(target_ref, hot_ref, cache_ref, table_ref, rows_ref, hot_in_ref, hot_rows_ref, narrow_ref):
+def masks_kernel(
+    target_ref, hot_ref, cache_ref, table_ref, labels_ref, out_weight_ref,
+    rows_ref, hot_in_ref, hot_rows_ref, narrow_ref, label_ref, out_held_ref,
+):
     square = (BLOCK, BLOCK)
     eye = iota(square, 0) == iota(square, 1)
     hot = hot_ref.wait()[...].astype(F32)
@@ -192,14 +197,17 @@
             chosen = ones_where(column_of(row, eye) == hot_lane)
             hot_in_ref[h * BLOCK : (h + 1) * BLOCK, k * BLOCK : (k + 1) * BLOCK] = dot(chosen, cache).astype(BF16)
     narrow_ref[...] = table_ref.wait()[...].astype(BF16)
+    labels = labels_ref.wait()[...].astype(F32)
+    for h in range(labels.shape[0]):
+        column = column_of(labels[h : h + 1, :], eye)
+        label_ref[h * BLOCK : (h + 1) * BLOCK, :] = jnp.broadcast_to(column, (BLOCK, BLOCK))
+    out_held_ref[...] = out_weight_ref.wait()[...]
 
 
 def layer_kernel(
-    returned_ref, target_ref, rows_ref, hot_in_ref, weight_ref, out_weight_ref, labels_ref,
+    returned_ref, target_ref, rows_ref, hot_in_ref, weight_ref, out_weight_ref, label_ref,
     outgoing_ref, inputs_ref, dhidden_ref, hot_dx_ref, head_ref,
 ):
-    square = (BLOCK, BLOCK)
-    eye = iota(square, 0) == iota(square, 1)
     width = BLOCK
     samples = target_ref.shape[0] // 2
     lane = iota_f((samples, BLOCK), 1)
@@ -212,13 +220,12 @@
     inputs = jnp.concatenate([hot_in_ref[...], cold[:samples], cold[samples:]], axis=1)
     inputs_ref[...] = inputs
     weight = weight_ref[...]
-    out_weight = out_weight_ref.wait()[...]
+    out_weight = out_weight_ref[...]
     preact = dot(inputs, weight)
     gates = jax.nn.sigmoid(preact)
     hidden = (preact * gates).astype(BF16).astype(F32)
     logits = jnp.sum(hidden * out_weight, axis=1, keepdims=True)
-    labels = labels_ref.wait()[...].astype(F32)
-    label = jnp.concatenate([column_of(labels[h : h + 1, :], eye) for h in range(samples // BLOCK)], axis=0)
+    label = label_ref[:, :1]
     errors = jax.nn.sigmoid(logits) - label
     slope = gates * (1.0 + preact * (1.0 - gates))
     dhidden = (errors * out_weight * slope).astype(BF16)
@@ -249,17 +256,23 @@
 
 def send_kernel(
     control_ref, inputs_ref, dhidden_ref, hot_rows_ref, hot_dx_ref, head_ref, pending_ref,
-    send_ref, picked_ref, pending_new_ref,
+    send_ref, picked_ref, pending_new_ref, flat_ref,
 ):
     put = ones_where(iota_f((pending_ref.shape[0], hot_rows_ref.shape[1]), 0) == hot_rows_ref[:1, :])
     pending_new_ref[...] = dot(put, hot_dx_ref[...]) + pending_ref[...]
     count = REFRESHED
     blocks = [pl.ds(pl.multiple_of(control_ref[2 + i] * BLOCK, BLOCK), BLOCK) for i in range(count)]
     for i, at in enumerate(blocks):
-        picked_ref[i * BLOCK : (i + 1) * BLOCK, :] = pending_new_ref[at, :]
-    end = count * BLOCK
-    picked_ref[end : end + 8, :] = head_ref[...]
-    picked_ref[end + 8 :, :] = jnp.zeros((picked_ref.shape[0] - end - 8, BLOCK), F32)
+        flat_ref[i * BLOCK : (i + 1) * BLOCK, :] = pending_new_ref[at, :]
+    rows = HELD - 1
+    count = picked_ref.shape[0] // 16
+    part = iota((1, BLOCK), 1) // (8 * BLOCK // count)
+    for i in range(count):
+        at = i * 16
+        q, p = divmod(i, count // 8)
+        picked_ref[at : at + rows, :] = flat_ref[i * rows : (i + 1) * rows, :]
+        picked_ref[at + rows : at + HELD, :] = jnp.where(part == p, head_ref[q : q + 1, :], 0.0)
+        picked_ref[at + HELD : at + 16, :] = jnp.zeros((16 - HELD, BLOCK), F32)
     for at in blocks:
         pending_new_ref[at, :] = jnp.zeros((BLOCK, BLOCK), F32)
     core, rep = 1 - control_ref[0], control_ref[1]
@@ -291,22 +304,38 @@
     total = unpack(parts_ref[0])
     for i in range(1, parts_ref.shape[0]):
         total = total + unpack(parts_ref[i])
+    count = total.shape[0]
     wide = total.shape[1] - BLOCK
-    tall = wide // BLOCK
-    for b in range(tall):
-        out_ref[:, b, :] = total[:, b * BLOCK : (b + 1) * BLOCK]
-    for z in range(out_ref.shape[0]):
-        out_ref[z, tall:, :] = total[:, wide:]
+    top, hot = total[:, :wide], total[:, wide:]
+    top_exponent = exponent_of(jnp.max(jnp.abs(top), axis=1, keepdims=True))
+    top = jnp.round(top * power(-top_exponent)).astype(jnp.int32)
+    pairs = (top[:, : wide // 2] & 65535) | (top[:, wide // 2 :] << 16)
+    most = jnp.max(jnp.max(jnp.abs(hot), axis=1, keepdims=True), axis=0, keepdims=True)
+    hot_exponent = exponent_of(jnp.maximum(most, 1e-20)) - 15.0
+    hot = jnp.round(hot * power(-hot_exponent)).astype(jnp.int32)
+    lane = iota((count, BLOCK), 1)
+    rows = [pairs[:, b : b + BLOCK] for b in range(0, wide // 2, BLOCK)]
+    rows += [jnp.broadcast_to(hot[r : r + 1], (count, BLOCK)) for r in range(HELD)]
+    rows += [jnp.where(lane < BLOCK // 2, top_exponent, hot_exponent).astype(jnp.int32)]
+    for r, row in enumerate(rows):
+        out_ref[pl.ds(r, count, stride=SENT), :] = row
 
 
 def column_kernel(parts_ref, top_ref, copies_ref):
-    total = parts_ref[0]
-    for i in range(1, parts_ref.shape[0]):
-        total = total + parts_ref[i]
-    tall = top_ref.shape[0]
-    top_ref[...] = total[:tall]
-    for i in range(copies_ref.shape[0]):
-        copies_ref[i] = total[tall:]
+    tall = top_ref.shape[0] // 2
+    low, high = jnp.zeros((tall, BLOCK), F32), jnp.zeros((tall, BLOCK), F32)
+    hot = jnp.zeros((HELD, BLOCK), F32)
+    for i in range(parts_ref.shape[0] // SENT):
+        at = i * SENT
+        scale = power(parts_ref[at + SENT - 1 : at + SENT, :].astype(F32))
+        pairs = parts_ref[at : at + tall, :]
+        low = low + ((pairs << 16) >> 16).astype(F32) * scale[:, :1]
+        high = high + (pairs >> 16).astype(F32) * scale[:, :1]
+        hot = hot + parts_ref[at + tall : at + tall + HELD, :].astype(F32) * scale[:, BLOCK - 1 :]
+    top_ref[:tall, :] = low
+    top_ref[tall:, :] = high
+    for i in range(copies_ref.shape[0] // HELD):
+        copies_ref[i * HELD : (i + 1) * HELD, :] = hot
 
 
 def adagrad(table_rows, accum_rows, gradient):
@@ -314,18 +343,24 @@
     return (table_rows - step_size * gradient / (jnp.sqrt(accum_next) + epsilon), accum_next)
 
 
-def hot_kernel(control_ref, sums_ref, cache_ref, accum_ref, cache_new_ref, accum_new_ref, out_grad_ref):
+def hot_kernel(control_ref, sums_ref, cache_ref, accum_ref, cache_new_ref, accum_new_ref, out_grad_ref, flat_ref):
     cache_new_ref[...] = cache_ref[...]
     accum_new_ref[...] = accum_ref[...]
+    rows = HELD - 1
+    pieces = sums_ref.shape[0] // HELD
+    for i in range(pieces):
+        flat_ref[i * rows : (i + 1) * rows, :] = sums_ref[i * HELD : i * HELD + rows, :]
+    for q in range(8):
+        parts = [sums_ref[i * HELD + rows : (i + 1) * HELD, :] for i in range(q * pieces // 8, (q + 1) * pieces // 8)]
+        out_grad_ref[q : q + 1, :] = sum(parts[1:], parts[0])
     count = REFRESHED
     for i in range(count):
         block = control_ref[2 + i]
         at = pl.ds(pl.multiple_of(block * BLOCK, BLOCK), BLOCK)
-        flush = sums_ref[i * BLOCK : (i + 1) * BLOCK, :] / (1.0 + control_ref[2 + count + block].astype(F32))
+        flush = flat_ref[i * BLOCK : (i + 1) * BLOCK, :] / (1.0 + control_ref[2 + count + block].astype(F32))
         cache_next, accum_next = adagrad(cache_ref[at, :], accum_ref[at, :], flush)
         cache_new_ref[at, :] = cache_next
         accum_new_ref[at, :] = accum_next
-    out_grad_ref[...] = sums_ref[count * BLOCK : count * BLOCK + 8, :]
 
 
 def cold_kernel(owned_ref, incoming_ref, grad_ref):
@@ -384,18 +419,20 @@
         kept=(1,),
     )
     asked = swap(request.reshape(owners, 1, BLOCK), DP).reshape(owners, BLOCK)
-    target_rows, hot_in, hot_id_rows, narrow = call(
+    target_rows, hot_in, hot_id_rows, narrow, label, out_held = call(
         masks_kernel,
         [
             ((8, lookups), F32),
             ((samples, feats * width), BF16),
             ((8, samples * feats), F32),
             ((own_rows, width), BF16),
+            ((samples, BLOCK), F32),
+            ((1, hidden_width), F32),
         ],
-        (target, hot_ids.T, hot_cache, cold_table),
-        loads=(1, 2, 3),
+        (target, hot_ids.T, hot_cache, cold_table, labels.reshape(2, BLOCK), out_weight.reshape(1, hidden_width)),
+        loads=(1, 2, 3, 4, 5),
         held=(0,),
-        kept=(0, 1, 2, 3),
+        kept=(0, 1, 2, 3, 4, 5),
     )
     (found,) = call(rows_kernel, [((slots, width), BF16)], (asked, narrow), held=(1,), scratch=[((slots, width), F32)])
     returned = swap(found.reshape(owners, SLOTS, width), DP).reshape(slots, width)
@@ -409,9 +446,8 @@
             ((samples * feats, width), BF16),
             ((8, BLOCK), F32),
         ],
-        (returned, target, target_rows, hot_in, top_weight, out_weight.reshape(1, hidden_width), labels.reshape(2, BLOCK)),
-        loads=(5, 6),
-        held=(1, 2, 3),
+        (returned, target, target_rows, hot_in, top_weight, out_held, label),
+        held=(1, 2, 3, 5, 6),
         kept=(1, 2, 3, 4),
     )
     half = inputs_width // 2
@@ -427,6 +463,7 @@
         smem=1,
         held=(1, 2, 3, 4, 5),
         kept=(1,),
+        scratch=[((REFRESHED * BLOCK, BLOCK), F32)],
         flops=10**9,
     )
     send, outgoing = lax.optimization_barrier((send, outgoing))
@@ -444,10 +481,10 @@
     paired, incoming = lax.optimization_barrier((paired, incoming))
     plane = swap(paired.reshape(near, far, packed), "dp_1")
     tall = hidden_width // BLOCK
-    (columns,) = call(plane_kernel, [((far, tall + far, BLOCK), F32)], (plane,))
-    columns = swap(columns, "dp_0")
-    top, copies = call(column_kernel, [((tall, BLOCK), F32), ((plane_size, far, BLOCK), F32)], (columns,))
-    sums = swap(copies, PLANE).reshape(plane_size * far, BLOCK)
+    (columns,) = call(plane_kernel, [((far * SENT, BLOCK), jnp.int32)], (plane,))
+    columns = swap(columns.reshape(far, 1, SENT * BLOCK), "dp_0").reshape(far * SENT, BLOCK)
+    top, copies = call(column_kernel, [((tall, BLOCK), F32), ((plane_size * HELD, BLOCK), F32)], (columns,))
+    sums = swap(copies.reshape(plane_size, 1, HELD * BLOCK), PLANE).reshape(plane_size * HELD, BLOCK)
 
     (grad,) = call(cold_kernel, [((own_rows, width), F32)], (owned, incoming))
     (grad,) = call(two_kernel, [((own_rows, width), F32)], (grad, from_rep(grad, 1)))
@@ -459,6 +496,7 @@
         [((hot_count, width), F32)] * 2 + [((8, BLOCK), F32)],
         (control, sums, hot_cache, hot_accum),
         smem=1,
+        scratch=[((REFRESHED * BLOCK, BLOCK), F32)],
     )
     return (
         cold_table_new,

time: 157 us -> 155 us (0.987)
  no operation moved by 1% of the time
where the time goes in v6:
time: 155 us; the launch traced here: 154 us
  starting transfers between devices  69.1 us (45%)
  waiting for transfers between devices  55.4 us (36%)
  Pallas kernels  17.7 us (11%)
  blocking collectives  10.2 us (7%)
    all_to_all x5, starting transfers between devices, swap(): return lax.all_to_all(x, axis, split_axis=0, concat_axis=0, tiled=True)  52.7 us
    all_to_all x5, waiting for transfers between devices, swap(): return lax.all_to_all(x, axis, split_axis=0, concat_axis=0, tiled=True)  41.9 us
    pallas_call x14, Pallas kernels, call(): pl.pallas_call(body, out_shape=[(pltpu.VMEM if i in kept else jax.ShapeDt...  17.7 us
    ppermute x5, starting transfers between devices, from_rep(): return lax.ppermute(piece, 'rep', [(i, i ^ distance) for i in range(4)])  14.1 us
    ppermute x5, waiting for transfers between devices, from_rep(): return lax.ppermute(piece, 'rep', [(i, i ^ distance) for i in range(4)])  13.5 us
    all_to_all x1, blocking collectives, swap(): return lax.all_to_all(x, axis, split_axis=0, concat_axis=0, tiled=True)  10.2 us
  transfers between devices with their start and end apart: 11, of which 8 were waited for; matrix products, arithmetic and copies ran while one was open for 0% of the time, Pallas kernels for 4%

profile of v6, /device:TPU:1, one launch (start us, length us, event | category | flops | bytes accessed | tf_op | source)
XLA Modules:
  0.0 154.0 jit_solution(10516073909601296454)
XLA Ops:
  0.6 2.4 %shard_map.180 = (f32[128,128]{1,0:T(8,128)}, f32[512,128]{1,0:T(8,128)S(1)}) custom-call(s32[4,128]{1,0:T(4,128)} %bitcast.30, s32[4,128]{1,0:T(4,128)} %bitcast.31), custom_call_target="tpu_custom_call" | custom-call | flops 1000000000 | bytes 10000000 | tf_op jit(solution)/shard_map/pallas_call | solution.py:61
  3.1 20.4 %all-to-all-start = ((f32[128,1,128]{2,1,0:T(1,128)}), f32[128,1,128]{2,1,0:T(1,128)S(1)}, u32[]{:S(2)}, u32[]{:S(2)}) async-start(f32[128,1,128]{2,1,0:T(1,128)} %bitcast.3), calls=%async_computation | async-start | bytes 131072 | tf_op jit(solution)/shard_map/all_to_all | solution.py:381
  23.5 1.7 %shard_map.182 = (f32[8,512]{1,0:T(8,128)S(1)}, bf16[256,256]{1,0:T(8,128)(2,1)S(1)}, f32[8,512]{1,0:T(8,128)S(1)}, bf16[512,128]{1,0:T(8,128)(2,1)S(1)}, f32[256,128]{1,0:T(8,128)S(1)}, /*index=5*/f32[1,1024]{1,0:T(1,128)S(1)}) custom-call(f32[512,128]{1,0:T(8,128)S(1)} %get-tuple-element.39.refs_0_.refs_1_, s32[2,256]{1,0:T(2,128)} %bitcast.32, ...), custom_call_target="tpu_custom_call" | custom-call | flops 1000000000 | bytes 10000000 | tf_op jit(solution)/shard_map/pallas_call | solution.py:61
  25.2 13.1 %all-to-all-done = f32[128,1,128]{2,1,0:T(1,128)S(1)} async-done(((f32[128,1,128]{2,1,0:T(1,128)}), f32[128,1,128]{2,1,0:T(1,128)S(1)}, u32[]{:S(2)}, u32[]{:S(2)}) %all-to-all-start) | async-done | bytes 65568 | tf_op jit(solution)/shard_map/all_to_all | solution.py:381
  38.3 1.2 shard_map.183
  39.5 5.7 %all-to-all-start.1 = ((bf16[128,8,128]{2,1,0:T(8,128)(2,1)}), bf16[128,8,128]{2,1,0:T(8,128)(2,1)S(1)}, u32[]{:S(2)}, u32[]{:S(2)}) async-start(bf16[128,8,128]{2,1,0:T(8,128)(2,1)} %bitcast.10), calls=%async_computation.1 | async-start | bytes 524288 | tf_op jit(solution)/shard_map/all_to_all | solution.py:381
  45.2 0.6 copy-done.6
  45.9 19.9 %all-to-all-done.1 = bf16[128,8,128]{2,1,0:T(8,128)(2,1)S(1)} async-done(((bf16[128,8,128]{2,1,0:T(8,128)(2,1)}), bf16[128,8,128]{2,1,0:T(8,128)(2,1)S(1)}, u32[]{:S(2)}, u32[]{:S(2)}) %all-to-all-start.1) | async-done | bytes 262176 | tf_op jit(solution)/shard_map/all_to_all | solution.py:381
  65.8 3.0 %shard_map.184 = (bf16[1024,128]{1,0:T(8,128)(2,1)}, bf16[256,512]{1,0:T(8,128)(2,1)S(1)}, bf16[256,1024]{1,0:T(8,128)(2,1)S(1)}, bf16[512,128]{1,0:T(8,128)(2,1)S(1)}, f32[8,128]{1,0:T(8,128)S(1)}) custom-call(bf16[1024,128]{1,0:T(8,128)(2,1)S(1)} %bitcast.23, f32[512,128]{1,0:T(8,128)S(1)} %get-tuple-element.39.refs_0_.refs_1_, ...), custom_call_target="tpu_custom_call" | custom-call | flops 1000000000 | bytes 10000000 | tf_op jit(solution)/shard_map/pallas_call | solution.py:61
  68.8 2.3 %shard_map.185 = (s16[256,1408]{1,0:T(8,128)(2,1)S(1)}, f32[512,128]{1,0:T(8,128)S(1)}, f32[1024,128]{1,0:T(8,128)}) custom-call(s32[13]{0:T(128)S(1)} %pad_add_fusion.refs_0_, bf16[256,512]{1,0:T(8,128)(2,1)S(1)} %get-tuple-element.45.refs_1_, bf16[256,1024]{1,0:T(8,128)(2,1)S(1)} %get-tuple-element.46.refs_2_, f32[8,512]{1,0:T(8,128)S(1)} %get-tuple-element.47.refs_3_, ...), custom_call_target="tpu_custom_call" | custom-call | flops 1000000000 | bytes 10000000 | tf_op jit(solution)/shard_map/pallas_call | solution.py:61
  71.1 2.3 %collective-permute-start = (s16[256,1408]{1,0:T(8,128)(2,1)S(1)}, s16[256,1408]{1,0:T(8,128)(2,1)S(1)}, u32[]{:S(2)}, u32[]{:S(2)}) collective-permute-start(s16[256,1408]{1,0:T(8,128)(2,1)S(1)} %get-tuple-element.53), channel_id=1, source_target_pairs={{0,4},{4,0},{1,5},{5,1},{2,6},{6,2},{3,7},{7,3},{8,12},{12,8},{9,1... | collective-permute-start | bytes 2162696 | tf_op jit(solution)/shard_map/ppermute | solution.py:470
  73.4 8.1 %all-to-all-start.2 = ((bf16[128,8,128]{2,1,0:T(8,128)(2,1)}), bf16[128,8,128]{2,1,0:T(8,128)(2,1)S(1)}, u32[]{:S(2)}, u32[]{:S(2)}) async-start(bf16[128,8,128]{2,1,0:T(8,128)(2,1)} %bitcast.12), calls=%async_computation.2 | async-start | bytes 524288 | tf_op jit(solution)/shard_map/all_to_all | solution.py:381
  81.6 1.3 shard_map.186
  82.9 3.2 %collective-permute-start.1 = (s16[64,1408]{1,0:T(8,128)(2,1)S(1)}, s16[64,1408]{1,0:T(8,128)(2,1)S(1)}, u32[]{:S(2)}, u32[]{:S(2)}) collective-permute-start(s16[64,1408]{1,0:T(8,128)(2,1)S(1)} %get-tuple-element.55), channel_id=1, source_target_pairs={{0,1},{1,0},{2,3},{3,2},{4,5},{5,4},{6,7},{7,6},{8,9},{9,8},{10,11... | collective-permute-start | bytes 540680 | tf_op jit(solution)/shard_map/ppermute | solution.py:385
  86.1 4.5 %collective-permute-start.2 = (s16[64,1408]{1,0:T(8,128)(2,1)S(1)}, s16[64,1408]{1,0:T(8,128)(2,1)S(1)}, u32[]{:S(2)}, u32[]{:S(2)}) collective-permute-start(s16[64,1408]{1,0:T(8,128)(2,1)S(1)} %get-tuple-element.56), channel_id=1, source_target_pairs={{0,2},{1,3},{2,0},{3,1},{4,6},{5,7},{6,4},{7,5},{8,10},{9,11},{10,... | collective-permute-start | bytes 540680 | tf_op jit(solution)/shard_map/ppermute | solution.py:385
  90.6 2.1 %collective-permute-start.3 = (s16[64,1408]{1,0:T(8,128)(2,1)S(1)}, s16[64,1408]{1,0:T(8,128)(2,1)S(1)}, u32[]{:S(2)}, u32[]{:S(2)}) collective-permute-start(s16[64,1408]{1,0:T(8,128)(2,1)S(1)} %get-tuple-element.57), channel_id=1, source_target_pairs={{0,3},{1,2},{2,1},{3,0},{4,7},{5,6},{6,5},{7,4},{8,11},{9,10},{10,... | collective-permute-start | bytes 540680 | tf_op jit(solution)/shard_map/ppermute | solution.py:385
  92.8 3.5 %collective-permute-done.2.refs_2_ = s16[64,1408]{1,0:T(8,128)(2,1)S(1)} collective-permute-done((s16[64,1408]{1,0:T(8,128)(2,1)S(1)}, s16[64,1408]{1,0:T(8,128)(2,1)S(1)}, u32[]{:S(2)}, u32[]{:S(2)}) %collective-permute-start.2) | collective-permute-done | bytes 180256 | tf_op jit(solution)/shard_map/ppermute | solution.py:385
  96.3 4.5 %collective-permute-done.3.refs_3_ = s16[64,1408]{1,0:T(8,128)(2,1)S(1)} collective-permute-done((s16[64,1408]{1,0:T(8,128)(2,1)S(1)}, s16[64,1408]{1,0:T(8,128)(2,1)S(1)}, u32[]{:S(2)}, u32[]{:S(2)}) %collective-permute-start.3) | collective-permute-done | bytes 180256 | tf_op jit(solution)/shard_map/ppermute | solution.py:385
  101.1 1.0 all-to-all-done.2
  102.0 10.2 %all_to_all.30.refs_0_ = s16[4,16,1408]{2,1,0:T(8,128)(2,1)S(1)} all-to-all(s16[4,16,1408]{2,1,0:T(8,128)(2,1)S(1)} %bitcast.25), channel_id=1, replica_groups=mesh['dp_0'=16,'dp_1'=4,'dp_2'=2,'rep'=4] {'dp_1'}, dimensions={0} | all-to-all | bytes 360448 | tf_op jit(solution)/shard_map/all_to_all | solution.py:381
  112.2 0.9 shard_map.191
  113.0 10.2 %all-to-all-start.4 = ((s32[16,1,2304]{2,1,0:T(1,128)}), s32[16,1,2304]{2,1,0:T(1,128)S(1)}, u32[]{:S(2)}, u32[]{:S(2)}) async-start(s32[16,1,2304]{2,1,0:T(1,128)} %bitcast.15), calls=%async_computation.4 | async-start | bytes 294912 | tf_op jit(solution)/shard_map/all_to_all | solution.py:381
  123.2 0.8 shard_map.181.refs_0_
  124.4 1.9 %collective-permute-start.4 = (f32[512,128]{1,0:T(8,128)S(1)}, f32[512,128]{1,0:T(8,128)S(1)}, u32[]{:S(2)}, u32[]{:S(2)}) collective-permute-start(f32[512,128]{1,0:T(8,128)S(1)} %shard_map.188.refs_0_), channel_id=1, source_target_pairs={{0,1},{1,0},{2,3},{3,2},{4,5},{5,4},{6,7},{7,6},{8,9},{9,8},{10,11... | collective-permute-start | bytes 786440 | tf_op jit(solution)/shard_map/ppermute | solution.py:385
  126.4 5.5 %collective-permute-done.4.refs_1_ = f32[512,128]{1,0:T(8,128)S(1)} collective-permute-done((f32[512,128]{1,0:T(8,128)S(1)}, f32[512,128]{1,0:T(8,128)S(1)}, u32[]{:S(2)}, u32[]{:S(2)}) %collective-permute-start.4) | collective-permute-done | bytes 262176 | tf_op jit(solution)/shard_map/ppermute | solution.py:385
  131.9 2.4 %collective-permute-start.5 = (f32[512,128]{1,0:T(8,128)S(1)}, f32[512,128]{1,0:T(8,128)S(1)}, u32[]{:S(2)}, u32[]{:S(2)}) collective-permute-start(f32[512,128]{1,0:T(8,128)S(1)} %shard_map.189.refs_0_), channel_id=1, source_target_pairs={{0,3},{1,2},{2,1},{3,0},{4,7},{5,6},{6,5},{7,4},{8,11},{9,10},{10,... | collective-permute-start | bytes 786440 | tf_op jit(solution)/shard_map/ppermute | solution.py:385
  134.3 1.0 all-to-all-done.4
  135.3 0.8 shard_map.192
  136.1 8.3 %all-to-all-start.5 = ((f32[32,1,1664]{2,1,0:T(1,128)}), f32[32,1,1664]{2,1,0:T(1,128)S(1)}, u32[]{:S(2)}, u32[]{:S(2)}) async-start(f32[32,1,1664]{2,1,0:T(1,128)} %bitcast.17), calls=%async_computation.5 | async-start | bytes 425984 | tf_op jit(solution)/shard_map/all_to_all | solution.py:381
  144.5 0.9 shard_map.190
  145.4 6.9 %all-to-all-done.5 = f32[32,1,1664]{2,1,0:T(1,128)S(1)} async-done(((f32[32,1,1664]{2,1,0:T(1,128)}), f32[32,1,1664]{2,1,0:T(1,128)S(1)}, u32[]{:S(2)}, u32[]{:S(2)}) %all-to-all-start.5) | async-done | bytes 213024 | tf_op jit(solution)/shard_map/all_to_all | solution.py:381
  152.4 1.6 %shard_map.193 = (f32[1024,128]{1,0:T(8,128)}, f32[1024,128]{1,0:T(8,128)}, f32[8,128]{1,0:T(8,128)}) custom-call(s32[13]{0:T(128)S(1)} %pad_add_fusion.refs_0_, f32[416,128]{1,0:T(8,128)S(1)} %bitcast.24, f32[1024,128]{1,0:T(8,128)S(1)} %copy-done.2, f32[1024,128]{1,0:T(8,128)S(1)} %copy-done.3), custom_call_target="tpu_custom_call" | custom-call | flops 1000000000 | bytes 10000000 | tf_op jit(solution)/shard_map/pallas_call | solution.py:61
  (22 shorter events, 0.9 us)
Async XLA Ops:
  3.1 35.2 %all-to-all-start = ((f32[128,1,128]{2,1,0:T(1,128)}), f32[128,1,128]{2,1,0:T(1,128)S(1)}, u32[]{:S(2)}, u32[]{:S(2)}) async-start(f32[128,1,128]{2,1,0:T(1,128)} %bitcast.3), calls=%async_computation | async-start | bytes 131072 | tf_op jit(solution)/shard_map/all_to_all | solution.py:381
  38.3 27.5 %copy-start = (bf16[512,1024]{1,0:T(8,128)(2,1)S(1)}, bf16[512,1024]{1,0:T(8,128)(2,1)}, u32[]{:S(2)}) copy-start(bf16[512,1024]{1,0:T(8,128)(2,1)} %refs_4_.1) | copy-start | bytes 3145732
  39.5 26.3 %all-to-all-start.1 = ((bf16[128,8,128]{2,1,0:T(8,128)(2,1)}), bf16[128,8,128]{2,1,0:T(8,128)(2,1)S(1)}, u32[]{:S(2)}, u32[]{:S(2)}) async-start(bf16[128,8,128]{2,1,0:T(8,128)(2,1)} %bitcast.10), calls=%async_computation.1 | async-start | bytes 524288 | tf_op jit(solution)/shard_map/all_to_all | solution.py:381
  45.2 0.7 copy-start.6
  45.2 0.7 copy-start.7
  65.8 3.0 %copy-start.1 = (f32[1024,128]{1,0:T(8,128)S(1)}, f32[1024,128]{1,0:T(8,128)}, u32[]{:S(2)}) copy-start(f32[1024,128]{1,0:T(8,128)} %refs_6_.1) | copy-start | bytes 1572868
  71.1 10.4 %collective-permute-start = (s16[256,1408]{1,0:T(8,128)(2,1)S(1)}, s16[256,1408]{1,0:T(8,128)(2,1)S(1)}, u32[]{:S(2)}, u32[]{:S(2)}) collective-permute-start(s16[256,1408]{1,0:T(8,128)(2,1)S(1)} %get-tuple-element.53), channel_id=1, source_target_pairs={{0,4},{4,0},{1,5},{5,1},{2,6},{6,2},{3,7},{7,3},{8,12},{12,8},{9,1... | collective-permute-start | bytes 2162696 | tf_op jit(solution)/shard_map/ppermute | solution.py:470
  73.4 28.6 %all-to-all-start.2 = ((bf16[128,8,128]{2,1,0:T(8,128)(2,1)}), bf16[128,8,128]{2,1,0:T(8,128)(2,1)S(1)}, u32[]{:S(2)}, u32[]{:S(2)}) async-start(bf16[128,8,128]{2,1,0:T(8,128)(2,1)} %bitcast.12), calls=%async_computation.2 | async-start | bytes 524288 | tf_op jit(solution)/shard_map/all_to_all | solution.py:381
  82.9 9.9 %collective-permute-start.1 = (s16[64,1408]{1,0:T(8,128)(2,1)S(1)}, s16[64,1408]{1,0:T(8,128)(2,1)S(1)}, u32[]{:S(2)}, u32[]{:S(2)}) collective-permute-start(s16[64,1408]{1,0:T(8,128)(2,1)S(1)} %get-tuple-element.55), channel_id=1, source_target_pairs={{0,1},{1,0},{2,3},{3,2},{4,5},{5,4},{6,7},{7,6},{8,9},{9,8},{10,11... | collective-permute-start | bytes 540680 | tf_op jit(solution)/shard_map/ppermute | solution.py:385
  86.1 10.2 %collective-permute-start.2 = (s16[64,1408]{1,0:T(8,128)(2,1)S(1)}, s16[64,1408]{1,0:T(8,128)(2,1)S(1)}, u32[]{:S(2)}, u32[]{:S(2)}) collective-permute-start(s16[64,1408]{1,0:T(8,128)(2,1)S(1)} %get-tuple-element.56), channel_id=1, source_target_pairs={{0,2},{1,3},{2,0},{3,1},{4,6},{5,7},{6,4},{7,5},{8,10},{9,11},{10,... | collective-permute-start | bytes 540680 | tf_op jit(solution)/shard_map/ppermute | solution.py:385
  90.6 10.1 %collective-permute-start.3 = (s16[64,1408]{1,0:T(8,128)(2,1)S(1)}, s16[64,1408]{1,0:T(8,128)(2,1)S(1)}, u32[]{:S(2)}, u32[]{:S(2)}) collective-permute-start(s16[64,1408]{1,0:T(8,128)(2,1)S(1)} %get-tuple-element.57), channel_id=1, source_target_pairs={{0,3},{1,2},{2,1},{3,0},{4,7},{5,6},{6,5},{7,4},{8,11},{9,10},{10,... | collective-permute-start | bytes 540680 | tf_op jit(solution)/shard_map/ppermute | solution.py:385
  113.0 22.2 %all-to-all-start.4 = ((s32[16,1,2304]{2,1,0:T(1,128)}), s32[16,1,2304]{2,1,0:T(1,128)S(1)}, u32[]{:S(2)}, u32[]{:S(2)}) async-start(s32[16,1,2304]{2,1,0:T(1,128)} %bitcast.15), calls=%async_computation.4 | async-start | bytes 294912 | tf_op jit(solution)/shard_map/all_to_all | solution.py:381
  124.4 7.4 %collective-permute-start.4 = (f32[512,128]{1,0:T(8,128)S(1)}, f32[512,128]{1,0:T(8,128)S(1)}, u32[]{:S(2)}, u32[]{:S(2)}) collective-permute-start(f32[512,128]{1,0:T(8,128)S(1)} %shard_map.188.refs_0_), channel_id=1, source_target_pairs={{0,1},{1,0},{2,3},{3,2},{4,5},{5,4},{6,7},{7,6},{8,9},{9,8},{10,11... | collective-permute-start | bytes 786440 | tf_op jit(solution)/shard_map/ppermute | solution.py:385
  131.9 12.6 %collective-permute-start.5 = (f32[512,128]{1,0:T(8,128)S(1)}, f32[512,128]{1,0:T(8,128)S(1)}, u32[]{:S(2)}, u32[]{:S(2)}) collective-permute-start(f32[512,128]{1,0:T(8,128)S(1)} %shard_map.189.refs_0_), channel_id=1, source_target_pairs={{0,3},{1,2},{2,1},{3,0},{4,7},{5,6},{6,5},{7,4},{8,11},{9,10},{10,... | collective-permute-start | bytes 786440 | tf_op jit(solution)/shard_map/ppermute | solution.py:385
  135.3 9.2 %copy-start.5 = (f32[512,128]{1,0:T(8,128)S(1)}, f32[512,128]{1,0:T(8,128)}, u32[]{:S(2)}) copy-start(f32[512,128]{1,0:T(8,128)} %refs_3_.4) | copy-start | bytes 786436
  136.1 8.4 %copy-start.4 = (f32[512,128]{1,0:T(8,128)S(1)}, f32[512,128]{1,0:T(8,128)}, u32[]{:S(2)}) copy-start(f32[512,128]{1,0:T(8,128)} %refs_2_.4) | copy-start | bytes 786436
  136.1 16.2 %all-to-all-start.5 = ((f32[32,1,1664]{2,1,0:T(1,128)}), f32[32,1,1664]{2,1,0:T(1,128)S(1)}, u32[]{:S(2)}, u32[]{:S(2)}) async-start(f32[32,1,1664]{2,1,0:T(1,128)} %bitcast.17), calls=%async_computation.5 | async-start | bytes 425984 | tf_op jit(solution)/shard_map/all_to_all | solution.py:381
  144.5 7.9 %copy-start.2 = (f32[1024,128]{1,0:T(8,128)S(1)}, f32[1024,128]{1,0:T(8,128)}, u32[]{:S(2)}) copy-start(f32[1024,128]{1,0:T(8,128)} %refs_2_.5) | copy-start | bytes 1572868
  144.5 7.9 %copy-start.3 = (f32[1024,128]{1,0:T(8,128)S(1)}, f32[1024,128]{1,0:T(8,128)}, u32[]{:S(2)}) copy-start(f32[1024,128]{1,0:T(8,128)} %refs_3_.5) | copy-start | bytes 1572868

commit v7 on v6

--- a/solution.py
+++ b/solution.py
@@ -133,28 +133,34 @@
 
 def requests_kernel(owner_ref, offset_ref, request_ref, target_ref):
     square = (BLOCK, BLOCK)
-    eye = iota(square, 0) == iota(square, 1)
     owner = owner_ref.wait()[...].astype(F32)
     offset = offset_ref.wait()[...].astype(F32)
     groups = owner.shape[0]
     lookups = groups * BLOCK
-    rows = [owner[s : s + 1, :] for s in range(groups)]
-    owner_col = jnp.concatenate([column_of(row, eye) for row in rows], axis=0)
-    offset_col = jnp.concatenate([column_of(offset[s : s + 1, :], eye) for s in range(groups)], axis=0)
+    columns = jnp.transpose(jnp.concatenate([owner, offset], axis=0))
+    owner_col = jnp.concatenate([columns[:, s : s + 1] for s in range(groups)], axis=0)
+    offset_col = jnp.concatenate([columns[:, groups + s : groups + s + 1] for s in range(groups)], axis=0)
     lane = iota_f((lookups, BLOCK), 1)
     named = owner_col == lane
-    before = ones_where(iota((lookups, lookups), 0) > iota((lookups, lookups), 1))
-    earlier = dot(before, ones_where(named))
-    rank = jnp.sum(jnp.where(named, earlier, 0.0), axis=1, keepdims=True)
+    before = ones_where(iota(square, 0) > iota(square, 1))
+    counts = jnp.where(named, 1.0, 0.0)
+    earlier = []
+    so_far = jnp.zeros((1, BLOCK), F32)
+    for s in range(groups):
+        block = counts[s * BLOCK : (s + 1) * BLOCK]
+        earlier.append(dot(before, block.astype(BF16)) + so_far)
+        so_far = so_far + jnp.sum(block, axis=0, keepdims=True)
+    rank = jnp.sum(jnp.where(named, jnp.concatenate(earlier, axis=0), 0.0), axis=1, keepdims=True)
     target_ref[...] = jnp.broadcast_to(owner_col * SLOTS + rank, (lookups, BLOCK))
-    placed = jnp.where(rank == lane, offset_col, 0.0)
+    high = jnp.where(offset_col >= 256.0, 1.0, 0.0)
+    placed = jnp.where(rank == lane, offset_col - 256.0 * high, jnp.where(rank == lane - SLOTS, high, 0.0))
     sublane = iota_f(square, 0)
-    named_t = jnp.concatenate([jnp.where(sublane == row, 1.0, 0.0) for row in rows], axis=1)
-    request_ref[...] = dot(named_t, placed, EXACT)
+    named_t = jnp.concatenate([ones_where(sublane == owner[s : s + 1, :]) for s in range(groups)], axis=1)
+    request_ref[...] = dot(named_t, placed.astype(BF16))
 
 
 def rows_kernel(asked_ref, table_ref, rows_ref, wide_ref):
-    asked = asked_ref[...]
+    asked = asked_ref[:, :SLOTS] + 256.0 * asked_ref[:, SLOTS : 2 * SLOTS]
     table = table_ref[...]
     sources = asked.shape[0]
     line = iota_f((sources, table.shape[0]), 1)
@@ -167,7 +173,9 @@
 def owned_kernel(asked_ref, owned_ref):
     slots = owned_ref.shape[1]
     source, line = iota((BLOCK, slots), 0), iota((BLOCK, slots), 1)
-    spread = dot(asked_ref[...], jnp.where(source == line % SLOTS, 1.0, 0.0), EXACT)
+    slot = line % SLOTS
+    worth = jnp.where(source == slot, 1.0, jnp.where(source == slot + SLOTS, 256.0, 0.0))
+    spread = dot(asked_ref[...], worth, EXACT)
     wanted = jnp.sum(jnp.where(source == line // SLOTS, spread, 0.0), axis=0, keepdims=True)
     owned_ref[...] = ones_where(iota_f(owned_ref.shape, 0) == wanted)
 
@@ -295,7 +303,7 @@
             piece[...] = both
 
 
-def four_kernel(own_ref, one_ref, two_ref, three_ref, sum_ref):
+def four_kernel(own_ref, two_ref, one_ref, three_ref, sum_ref):
     total = (own_ref[...] + unpack(one_ref[...])) + (unpack(two_ref[...]) + unpack(three_ref[...]))
     pack(total, sum_ref)
 
@@ -477,7 +485,7 @@
         held=(1, 2, 3),
     )
     two, one, three = (from_rep(pieces[d], d) for d in (2, 1, 3))
-    (paired,) = call(four_kernel, [((half // 4, packed), I16)], (pieces[0], one, two, three))
+    (paired,) = call(four_kernel, [((half // 4, packed), I16)], (pieces[0], two, one, three))
     paired, incoming = lax.optimization_barrier((paired, incoming))
     plane = swap(paired.reshape(near, far, packed), "dp_1")
     tall = hidden_width // BLOCK

time: 155 us -> 152 us (0.981)
  starting transfers between devices: 69.1 us -> 66.5 us
    all_to_all x5, starting transfers between devices: 52.7 us -> 49.8 us  [swap(): return lax.all_to_all(x, axis, split_axis=0, concat_axis=0, tiled=True)]
    ppermute x5, waiting for transfers between devices: 13.5 us -> 10.7 us  [from_rep(): return lax.ppermute(piece, 'rep', [(i, i ^ distance) for i in range(4)])]
    all_to_all x5, waiting for transfers between devices: 41.9 us -> 44.4 us  [swap(): return lax.all_to_all(x, axis, split_axis=0, concat_axis=0, tiled=True)]
where the time goes in v7:
time: 152 us; the launch traced here: 151 us
  starting transfers between devices  66.5 us (44%)
  waiting for transfers between devices  55.1 us (36%)
  Pallas kernels  17.7 us (12%)
  blocking collectives  10.2 us (7%)
    all_to_all x5, starting transfers between devices, swap(): return lax.all_to_all(x, axis, split_axis=0, concat_axis=0, tiled=True)  49.8 us
    all_to_all x5, waiting for transfers between devices, swap(): return lax.all_to_all(x, axis, split_axis=0, concat_axis=0, tiled=True)  44.4 us
    pallas_call x14, Pallas kernels, call(): pl.pallas_call(body, out_shape=[(pltpu.VMEM if i in kept else jax.ShapeDt...  17.7 us
    ppermute x5, starting transfers between devices, from_rep(): return lax.ppermute(piece, 'rep', [(i, i ^ distance) for i in range(4)])  14.4 us
    ppermute x5, waiting for transfers between devices, from_rep(): return lax.ppermute(piece, 'rep', [(i, i ^ distance) for i in range(4)])  10.7 us
    all_to_all x1, blocking collectives, swap(): return lax.all_to_all(x, axis, split_axis=0, concat_axis=0, tiled=True)  10.2 us
  transfers between devices with their start and end apart: 11, of which 8 were waited for; matrix products, arithmetic and copies ran while one was open for 0% of the time, Pallas kernels for 4%

profile of v7, /device:TPU:1, one launch (start us, length us, event | category | flops | bytes accessed | tf_op | source)
XLA Modules:
  0.0 151.1 jit_solution(1601748641255237656)
XLA Ops:
  0.6 2.3 %shard_map.180 = (f32[128,128]{1,0:T(8,128)}, f32[512,128]{1,0:T(8,128)S(1)}) custom-call(s32[4,128]{1,0:T(4,128)} %bitcast.30, s32[4,128]{1,0:T(4,128)} %bitcast.31), custom_call_target="tpu_custom_call" | custom-call | flops 1000000000 | bytes 10000000 | tf_op jit(solution)/shard_map/pallas_call | solution.py:61
  3.0 20.4 %all-to-all-start = ((f32[128,1,128]{2,1,0:T(1,128)}), f32[128,1,128]{2,1,0:T(1,128)S(1)}, u32[]{:S(2)}, u32[]{:S(2)}) async-start(f32[128,1,128]{2,1,0:T(1,128)} %bitcast.3), calls=%async_computation | async-start | bytes 131072 | tf_op jit(solution)/shard_map/all_to_all | solution.py:389
  23.4 1.7 %shard_map.182 = (f32[8,512]{1,0:T(8,128)S(1)}, bf16[256,256]{1,0:T(8,128)(2,1)S(1)}, f32[8,512]{1,0:T(8,128)S(1)}, bf16[512,128]{1,0:T(8,128)(2,1)S(1)}, f32[256,128]{1,0:T(8,128)S(1)}, /*index=5*/f32[1,1024]{1,0:T(1,128)S(1)}) custom-call(f32[512,128]{1,0:T(8,128)S(1)} %get-tuple-element.39.refs_0_.refs_1_, s32[2,256]{1,0:T(2,128)} %bitcast.32, ...), custom_call_target="tpu_custom_call" | custom-call | flops 1000000000 | bytes 10000000 | tf_op jit(solution)/shard_map/pallas_call | solution.py:61
  25.1 13.1 %all-to-all-done = f32[128,1,128]{2,1,0:T(1,128)S(1)} async-done(((f32[128,1,128]{2,1,0:T(1,128)}), f32[128,1,128]{2,1,0:T(1,128)S(1)}, u32[]{:S(2)}, u32[]{:S(2)}) %all-to-all-start) | async-done | bytes 65568 | tf_op jit(solution)/shard_map/all_to_all | solution.py:389
  38.2 1.3 shard_map.183
  39.5 5.7 %all-to-all-start.1 = ((bf16[128,8,128]{2,1,0:T(8,128)(2,1)}), bf16[128,8,128]{2,1,0:T(8,128)(2,1)S(1)}, u32[]{:S(2)}, u32[]{:S(2)}) async-start(bf16[128,8,128]{2,1,0:T(8,128)(2,1)} %bitcast.10), calls=%async_computation.1 | async-start | bytes 524288 | tf_op jit(solution)/shard_map/all_to_all | solution.py:389
  45.2 0.6 copy-done.6
  45.9 19.9 %all-to-all-done.1 = bf16[128,8,128]{2,1,0:T(8,128)(2,1)S(1)} async-done(((bf16[128,8,128]{2,1,0:T(8,128)(2,1)}), bf16[128,8,128]{2,1,0:T(8,128)(2,1)S(1)}, u32[]{:S(2)}, u32[]{:S(2)}) %all-to-all-start.1) | async-done | bytes 262176 | tf_op jit(solution)/shard_map/all_to_all | solution.py:389
  65.8 3.0 %shard_map.184 = (bf16[1024,128]{1,0:T(8,128)(2,1)}, bf16[256,512]{1,0:T(8,128)(2,1)S(1)}, bf16[256,1024]{1,0:T(8,128)(2,1)S(1)}, bf16[512,128]{1,0:T(8,128)(2,1)S(1)}, f32[8,128]{1,0:T(8,128)S(1)}) custom-call(bf16[1024,128]{1,0:T(8,128)(2,1)S(1)} %bitcast.23, f32[512,128]{1,0:T(8,128)S(1)} %get-tuple-element.39.refs_0_.refs_1_, ...), custom_call_target="tpu_custom_call" | custom-call | flops 1000000000 | bytes 10000000 | tf_op jit(solution)/shard_map/pallas_call | solution.py:61
  68.8 2.3 %shard_map.185 = (s16[256,1408]{1,0:T(8,128)(2,1)S(1)}, f32[512,128]{1,0:T(8,128)S(1)}, f32[1024,128]{1,0:T(8,128)}) custom-call(s32[13]{0:T(128)S(1)} %pad_add_fusion.refs_0_, bf16[256,512]{1,0:T(8,128)(2,1)S(1)} %get-tuple-element.45.refs_1_, bf16[256,1024]{1,0:T(8,128)(2,1)S(1)} %get-tuple-element.46.refs_2_, f32[8,512]{1,0:T(8,128)S(1)} %get-tuple-element.47.refs_3_, ...), custom_call_target="tpu_custom_call" | custom-call | flops 1000000000 | bytes 10000000 | tf_op jit(solution)/shard_map/pallas_call | solution.py:61
  71.1 2.3 %collective-permute-start = (s16[256,1408]{1,0:T(8,128)(2,1)S(1)}, s16[256,1408]{1,0:T(8,128)(2,1)S(1)}, u32[]{:S(2)}, u32[]{:S(2)}) collective-permute-start(s16[256,1408]{1,0:T(8,128)(2,1)S(1)} %get-tuple-element.53), channel_id=1, source_target_pairs={{0,4},{4,0},{1,5},{5,1},{2,6},{6,2},{3,7},{7,3},{8,12},{12,8},{9,1... | collective-permute-start | bytes 2162696 | tf_op jit(solution)/shard_map/ppermute | solution.py:478
  73.4 8.1 %all-to-all-start.2 = ((bf16[128,8,128]{2,1,0:T(8,128)(2,1)}), bf16[128,8,128]{2,1,0:T(8,128)(2,1)S(1)}, u32[]{:S(2)}, u32[]{:S(2)}) async-start(bf16[128,8,128]{2,1,0:T(8,128)(2,1)} %bitcast.12), calls=%async_computation.2 | async-start | bytes 524288 | tf_op jit(solution)/shard_map/all_to_all | solution.py:389
  81.5 1.3 shard_map.186
  82.9 4.8 %collective-permute-start.1 = (s16[64,1408]{1,0:T(8,128)(2,1)S(1)}, s16[64,1408]{1,0:T(8,128)(2,1)S(1)}, u32[]{:S(2)}, u32[]{:S(2)}) collective-permute-start(s16[64,1408]{1,0:T(8,128)(2,1)S(1)} %get-tuple-element.55), channel_id=1, source_target_pairs={{0,2},{1,3},{2,0},{3,1},{4,6},{5,7},{6,4},{7,5},{8,10},{9,11},{10,... | collective-permute-start | bytes 540680 | tf_op jit(solution)/shard_map/ppermute | solution.py:393
  87.7 2.3 %collective-permute-start.2 = (s16[64,1408]{1,0:T(8,128)(2,1)S(1)}, s16[64,1408]{1,0:T(8,128)(2,1)S(1)}, u32[]{:S(2)}, u32[]{:S(2)}) collective-permute-start(s16[64,1408]{1,0:T(8,128)(2,1)S(1)} %get-tuple-element.56), channel_id=1, source_target_pairs={{0,1},{1,0},{2,3},{3,2},{4,5},{5,4},{6,7},{7,6},{8,9},{9,8},{10,11... | collective-permute-start | bytes 540680 | tf_op jit(solution)/shard_map/ppermute | solution.py:393
  90.0 2.3 %collective-permute-start.3 = (s16[64,1408]{1,0:T(8,128)(2,1)S(1)}, s16[64,1408]{1,0:T(8,128)(2,1)S(1)}, u32[]{:S(2)}, u32[]{:S(2)}) collective-permute-start(s16[64,1408]{1,0:T(8,128)(2,1)S(1)} %get-tuple-element.57), channel_id=1, source_target_pairs={{0,3},{1,2},{2,1},{3,0},{4,7},{5,6},{6,5},{7,4},{8,11},{9,10},{10,... | collective-permute-start | bytes 540680 | tf_op jit(solution)/shard_map/ppermute | solution.py:393
  92.3 3.9 %collective-permute-done.2.refs_2_ = s16[64,1408]{1,0:T(8,128)(2,1)S(1)} collective-permute-done((s16[64,1408]{1,0:T(8,128)(2,1)S(1)}, s16[64,1408]{1,0:T(8,128)(2,1)S(1)}, u32[]{:S(2)}, u32[]{:S(2)}) %collective-permute-start.2) | collective-permute-done | bytes 180256 | tf_op jit(solution)/shard_map/ppermute | solution.py:393
  96.2 1.5 %collective-permute-done.3.refs_3_ = s16[64,1408]{1,0:T(8,128)(2,1)S(1)} collective-permute-done((s16[64,1408]{1,0:T(8,128)(2,1)S(1)}, s16[64,1408]{1,0:T(8,128)(2,1)S(1)}, u32[]{:S(2)}, u32[]{:S(2)}) %collective-permute-start.3) | collective-permute-done | bytes 180256 | tf_op jit(solution)/shard_map/ppermute | solution.py:393
  98.1 4.0 %all-to-all-done.2 = bf16[128,8,128]{2,1,0:T(8,128)(2,1)S(1)} async-done(((bf16[128,8,128]{2,1,0:T(8,128)(2,1)}), bf16[128,8,128]{2,1,0:T(8,128)(2,1)S(1)}, u32[]{:S(2)}, u32[]{:S(2)}) %all-to-all-start.2) | async-done | bytes 262176 | tf_op jit(solution)/shard_map/all_to_all | solution.py:389
  102.0 10.2 %all_to_all.30.refs_0_ = s16[4,16,1408]{2,1,0:T(8,128)(2,1)S(1)} all-to-all(s16[4,16,1408]{2,1,0:T(8,128)(2,1)S(1)} %bitcast.25), channel_id=1, replica_groups=mesh['dp_0'=16,'dp_1'=4,'dp_2'=2,'rep'=4] {'dp_1'}, dimensions={0} | all-to-all | bytes 360448 | tf_op jit(solution)/shard_map/all_to_all | solution.py:389
  112.2 0.9 shard_map.191
  113.0 7.1 %all-to-all-start.4 = ((s32[16,1,2304]{2,1,0:T(1,128)}), s32[16,1,2304]{2,1,0:T(1,128)S(1)}, u32[]{:S(2)}, u32[]{:S(2)}) async-start(s32[16,1,2304]{2,1,0:T(1,128)} %bitcast.15), calls=%async_computation.4 | async-start | bytes 294912 | tf_op jit(solution)/shard_map/all_to_all | solution.py:389
  120.1 0.8 shard_map.181.refs_0_
  121.4 1.9 %collective-permute-start.4 = (f32[512,128]{1,0:T(8,128)S(1)}, f32[512,128]{1,0:T(8,128)S(1)}, u32[]{:S(2)}, u32[]{:S(2)}) collective-permute-start(f32[512,128]{1,0:T(8,128)S(1)} %shard_map.188.refs_0_), channel_id=1, source_target_pairs={{0,1},{1,0},{2,3},{3,2},{4,5},{5,4},{6,7},{7,6},{8,9},{9,8},{10,11... | collective-permute-start | bytes 786440 | tf_op jit(solution)/shard_map/ppermute | solution.py:393
  123.3 5.2 %collective-permute-done.4.refs_1_ = f32[512,128]{1,0:T(8,128)S(1)} collective-permute-done((f32[512,128]{1,0:T(8,128)S(1)}, f32[512,128]{1,0:T(8,128)S(1)}, u32[]{:S(2)}, u32[]{:S(2)}) %collective-permute-start.4) | collective-permute-done | bytes 262176 | tf_op jit(solution)/shard_map/ppermute | solution.py:393
  128.6 3.0 %collective-permute-start.5 = (f32[512,128]{1,0:T(8,128)S(1)}, f32[512,128]{1,0:T(8,128)S(1)}, u32[]{:S(2)}, u32[]{:S(2)}) collective-permute-start(f32[512,128]{1,0:T(8,128)S(1)} %shard_map.189.refs_0_), channel_id=1, source_target_pairs={{0,3},{1,2},{2,1},{3,0},{4,7},{5,6},{6,5},{7,4},{8,11},{9,10},{10,... | collective-permute-start | bytes 786440 | tf_op jit(solution)/shard_map/ppermute | solution.py:393
  131.6 0.6 all-to-all-done.4
  132.2 0.8 shard_map.192
  133.0 8.5 %all-to-all-start.5 = ((f32[32,1,1664]{2,1,0:T(1,128)}), f32[32,1,1664]{2,1,0:T(1,128)S(1)}, u32[]{:S(2)}, u32[]{:S(2)}) async-start(f32[32,1,1664]{2,1,0:T(1,128)} %bitcast.17), calls=%async_computation.5 | async-start | bytes 425984 | tf_op jit(solution)/shard_map/all_to_all | solution.py:389
  141.6 0.9 shard_map.190
  142.6 6.9 %all-to-all-done.5 = f32[32,1,1664]{2,1,0:T(1,128)S(1)} async-done(((f32[32,1,1664]{2,1,0:T(1,128)}), f32[32,1,1664]{2,1,0:T(1,128)S(1)}, u32[]{:S(2)}, u32[]{:S(2)}) %all-to-all-start.5) | async-done | bytes 213024 | tf_op jit(solution)/shard_map/all_to_all | solution.py:389
  149.5 1.6 %shard_map.193 = (f32[1024,128]{1,0:T(8,128)}, f32[1024,128]{1,0:T(8,128)}, f32[8,128]{1,0:T(8,128)}) custom-call(s32[13]{0:T(128)S(1)} %pad_add_fusion.refs_0_, f32[416,128]{1,0:T(8,128)S(1)} %bitcast.24, f32[1024,128]{1,0:T(8,128)S(1)} %copy-done.2, f32[1024,128]{1,0:T(8,128)S(1)} %copy-done.3), custom_call_target="tpu_custom_call" | custom-call | flops 1000000000 | bytes 10000000 | tf_op jit(solution)/shard_map/pallas_call | solution.py:61
  (22 shorter events, 0.9 us)
Async XLA Ops:
  3.0 35.2 %all-to-all-start = ((f32[128,1,128]{2,1,0:T(1,128)}), f32[128,1,128]{2,1,0:T(1,128)S(1)}, u32[]{:S(2)}, u32[]{:S(2)}) async-start(f32[128,1,128]{2,1,0:T(1,128)} %bitcast.3), calls=%async_computation | async-start | bytes 131072 | tf_op jit(solution)/shard_map/all_to_all | solution.py:389
  38.2 27.6 %copy-start = (bf16[512,1024]{1,0:T(8,128)(2,1)S(1)}, bf16[512,1024]{1,0:T(8,128)(2,1)}, u32[]{:S(2)}) copy-start(bf16[512,1024]{1,0:T(8,128)(2,1)} %refs_4_.1) | copy-start | bytes 3145732
  39.5 26.3 %all-to-all-start.1 = ((bf16[128,8,128]{2,1,0:T(8,128)(2,1)}), bf16[128,8,128]{2,1,0:T(8,128)(2,1)S(1)}, u32[]{:S(2)}, u32[]{:S(2)}) async-start(bf16[128,8,128]{2,1,0:T(8,128)(2,1)} %bitcast.10), calls=%async_computation.1 | async-start | bytes 524288 | tf_op jit(solution)/shard_map/all_to_all | solution.py:389
  45.2 0.7 copy-start.6
  45.2 0.7 copy-start.7
  65.8 3.0 %copy-start.1 = (f32[1024,128]{1,0:T(8,128)S(1)}, f32[1024,128]{1,0:T(8,128)}, u32[]{:S(2)}) copy-start(f32[1024,128]{1,0:T(8,128)} %refs_6_.1) | copy-start | bytes 1572868
  71.1 10.4 %collective-permute-start = (s16[256,1408]{1,0:T(8,128)(2,1)S(1)}, s16[256,1408]{1,0:T(8,128)(2,1)S(1)}, u32[]{:S(2)}, u32[]{:S(2)}) collective-permute-start(s16[256,1408]{1,0:T(8,128)(2,1)S(1)} %get-tuple-element.53), channel_id=1, source_target_pairs={{0,4},{4,0},{1,5},{5,1},{2,6},{6,2},{3,7},{7,3},{8,12},{12,8},{9,1... | collective-permute-start | bytes 2162696 | tf_op jit(solution)/shard_map/ppermute | solution.py:478
  73.4 28.6 %all-to-all-start.2 = ((bf16[128,8,128]{2,1,0:T(8,128)(2,1)}), bf16[128,8,128]{2,1,0:T(8,128)(2,1)S(1)}, u32[]{:S(2)}, u32[]{:S(2)}) async-start(bf16[128,8,128]{2,1,0:T(8,128)(2,1)} %bitcast.12), calls=%async_computation.2 | async-start | bytes 524288 | tf_op jit(solution)/shard_map/all_to_all | solution.py:389
  82.9 9.5 %collective-permute-start.1 = (s16[64,1408]{1,0:T(8,128)(2,1)S(1)}, s16[64,1408]{1,0:T(8,128)(2,1)S(1)}, u32[]{:S(2)}, u32[]{:S(2)}) collective-permute-start(s16[64,1408]{1,0:T(8,128)(2,1)S(1)} %get-tuple-element.55), channel_id=1, source_target_pairs={{0,2},{1,3},{2,0},{3,1},{4,6},{5,7},{6,4},{7,5},{8,10},{9,11},{10,... | collective-permute-start | bytes 540680 | tf_op jit(solution)/shard_map/ppermute | solution.py:393
  87.7 8.5 %collective-permute-start.2 = (s16[64,1408]{1,0:T(8,128)(2,1)S(1)}, s16[64,1408]{1,0:T(8,128)(2,1)S(1)}, u32[]{:S(2)}, u32[]{:S(2)}) collective-permute-start(s16[64,1408]{1,0:T(8,128)(2,1)S(1)} %get-tuple-element.56), channel_id=1, source_target_pairs={{0,1},{1,0},{2,3},{3,2},{4,5},{5,4},{6,7},{7,6},{8,9},{9,8},{10,11... | collective-permute-start | bytes 540680 | tf_op jit(solution)/shard_map/ppermute | solution.py:393
  90.0 7.7 %collective-permute-start.3 = (s16[64,1408]{1,0:T(8,128)(2,1)S(1)}, s16[64,1408]{1,0:T(8,128)(2,1)S(1)}, u32[]{:S(2)}, u32[]{:S(2)}) collective-permute-start(s16[64,1408]{1,0:T(8,128)(2,1)S(1)} %get-tuple-element.57), channel_id=1, source_target_pairs={{0,3},{1,2},{2,1},{3,0},{4,7},{5,6},{6,5},{7,4},{8,11},{9,10},{10,... | collective-permute-start | bytes 540680 | tf_op jit(solution)/shard_map/ppermute | solution.py:393
  113.0 19.2 %all-to-all-start.4 = ((s32[16,1,2304]{2,1,0:T(1,128)}), s32[16,1,2304]{2,1,0:T(1,128)S(1)}, u32[]{:S(2)}, u32[]{:S(2)}) async-start(s32[16,1,2304]{2,1,0:T(1,128)} %bitcast.15), calls=%async_computation.4 | async-start | bytes 294912 | tf_op jit(solution)/shard_map/all_to_all | solution.py:389
  121.4 7.2 %collective-permute-start.4 = (f32[512,128]{1,0:T(8,128)S(1)}, f32[512,128]{1,0:T(8,128)S(1)}, u32[]{:S(2)}, u32[]{:S(2)}) collective-permute-start(f32[512,128]{1,0:T(8,128)S(1)} %shard_map.188.refs_0_), channel_id=1, source_target_pairs={{0,1},{1,0},{2,3},{3,2},{4,5},{5,4},{6,7},{7,6},{8,9},{9,8},{10,11... | collective-permute-start | bytes 786440 | tf_op jit(solution)/shard_map/ppermute | solution.py:393
  128.6 13.0 %collective-permute-start.5 = (f32[512,128]{1,0:T(8,128)S(1)}, f32[512,128]{1,0:T(8,128)S(1)}, u32[]{:S(2)}, u32[]{:S(2)}) collective-permute-start(f32[512,128]{1,0:T(8,128)S(1)} %shard_map.189.refs_0_), channel_id=1, source_target_pairs={{0,3},{1,2},{2,1},{3,0},{4,7},{5,6},{6,5},{7,4},{8,11},{9,10},{10,... | collective-permute-start | bytes 786440 | tf_op jit(solution)/shard_map/ppermute | solution.py:393
  132.2 9.4 %copy-start.5 = (f32[512,128]{1,0:T(8,128)S(1)}, f32[512,128]{1,0:T(8,128)}, u32[]{:S(2)}) copy-start(f32[512,128]{1,0:T(8,128)} %refs_3_.4) | copy-start | bytes 786436
  133.0 8.6 %copy-start.4 = (f32[512,128]{1,0:T(8,128)S(1)}, f32[512,128]{1,0:T(8,128)}, u32[]{:S(2)}) copy-start(f32[512,128]{1,0:T(8,128)} %refs_2_.4) | copy-start | bytes 786436
  133.0 16.5 %all-to-all-start.5 = ((f32[32,1,1664]{2,1,0:T(1,128)}), f32[32,1,1664]{2,1,0:T(1,128)S(1)}, u32[]{:S(2)}, u32[]{:S(2)}) async-start(f32[32,1,1664]{2,1,0:T(1,128)} %bitcast.17), calls=%async_computation.5 | async-start | bytes 425984 | tf_op jit(solution)/shard_map/all_to_all | solution.py:389
  141.6 7.9 %copy-start.2 = (f32[1024,128]{1,0:T(8,128)S(1)}, f32[1024,128]{1,0:T(8,128)}, u32[]{:S(2)}) copy-start(f32[1024,128]{1,0:T(8,128)} %refs_2_.5) | copy-start | bytes 1572868
  141.6 7.9 %copy-start.3 = (f32[1024,128]{1,0:T(8,128)S(1)}, f32[1024,128]{1,0:T(8,128)}, u32[]{:S(2)}) copy-start(f32[1024,128]{1,0:T(8,128)} %refs_3_.5) | copy-start | bytes 1572868

commit v8 on v7

--- a/solution.py
+++ b/solution.py
@@ -250,10 +250,13 @@
 
 
 def half_of_top(core, rep, inputs, dhidden):
-    shape = (inputs.shape[1] // 2, inputs.shape[1])
+    wide = inputs.shape[1]
+    shape = (wide // 2, BLOCK)
     line = iota(shape, 0)
     row = (line & 15) * 32 + ((line >> 4) & 3) * 8 + core * 4 + ((line >> 6) ^ rep)
-    ordered = dot_t(ones_where(row == iota(shape, 1)), inputs).astype(BF16)
+    lane = iota(shape, 1)
+    order = jnp.concatenate([ones_where(row == lane + b) for b in range(0, wide, BLOCK)], axis=1)
+    ordered = dot_t(order, inputs).astype(BF16)
     return dot(ordered, dhidden)
 
 
@@ -470,7 +473,7 @@
         (control, inputs, dhidden, hot_id_rows, hot_dx, head, pending),
         smem=1,
         held=(1, 2, 3, 4, 5),
-        kept=(1,),
+        kept=(1, 2),
         scratch=[((REFRESHED * BLOCK, BLOCK), F32)],
         flops=10**9,
     )

time: 152 us -> 151 us (level)
  transfers between devices with their start and end apart: 11 -> 11, of which waited for: 8 -> 8; matrix products, arithmetic and copies ran while one was open for 0% -> 1% of each run, Pallas kernels for 4% -> 4%
where the time goes in v8:
time: 151 us; the launch traced here: 150 us
  starting transfers between devices  66.4 us (44%)
  waiting for transfers between devices  53.9 us (36%)
  Pallas kernels  17 us (11%)
  blocking collectives  10.2 us (7%)
  local copies, waits for them, and re-layouts  1.87 us (1%)
    all_to_all x5, starting transfers between devices, swap(): return lax.all_to_all(x, axis, split_axis=0, concat_axis=0, tiled=True)  49.7 us
    all_to_all x5, waiting for transfers between devices, swap(): return lax.all_to_all(x, axis, split_axis=0, concat_axis=0, tiled=True)  43.3 us
    pallas_call x14, Pallas kernels, call(): pl.pallas_call(body, out_shape=[(pltpu.VMEM if i in kept else jax.ShapeDt...  17 us
    ppermute x5, starting transfers between devices, from_rep(): return lax.ppermute(piece, 'rep', [(i, i ^ distance) for i in range(4)])  14.4 us
    ppermute x5, waiting for transfers between devices, from_rep(): return lax.ppermute(piece, 'rep', [(i, i ^ distance) for i in range(4)])  10.7 us
    all_to_all x1, blocking collectives, swap(): return lax.all_to_all(x, axis, split_axis=0, concat_axis=0, tiled=True)  10.2 us
  transfers between devices with their start and end apart: 11, of which 8 were waited for; matrix products, arithmetic and copies ran while one was open for 1% of the time, Pallas kernels for 4%

profile of v8, /device:TPU:1, one launch (start us, length us, event | category | flops | bytes accessed | tf_op | source)
XLA Modules:
  0.0 150.3 jit_solution(14104643358726510043)
XLA Ops:
  0.6 2.3 %shard_map.180 = (f32[128,128]{1,0:T(8,128)}, f32[512,128]{1,0:T(8,128)S(1)}) custom-call(s32[4,128]{1,0:T(4,128)} %bitcast.30, s32[4,128]{1,0:T(4,128)} %bitcast.31), custom_call_target="tpu_custom_call" | custom-call | flops 1000000000 | bytes 10000000 | tf_op jit(solution)/shard_map/pallas_call | solution.py:61
  3.0 20.4 %all-to-all-start = ((f32[128,1,128]{2,1,0:T(1,128)}), f32[128,1,128]{2,1,0:T(1,128)S(1)}, u32[]{:S(2)}, u32[]{:S(2)}) async-start(f32[128,1,128]{2,1,0:T(1,128)} %bitcast.3), calls=%async_computation | async-start | bytes 131072 | tf_op jit(solution)/shard_map/all_to_all | solution.py:392
  23.4 1.7 %shard_map.182 = (f32[8,512]{1,0:T(8,128)S(1)}, bf16[256,256]{1,0:T(8,128)(2,1)S(1)}, f32[8,512]{1,0:T(8,128)S(1)}, bf16[512,128]{1,0:T(8,128)(2,1)S(1)}, f32[256,128]{1,0:T(8,128)S(1)}, /*index=5*/f32[1,1024]{1,0:T(1,128)S(1)}) custom-call(f32[512,128]{1,0:T(8,128)S(1)} %get-tuple-element.39.refs_0_.refs_1_, s32[2,256]{1,0:T(2,128)} %bitcast.32, ...), custom_call_target="tpu_custom_call" | custom-call | flops 1000000000 | bytes 10000000 | tf_op jit(solution)/shard_map/pallas_call | solution.py:61
  25.1 13.1 %all-to-all-done = f32[128,1,128]{2,1,0:T(1,128)S(1)} async-done(((f32[128,1,128]{2,1,0:T(1,128)}), f32[128,1,128]{2,1,0:T(1,128)S(1)}, u32[]{:S(2)}, u32[]{:S(2)}) %all-to-all-start) | async-done | bytes 65568 | tf_op jit(solution)/shard_map/all_to_all | solution.py:392
  38.2 1.3 shard_map.183
  39.5 5.7 %all-to-all-start.1 = ((bf16[128,8,128]{2,1,0:T(8,128)(2,1)}), bf16[128,8,128]{2,1,0:T(8,128)(2,1)S(1)}, u32[]{:S(2)}, u32[]{:S(2)}) async-start(bf16[128,8,128]{2,1,0:T(8,128)(2,1)} %bitcast.10), calls=%async_computation.1 | async-start | bytes 524288 | tf_op jit(solution)/shard_map/all_to_all | solution.py:392
  45.2 0.6 copy-done.6
  45.9 19.9 %all-to-all-done.1 = bf16[128,8,128]{2,1,0:T(8,128)(2,1)S(1)} async-done(((bf16[128,8,128]{2,1,0:T(8,128)(2,1)}), bf16[128,8,128]{2,1,0:T(8,128)(2,1)S(1)}, u32[]{:S(2)}, u32[]{:S(2)}) %all-to-all-start.1) | async-done | bytes 262176 | tf_op jit(solution)/shard_map/all_to_all | solution.py:392
  65.8 3.0 %shard_map.184 = (bf16[1024,128]{1,0:T(8,128)(2,1)}, bf16[256,512]{1,0:T(8,128)(2,1)S(1)}, bf16[256,1024]{1,0:T(8,128)(2,1)S(1)}, bf16[512,128]{1,0:T(8,128)(2,1)S(1)}, f32[8,128]{1,0:T(8,128)S(1)}) custom-call(bf16[1024,128]{1,0:T(8,128)(2,1)S(1)} %bitcast.23, f32[512,128]{1,0:T(8,128)S(1)} %get-tuple-element.39.refs_0_.refs_1_, ...), custom_call_target="tpu_custom_call" | custom-call | flops 1000000000 | bytes 10000000 | tf_op jit(solution)/shard_map/pallas_call | solution.py:61
  68.8 1.6 %shard_map.185 = (s16[256,1408]{1,0:T(8,128)(2,1)S(1)}, f32[512,128]{1,0:T(8,128)S(1)}, f32[1024,128]{1,0:T(8,128)S(1)}) custom-call(s32[13]{0:T(128)S(1)} %pad_add_fusion.refs_0_, bf16[256,512]{1,0:T(8,128)(2,1)S(1)} %get-tuple-element.45.refs_1_, bf16[256,1024]{1,0:T(8,128)(2,1)S(1)} %get-tuple-element.46.refs_2_, f32[8,512]{1,0:T(8,128)S(1)} %get-tuple-element.47.refs_3_, ...), custom_call_target="tpu_custom_call" | custom-call | flops 1000000000 | bytes 10000000 | tf_op jit(solution)/shard_map/pallas_call | solution.py:61
  70.4 2.3 %collective-permute-start = (s16[256,1408]{1,0:T(8,128)(2,1)S(1)}, s16[256,1408]{1,0:T(8,128)(2,1)S(1)}, u32[]{:S(2)}, u32[]{:S(2)}) collective-permute-start(s16[256,1408]{1,0:T(8,128)(2,1)S(1)} %get-tuple-element.53), channel_id=1, source_target_pairs={{0,4},{4,0},{1,5},{5,1},{2,6},{6,2},{3,7},{7,3},{8,12},{12,8},{9,1... | collective-permute-start | bytes 2162696 | tf_op jit(solution)/shard_map/ppermute | solution.py:481
  72.7 8.1 %all-to-all-start.2 = ((bf16[128,8,128]{2,1,0:T(8,128)(2,1)}), bf16[128,8,128]{2,1,0:T(8,128)(2,1)S(1)}, u32[]{:S(2)}, u32[]{:S(2)}) async-start(bf16[128,8,128]{2,1,0:T(8,128)(2,1)} %bitcast.12), calls=%async_computation.2 | async-start | bytes 524288 | tf_op jit(solution)/shard_map/all_to_all | solution.py:392
  80.8 1.3 shard_map.186
  82.2 4.8 %collective-permute-start.1 = (s16[64,1408]{1,0:T(8,128)(2,1)S(1)}, s16[64,1408]{1,0:T(8,128)(2,1)S(1)}, u32[]{:S(2)}, u32[]{:S(2)}) collective-permute-start(s16[64,1408]{1,0:T(8,128)(2,1)S(1)} %get-tuple-element.55), channel_id=1, source_target_pairs={{0,2},{1,3},{2,0},{3,1},{4,6},{5,7},{6,4},{7,5},{8,10},{9,11},{10,... | collective-permute-start | bytes 540680 | tf_op jit(solution)/shard_map/ppermute | solution.py:396
  87.0 2.3 %collective-permute-start.2 = (s16[64,1408]{1,0:T(8,128)(2,1)S(1)}, s16[64,1408]{1,0:T(8,128)(2,1)S(1)}, u32[]{:S(2)}, u32[]{:S(2)}) collective-permute-start(s16[64,1408]{1,0:T(8,128)(2,1)S(1)} %get-tuple-element.56), channel_id=1, source_target_pairs={{0,1},{1,0},{2,3},{3,2},{4,5},{5,4},{6,7},{7,6},{8,9},{9,8},{10,11... | collective-permute-start | bytes 540680 | tf_op jit(solution)/shard_map/ppermute | solution.py:396
  89.3 2.3 %collective-permute-start.3 = (s16[64,1408]{1,0:T(8,128)(2,1)S(1)}, s16[64,1408]{1,0:T(8,128)(2,1)S(1)}, u32[]{:S(2)}, u32[]{:S(2)}) collective-permute-start(s16[64,1408]{1,0:T(8,128)(2,1)S(1)} %get-tuple-element.57), channel_id=1, source_target_pairs={{0,3},{1,2},{2,1},{3,0},{4,7},{5,6},{6,5},{7,4},{8,11},{9,10},{10,... | collective-permute-start | bytes 540680 | tf_op jit(solution)/shard_map/ppermute | solution.py:396
  91.6 3.9 %collective-permute-done.2.refs_2_ = s16[64,1408]{1,0:T(8,128)(2,1)S(1)} collective-permute-done((s16[64,1408]{1,0:T(8,128)(2,1)S(1)}, s16[64,1408]{1,0:T(8,128)(2,1)S(1)}, u32[]{:S(2)}, u32[]{:S(2)}) %collective-permute-start.2) | collective-permute-done | bytes 180256 | tf_op jit(solution)/shard_map/ppermute | solution.py:396
  95.5 1.5 %collective-permute-done.3.refs_3_ = s16[64,1408]{1,0:T(8,128)(2,1)S(1)} collective-permute-done((s16[64,1408]{1,0:T(8,128)(2,1)S(1)}, s16[64,1408]{1,0:T(8,128)(2,1)S(1)}, u32[]{:S(2)}, u32[]{:S(2)}) %collective-permute-start.3) | collective-permute-done | bytes 180256 | tf_op jit(solution)/shard_map/ppermute | solution.py:396
  97.4 4.0 %all-to-all-done.2 = bf16[128,8,128]{2,1,0:T(8,128)(2,1)S(1)} async-done(((bf16[128,8,128]{2,1,0:T(8,128)(2,1)}), bf16[128,8,128]{2,1,0:T(8,128)(2,1)S(1)}, u32[]{:S(2)}, u32[]{:S(2)}) %all-to-all-start.2) | async-done | bytes 262176 | tf_op jit(solution)/shard_map/all_to_all | solution.py:392
  101.3 10.2 %all_to_all.30.refs_0_ = s16[4,16,1408]{2,1,0:T(8,128)(2,1)S(1)} all-to-all(s16[4,16,1408]{2,1,0:T(8,128)(2,1)S(1)} %bitcast.25), channel_id=1, replica_groups=mesh['dp_0'=16,'dp_1'=4,'dp_2'=2,'rep'=4] {'dp_1'}, dimensions={0} | all-to-all | bytes 360448 | tf_op jit(solution)/shard_map/all_to_all | solution.py:392
  111.5 0.9 shard_map.191
  112.3 7.1 %all-to-all-start.4 = ((s32[16,1,2304]{2,1,0:T(1,128)}), s32[16,1,2304]{2,1,0:T(1,128)S(1)}, u32[]{:S(2)}, u32[]{:S(2)}) async-start(s32[16,1,2304]{2,1,0:T(1,128)} %bitcast.15), calls=%async_computation.4 | async-start | bytes 294912 | tf_op jit(solution)/shard_map/all_to_all | solution.py:392
  119.4 0.8 shard_map.181.refs_0_
  120.7 1.9 %collective-permute-start.4 = (f32[512,128]{1,0:T(8,128)S(1)}, f32[512,128]{1,0:T(8,128)S(1)}, u32[]{:S(2)}, u32[]{:S(2)}) collective-permute-start(f32[512,128]{1,0:T(8,128)S(1)} %shard_map.188.refs_0_), channel_id=1, source_target_pairs={{0,1},{1,0},{2,3},{3,2},{4,5},{5,4},{6,7},{7,6},{8,9},{9,8},{10,11... | collective-permute-start | bytes 786440 | tf_op jit(solution)/shard_map/ppermute | solution.py:396
  122.6 5.2 %collective-permute-done.4.refs_1_ = f32[512,128]{1,0:T(8,128)S(1)} collective-permute-done((f32[512,128]{1,0:T(8,128)S(1)}, f32[512,128]{1,0:T(8,128)S(1)}, u32[]{:S(2)}, u32[]{:S(2)}) %collective-permute-start.4) | collective-permute-done | bytes 262176 | tf_op jit(solution)/shard_map/ppermute | solution.py:396
  127.9 3.0 %collective-permute-start.5 = (f32[512,128]{1,0:T(8,128)S(1)}, f32[512,128]{1,0:T(8,128)S(1)}, u32[]{:S(2)}, u32[]{:S(2)}) collective-permute-start(f32[512,128]{1,0:T(8,128)S(1)} %shard_map.189.refs_0_), channel_id=1, source_target_pairs={{0,3},{1,2},{2,1},{3,0},{4,7},{5,6},{6,5},{7,4},{8,11},{9,10},{10,... | collective-permute-start | bytes 786440 | tf_op jit(solution)/shard_map/ppermute | solution.py:396
  131.5 0.8 shard_map.192
  132.3 8.4 %all-to-all-start.5 = ((f32[32,1,1664]{2,1,0:T(1,128)}), f32[32,1,1664]{2,1,0:T(1,128)S(1)}, u32[]{:S(2)}, u32[]{:S(2)}) async-start(f32[32,1,1664]{2,1,0:T(1,128)} %bitcast.17), calls=%async_computation.5 | async-start | bytes 425984 | tf_op jit(solution)/shard_map/all_to_all | solution.py:392
  140.8 0.8 copy.23
  142.0 0.9 shard_map.190
  142.9 5.8 %all-to-all-done.5 = f32[32,1,1664]{2,1,0:T(1,128)S(1)} async-done(((f32[32,1,1664]{2,1,0:T(1,128)}), f32[32,1,1664]{2,1,0:T(1,128)S(1)}, u32[]{:S(2)}, u32[]{:S(2)}) %all-to-all-start.5) | async-done | bytes 213024 | tf_op jit(solution)/shard_map/all_to_all | solution.py:392
  148.7 1.6 %shard_map.193 = (f32[1024,128]{1,0:T(8,128)}, f32[1024,128]{1,0:T(8,128)}, f32[8,128]{1,0:T(8,128)}) custom-call(s32[13]{0:T(128)S(1)} %pad_add_fusion.refs_0_, f32[416,128]{1,0:T(8,128)S(1)} %bitcast.24, f32[1024,128]{1,0:T(8,128)S(1)} %copy-done.2, f32[1024,128]{1,0:T(8,128)S(1)} %copy-done.3), custom_call_target="tpu_custom_call" | custom-call | flops 1000000000 | bytes 10000000 | tf_op jit(solution)/shard_map/pallas_call | solution.py:61
  (23 shorter events, 1.9 us)
Async XLA Ops:
  3.0 35.2 %all-to-all-start = ((f32[128,1,128]{2,1,0:T(1,128)}), f32[128,1,128]{2,1,0:T(1,128)S(1)}, u32[]{:S(2)}, u32[]{:S(2)}) async-start(f32[128,1,128]{2,1,0:T(1,128)} %bitcast.3), calls=%async_computation | async-start | bytes 131072 | tf_op jit(solution)/shard_map/all_to_all | solution.py:392
  38.2 27.6 %copy-start = (bf16[512,1024]{1,0:T(8,128)(2,1)S(1)}, bf16[512,1024]{1,0:T(8,128)(2,1)}, u32[]{:S(2)}) copy-start(bf16[512,1024]{1,0:T(8,128)(2,1)} %refs_4_.1) | copy-start | bytes 3145732
  39.5 26.3 %all-to-all-start.1 = ((bf16[128,8,128]{2,1,0:T(8,128)(2,1)}), bf16[128,8,128]{2,1,0:T(8,128)(2,1)S(1)}, u32[]{:S(2)}, u32[]{:S(2)}) async-start(bf16[128,8,128]{2,1,0:T(8,128)(2,1)} %bitcast.10), calls=%async_computation.1 | async-start | bytes 524288 | tf_op jit(solution)/shard_map/all_to_all | solution.py:392
  45.2 0.7 copy-start.6
  45.2 0.7 copy-start.7
  65.8 3.0 %copy-start.1 = (f32[1024,128]{1,0:T(8,128)S(1)}, f32[1024,128]{1,0:T(8,128)}, u32[]{:S(2)}) copy-start(f32[1024,128]{1,0:T(8,128)} %refs_6_.1) | copy-start | bytes 1572868
  70.4 10.4 %collective-permute-start = (s16[256,1408]{1,0:T(8,128)(2,1)S(1)}, s16[256,1408]{1,0:T(8,128)(2,1)S(1)}, u32[]{:S(2)}, u32[]{:S(2)}) collective-permute-start(s16[256,1408]{1,0:T(8,128)(2,1)S(1)} %get-tuple-element.53), channel_id=1, source_target_pairs={{0,4},{4,0},{1,5},{5,1},{2,6},{6,2},{3,7},{7,3},{8,12},{12,8},{9,1... | collective-permute-start | bytes 2162696 | tf_op jit(solution)/shard_map/ppermute | solution.py:481
  72.7 28.6 %all-to-all-start.2 = ((bf16[128,8,128]{2,1,0:T(8,128)(2,1)}), bf16[128,8,128]{2,1,0:T(8,128)(2,1)S(1)}, u32[]{:S(2)}, u32[]{:S(2)}) async-start(bf16[128,8,128]{2,1,0:T(8,128)(2,1)} %bitcast.12), calls=%async_computation.2 | async-start | bytes 524288 | tf_op jit(solution)/shard_map/all_to_all | solution.py:392
  82.2 9.5 %collective-permute-start.1 = (s16[64,1408]{1,0:T(8,128)(2,1)S(1)}, s16[64,1408]{1,0:T(8,128)(2,1)S(1)}, u32[]{:S(2)}, u32[]{:S(2)}) collective-permute-start(s16[64,1408]{1,0:T(8,128)(2,1)S(1)} %get-tuple-element.55), channel_id=1, source_target_pairs={{0,2},{1,3},{2,0},{3,1},{4,6},{5,7},{6,4},{7,5},{8,10},{9,11},{10,... | collective-permute-start | bytes 540680 | tf_op jit(solution)/shard_map/ppermute | solution.py:396
  87.0 8.5 %collective-permute-start.2 = (s16[64,1408]{1,0:T(8,128)(2,1)S(1)}, s16[64,1408]{1,0:T(8,128)(2,1)S(1)}, u32[]{:S(2)}, u32[]{:S(2)}) collective-permute-start(s16[64,1408]{1,0:T(8,128)(2,1)S(1)} %get-tuple-element.56), channel_id=1, source_target_pairs={{0,1},{1,0},{2,3},{3,2},{4,5},{5,4},{6,7},{7,6},{8,9},{9,8},{10,11... | collective-permute-start | bytes 540680 | tf_op jit(solution)/shard_map/ppermute | solution.py:396
  89.3 7.7 %collective-permute-start.3 = (s16[64,1408]{1,0:T(8,128)(2,1)S(1)}, s16[64,1408]{1,0:T(8,128)(2,1)S(1)}, u32[]{:S(2)}, u32[]{:S(2)}) collective-permute-start(s16[64,1408]{1,0:T(8,128)(2,1)S(1)} %get-tuple-element.57), channel_id=1, source_target_pairs={{0,3},{1,2},{2,1},{3,0},{4,7},{5,6},{6,5},{7,4},{8,11},{9,10},{10,... | collective-permute-start | bytes 540680 | tf_op jit(solution)/shard_map/ppermute | solution.py:396
  112.3 19.2 %all-to-all-start.4 = ((s32[16,1,2304]{2,1,0:T(1,128)}), s32[16,1,2304]{2,1,0:T(1,128)S(1)}, u32[]{:S(2)}, u32[]{:S(2)}) async-start(s32[16,1,2304]{2,1,0:T(1,128)} %bitcast.15), calls=%async_computation.4 | async-start | bytes 294912 | tf_op jit(solution)/shard_map/all_to_all | solution.py:392
  120.7 7.2 %collective-permute-start.4 = (f32[512,128]{1,0:T(8,128)S(1)}, f32[512,128]{1,0:T(8,128)S(1)}, u32[]{:S(2)}, u32[]{:S(2)}) collective-permute-start(f32[512,128]{1,0:T(8,128)S(1)} %shard_map.188.refs_0_), channel_id=1, source_target_pairs={{0,1},{1,0},{2,3},{3,2},{4,5},{5,4},{6,7},{7,6},{8,9},{9,8},{10,11... | collective-permute-start | bytes 786440 | tf_op jit(solution)/shard_map/ppermute | solution.py:396
  127.9 13.7 %collective-permute-start.5 = (f32[512,128]{1,0:T(8,128)S(1)}, f32[512,128]{1,0:T(8,128)S(1)}, u32[]{:S(2)}, u32[]{:S(2)}) collective-permute-start(f32[512,128]{1,0:T(8,128)S(1)} %shard_map.189.refs_0_), channel_id=1, source_target_pairs={{0,3},{1,2},{2,1},{3,0},{4,7},{5,6},{6,5},{7,4},{8,11},{9,10},{10,... | collective-permute-start | bytes 786440 | tf_op jit(solution)/shard_map/ppermute | solution.py:396
  132.3 16.3 %all-to-all-start.5 = ((f32[32,1,1664]{2,1,0:T(1,128)}), f32[32,1,1664]{2,1,0:T(1,128)S(1)}, u32[]{:S(2)}, u32[]{:S(2)}) async-start(f32[32,1,1664]{2,1,0:T(1,128)} %bitcast.17), calls=%async_computation.5 | async-start | bytes 425984 | tf_op jit(solution)/shard_map/all_to_all | solution.py:392
  140.7 1.0 copy-start.4
  140.8 1.2 copy-start.5
  141.6 7.1 %copy-start.2 = (f32[1024,128]{1,0:T(8,128)S(1)}, f32[1024,128]{1,0:T(8,128)}, u32[]{:S(2)}) copy-start(f32[1024,128]{1,0:T(8,128)} %refs_2_.5) | copy-start | bytes 1572868
  141.6 7.1 %copy-start.3 = (f32[1024,128]{1,0:T(8,128)S(1)}, f32[1024,128]{1,0:T(8,128)}, u32[]{:S(2)}) copy-start(f32[1024,128]{1,0:T(8,128)} %refs_3_.5) | copy-start | bytes 1572868

commit v9 on v8

--- a/solution.py
+++ b/solution.py
@@ -492,12 +492,13 @@
     paired, incoming = lax.optimization_barrier((paired, incoming))
     plane = swap(paired.reshape(near, far, packed), "dp_1")
     tall = hidden_width // BLOCK
+    (grad,) = call(cold_kernel, [((own_rows, width), F32)], (owned, incoming))
+    plane, grad = lax.optimization_barrier((plane, grad))
     (columns,) = call(plane_kernel, [((far * SENT, BLOCK), jnp.int32)], (plane,))
     columns = swap(columns.reshape(far, 1, SENT * BLOCK), "dp_0").reshape(far * SENT, BLOCK)
     top, copies = call(column_kernel, [((tall, BLOCK), F32), ((plane_size * HELD, BLOCK), F32)], (columns,))
     sums = swap(copies.reshape(plane_size, 1, HELD * BLOCK), PLANE).reshape(plane_size * HELD, BLOCK)
 
-    (grad,) = call(cold_kernel, [((own_rows, width), F32)], (owned, incoming))
     (grad,) = call(two_kernel, [((own_rows, width), F32)], (grad, from_rep(grad, 1)))
     cold_table_new, cold_accum_new = call(
         update_kernel, [((own_rows, width), F32)] * 2, (grad, from_rep(grad, 3), cold_table, cold_accum)

time: 151 us -> 152 us (level)
  blocking collectives: 10.2 us -> 0 us
  starting transfers between devices: 66.4 us -> 72.3 us
  waiting for transfers between devices: 53.9 us -> 58.3 us
    all_to_all x1 -> x0, blocking collectives: 10.2 us -> none  [swap(): return lax.all_to_all(x, axis, split_axis=0, concat_axis=0, tiled=True)]
    all_to_all x5 -> x6, starting transfers between devices: 49.7 us -> 55.6 us  [swap(): return lax.all_to_all(x, axis, split_axis=0, concat_axis=0, tiled=True)]
    all_to_all x5 -> x6, waiting for transfers between devices: 43.3 us -> 47.7 us  [swap(): return lax.all_to_all(x, axis, split_axis=0, concat_axis=0, tiled=True)]
  transfers between devices with their start and end apart: 11 -> 12, of which waited for: 8 -> 9; matrix products, arithmetic and copies ran while one was open for 1% -> 1% of each run, Pallas kernels for 4% -> 5%
where the time goes in v9:
time: 152 us; the launch traced here: 151 us
  starting transfers between devices  72.3 us (48%)
  waiting for transfers between devices  58.3 us (38%)
  Pallas kernels  17.7 us (12%)
  local copies, waits for them, and re-layouts  1.87 us (1%)
    all_to_all x6, starting transfers between devices, swap(): return lax.all_to_all(x, axis, split_axis=0, concat_axis=0, tiled=True)  55.6 us
    all_to_all x6, waiting for transfers between devices, swap(): return lax.all_to_all(x, axis, split_axis=0, concat_axis=0, tiled=True)  47.7 us
    pallas_call x14, Pallas kernels, call(): pl.pallas_call(body, out_shape=[(pltpu.VMEM if i in kept else jax.ShapeDt...  17.7 us
    ppermute x5, starting transfers between devices, from_rep(): return lax.ppermute(piece, 'rep', [(i, i ^ distance) for i in range(4)])  14.4 us
    ppermute x5, waiting for transfers between devices, from_rep(): return lax.ppermute(piece, 'rep', [(i, i ^ distance) for i in range(4)])  10.6 us
  transfers between devices with their start and end apart: 12, of which 9 were waited for; matrix products, arithmetic and copies ran while one was open for 1% of the time, Pallas kernels for 5%

profile of v9, /device:TPU:1, one launch (start us, length us, event | category | flops | bytes accessed | tf_op | source)
XLA Modules:
  0.0 151.1 jit_solution(3860203109407532033)
XLA Ops:
  0.6 2.3 %shard_map.180 = (f32[128,128]{1,0:T(8,128)}, f32[512,128]{1,0:T(8,128)S(1)}) custom-call(s32[4,128]{1,0:T(4,128)} %bitcast.29, s32[4,128]{1,0:T(4,128)} %bitcast.30), custom_call_target="tpu_custom_call" | custom-call | flops 1000000000 | bytes 10000000 | tf_op jit(solution)/shard_map/pallas_call | solution.py:61
  3.0 20.4 %all-to-all-start = ((f32[128,1,128]{2,1,0:T(1,128)}), f32[128,1,128]{2,1,0:T(1,128)S(1)}, u32[]{:S(2)}, u32[]{:S(2)}) async-start(f32[128,1,128]{2,1,0:T(1,128)} %bitcast.5), calls=%async_computation | async-start | bytes 131072 | tf_op jit(solution)/shard_map/all_to_all | solution.py:392
  23.4 1.7 %shard_map.181 = (f32[8,512]{1,0:T(8,128)S(1)}, bf16[256,256]{1,0:T(8,128)(2,1)S(1)}, f32[8,512]{1,0:T(8,128)S(1)}, bf16[512,128]{1,0:T(8,128)(2,1)S(1)}, f32[256,128]{1,0:T(8,128)S(1)}, /*index=5*/f32[1,1024]{1,0:T(1,128)S(1)}) custom-call(f32[512,128]{1,0:T(8,128)S(1)} %get-tuple-element.41.refs_0_.refs_1_, s32[2,256]{1,0:T(2,128)} %bitcast.31, ...), custom_call_target="tpu_custom_call" | custom-call | flops 1000000000 | bytes 10000000 | tf_op jit(solution)/shard_map/pallas_call | solution.py:61
  25.1 13.1 %all-to-all-done = f32[128,1,128]{2,1,0:T(1,128)S(1)} async-done(((f32[128,1,128]{2,1,0:T(1,128)}), f32[128,1,128]{2,1,0:T(1,128)S(1)}, u32[]{:S(2)}, u32[]{:S(2)}) %all-to-all-start) | async-done | bytes 65568 | tf_op jit(solution)/shard_map/all_to_all | solution.py:392
  38.2 1.3 shard_map.182
  39.5 5.7 %all-to-all-start.1 = ((bf16[128,8,128]{2,1,0:T(8,128)(2,1)}), bf16[128,8,128]{2,1,0:T(8,128)(2,1)S(1)}, u32[]{:S(2)}, u32[]{:S(2)}) async-start(bf16[128,8,128]{2,1,0:T(8,128)(2,1)} %bitcast.10), calls=%async_computation.1 | async-start | bytes 524288 | tf_op jit(solution)/shard_map/all_to_all | solution.py:392
  45.9 19.9 %all-to-all-done.1 = bf16[128,8,128]{2,1,0:T(8,128)(2,1)S(1)} async-done(((bf16[128,8,128]{2,1,0:T(8,128)(2,1)}), bf16[128,8,128]{2,1,0:T(8,128)(2,1)S(1)}, u32[]{:S(2)}, u32[]{:S(2)}) %all-to-all-start.1) | async-done | bytes 262176 | tf_op jit(solution)/shard_map/all_to_all | solution.py:392
  65.8 3.0 %shard_map.183 = (bf16[1024,128]{1,0:T(8,128)(2,1)}, bf16[256,512]{1,0:T(8,128)(2,1)S(1)}, bf16[256,1024]{1,0:T(8,128)(2,1)S(1)}, bf16[512,128]{1,0:T(8,128)(2,1)S(1)}, f32[8,128]{1,0:T(8,128)S(1)}) custom-call(bf16[1024,128]{1,0:T(8,128)(2,1)S(1)} %bitcast.23, f32[512,128]{1,0:T(8,128)S(1)} %get-tuple-element.41.refs_0_.refs_1_, ...), custom_call_target="tpu_custom_call" | custom-call | flops 1000000000 | bytes 10000000 | tf_op jit(solution)/shard_map/pallas_call | solution.py:61
  68.8 1.6 %shard_map.184 = (s16[256,1408]{1,0:T(8,128)(2,1)S(1)}, f32[512,128]{1,0:T(8,128)S(1)}, f32[1024,128]{1,0:T(8,128)S(1)}) custom-call(s32[13]{0:T(128)S(1)} %pad_add_fusion.refs_0_, bf16[256,512]{1,0:T(8,128)(2,1)S(1)} %get-tuple-element.47.refs_1_, bf16[256,1024]{1,0:T(8,128)(2,1)S(1)} %get-tuple-element.48.refs_2_, f32[8,512]{1,0:T(8,128)S(1)} %get-tuple-element.49.refs_3_, ...), custom_call_target="tpu_custom_call" | custom-call | flops 1000000000 | bytes 10000000 | tf_op jit(solution)/shard_map/pallas_call | solution.py:61
  70.4 2.3 %collective-permute-start = (s16[256,1408]{1,0:T(8,128)(2,1)S(1)}, s16[256,1408]{1,0:T(8,128)(2,1)S(1)}, u32[]{:S(2)}, u32[]{:S(2)}) collective-permute-start(s16[256,1408]{1,0:T(8,128)(2,1)S(1)} %get-tuple-element.55), channel_id=1, source_target_pairs={{0,4},{4,0},{1,5},{5,1},{2,6},{6,2},{3,7},{7,3},{8,12},{12,8},{9,1... | collective-permute-start | bytes 2162696 | tf_op jit(solution)/shard_map/ppermute | solution.py:481
  72.7 8.1 %all-to-all-start.2 = ((bf16[128,8,128]{2,1,0:T(8,128)(2,1)}), bf16[128,8,128]{2,1,0:T(8,128)(2,1)S(1)}, u32[]{:S(2)}, u32[]{:S(2)}) async-start(bf16[128,8,128]{2,1,0:T(8,128)(2,1)} %bitcast.12), calls=%async_computation.2 | async-start | bytes 524288 | tf_op jit(solution)/shard_map/all_to_all | solution.py:392
  80.8 1.3 shard_map.185
  82.2 4.8 %collective-permute-start.1 = (s16[64,1408]{1,0:T(8,128)(2,1)S(1)}, s16[64,1408]{1,0:T(8,128)(2,1)S(1)}, u32[]{:S(2)}, u32[]{:S(2)}) collective-permute-start(s16[64,1408]{1,0:T(8,128)(2,1)S(1)} %get-tuple-element.57), channel_id=1, source_target_pairs={{0,2},{1,3},{2,0},{3,1},{4,6},{5,7},{6,4},{7,5},{8,10},{9,11},{10,... | collective-permute-start | bytes 540680 | tf_op jit(solution)/shard_map/ppermute | solution.py:396
  87.0 2.3 %collective-permute-start.2 = (s16[64,1408]{1,0:T(8,128)(2,1)S(1)}, s16[64,1408]{1,0:T(8,128)(2,1)S(1)}, u32[]{:S(2)}, u32[]{:S(2)}) collective-permute-start(s16[64,1408]{1,0:T(8,128)(2,1)S(1)} %get-tuple-element.58), channel_id=1, source_target_pairs={{0,1},{1,0},{2,3},{3,2},{4,5},{5,4},{6,7},{7,6},{8,9},{9,8},{10,11... | collective-permute-start | bytes 540680 | tf_op jit(solution)/shard_map/ppermute | solution.py:396
  89.3 2.3 %collective-permute-start.3 = (s16[64,1408]{1,0:T(8,128)(2,1)S(1)}, s16[64,1408]{1,0:T(8,128)(2,1)S(1)}, u32[]{:S(2)}, u32[]{:S(2)}) collective-permute-start(s16[64,1408]{1,0:T(8,128)(2,1)S(1)} %get-tuple-element.59), channel_id=1, source_target_pairs={{0,3},{1,2},{2,1},{3,0},{4,7},{5,6},{6,5},{7,4},{8,11},{9,10},{10,... | collective-permute-start | bytes 540680 | tf_op jit(solution)/shard_map/ppermute | solution.py:396
  91.6 3.9 %collective-permute-done.2.refs_2_ = s16[64,1408]{1,0:T(8,128)(2,1)S(1)} collective-permute-done((s16[64,1408]{1,0:T(8,128)(2,1)S(1)}, s16[64,1408]{1,0:T(8,128)(2,1)S(1)}, u32[]{:S(2)}, u32[]{:S(2)}) %collective-permute-start.2) | collective-permute-done | bytes 180256 | tf_op jit(solution)/shard_map/ppermute | solution.py:396
  95.5 1.5 %collective-permute-done.3.refs_3_ = s16[64,1408]{1,0:T(8,128)(2,1)S(1)} collective-permute-done((s16[64,1408]{1,0:T(8,128)(2,1)S(1)}, s16[64,1408]{1,0:T(8,128)(2,1)S(1)}, u32[]{:S(2)}, u32[]{:S(2)}) %collective-permute-start.3) | collective-permute-done | bytes 180256 | tf_op jit(solution)/shard_map/ppermute | solution.py:396
  97.1 0.9 shard_map.186
  98.0 3.3 %all-to-all-done.2 = bf16[128,8,128]{2,1,0:T(8,128)(2,1)S(1)} async-done(((bf16[128,8,128]{2,1,0:T(8,128)(2,1)}), bf16[128,8,128]{2,1,0:T(8,128)(2,1)S(1)}, u32[]{:S(2)}, u32[]{:S(2)}) %all-to-all-start.2) | async-done | bytes 262176 | tf_op jit(solution)/shard_map/all_to_all | solution.py:392
  101.3 5.3 %all-to-all-start.3 = ((s16[4,16,1408]{2,1,0:T(8,128)(2,1)}), s16[4,16,1408]{2,1,0:T(8,128)(2,1)S(1)}, u32[]{:S(2)}, u32[]{:S(2)}) async-start(s16[4,16,1408]{2,1,0:T(8,128)(2,1)} %bitcast.14), calls=%async_computation.3 | async-start | bytes 360448 | tf_op jit(solution)/shard_map/all_to_all | solution.py:392
  107.8 3.9 %all-to-all-done.3.refs_0_ = s16[4,16,1408]{2,1,0:T(8,128)(2,1)S(1)} async-done(((s16[4,16,1408]{2,1,0:T(8,128)(2,1)}), s16[4,16,1408]{2,1,0:T(8,128)(2,1)S(1)}, u32[]{:S(2)}, u32[]{:S(2)}) %all-to-all-start.3) | async-done | bytes 180256 | tf_op jit(solution)/shard_map/all_to_all | solution.py:392
  111.7 0.9 shard_map.191
  112.5 7.7 %all-to-all-start.4 = ((s32[16,1,2304]{2,1,0:T(1,128)}), s32[16,1,2304]{2,1,0:T(1,128)S(1)}, u32[]{:S(2)}, u32[]{:S(2)}) async-start(s32[16,1,2304]{2,1,0:T(1,128)} %bitcast.15), calls=%async_computation.4 | async-start | bytes 294912 | tf_op jit(solution)/shard_map/all_to_all | solution.py:392
  120.3 1.9 %collective-permute-start.4 = (f32[512,128]{1,0:T(8,128)S(1)}, f32[512,128]{1,0:T(8,128)S(1)}, u32[]{:S(2)}, u32[]{:S(2)}) collective-permute-start(f32[512,128]{1,0:T(8,128)S(1)} %shard_map.188.refs_0_), channel_id=1, source_target_pairs={{0,1},{1,0},{2,3},{3,2},{4,5},{5,4},{6,7},{7,6},{8,9},{9,8},{10,11... | collective-permute-start | bytes 786440 | tf_op jit(solution)/shard_map/ppermute | solution.py:396
  122.2 5.2 %collective-permute-done.4.refs_1_ = f32[512,128]{1,0:T(8,128)S(1)} collective-permute-done((f32[512,128]{1,0:T(8,128)S(1)}, f32[512,128]{1,0:T(8,128)S(1)}, u32[]{:S(2)}, u32[]{:S(2)}) %collective-permute-start.4) | collective-permute-done | bytes 262176 | tf_op jit(solution)/shard_map/ppermute | solution.py:396
  127.4 3.1 %collective-permute-start.5 = (f32[512,128]{1,0:T(8,128)S(1)}, f32[512,128]{1,0:T(8,128)S(1)}, u32[]{:S(2)}, u32[]{:S(2)}) collective-permute-start(f32[512,128]{1,0:T(8,128)S(1)} %shard_map.189.refs_0_), channel_id=1, source_target_pairs={{0,3},{1,2},{2,1},{3,0},{4,7},{5,6},{6,5},{7,4},{8,11},{9,10},{10,... | collective-permute-start | bytes 786440 | tf_op jit(solution)/shard_map/ppermute | solution.py:396
  130.5 1.8 %all-to-all-done.4 = s32[16,1,2304]{2,1,0:T(1,128)S(1)} async-done(((s32[16,1,2304]{2,1,0:T(1,128)}), s32[16,1,2304]{2,1,0:T(1,128)S(1)}, u32[]{:S(2)}, u32[]{:S(2)}) %all-to-all-start.4) | async-done | bytes 147488 | tf_op jit(solution)/shard_map/all_to_all | solution.py:392
  132.3 0.8 shard_map.192
  133.2 8.4 %all-to-all-start.5 = ((f32[32,1,1664]{2,1,0:T(1,128)}), f32[32,1,1664]{2,1,0:T(1,128)S(1)}, u32[]{:S(2)}, u32[]{:S(2)}) async-start(f32[32,1,1664]{2,1,0:T(1,128)} %bitcast.17), calls=%async_computation.5 | async-start | bytes 425984 | tf_op jit(solution)/shard_map/all_to_all | solution.py:392
  142.8 0.9 shard_map.190
  143.7 5.8 %all-to-all-done.5 = f32[32,1,1664]{2,1,0:T(1,128)S(1)} async-done(((f32[32,1,1664]{2,1,0:T(1,128)}), f32[32,1,1664]{2,1,0:T(1,128)S(1)}, u32[]{:S(2)}, u32[]{:S(2)}) %all-to-all-start.5) | async-done | bytes 213024 | tf_op jit(solution)/shard_map/all_to_all | solution.py:392
  149.5 1.6 %shard_map.193 = (f32[1024,128]{1,0:T(8,128)}, f32[1024,128]{1,0:T(8,128)}, f32[8,128]{1,0:T(8,128)}) custom-call(s32[13]{0:T(128)S(1)} %pad_add_fusion.refs_0_, f32[416,128]{1,0:T(8,128)S(1)} %bitcast.24, f32[1024,128]{1,0:T(8,128)S(1)} %copy-done.2, f32[1024,128]{1,0:T(8,128)S(1)} %copy-done.3), custom_call_target="tpu_custom_call" | custom-call | flops 1000000000 | bytes 10000000 | tf_op jit(solution)/shard_map/pallas_call | solution.py:61
  (24 shorter events, 3.2 us)
Async XLA Ops:
  3.0 35.2 %all-to-all-start = ((f32[128,1,128]{2,1,0:T(1,128)}), f32[128,1,128]{2,1,0:T(1,128)S(1)}, u32[]{:S(2)}, u32[]{:S(2)}) async-start(f32[128,1,128]{2,1,0:T(1,128)} %bitcast.5), calls=%async_computation | async-start | bytes 131072 | tf_op jit(solution)/shard_map/all_to_all | solution.py:392
  38.2 27.6 %copy-start = (bf16[512,1024]{1,0:T(8,128)(2,1)S(1)}, bf16[512,1024]{1,0:T(8,128)(2,1)}, u32[]{:S(2)}) copy-start(bf16[512,1024]{1,0:T(8,128)(2,1)} %refs_4_.1) | copy-start | bytes 3145732
  39.5 26.3 %all-to-all-start.1 = ((bf16[128,8,128]{2,1,0:T(8,128)(2,1)}), bf16[128,8,128]{2,1,0:T(8,128)(2,1)S(1)}, u32[]{:S(2)}, u32[]{:S(2)}) async-start(bf16[128,8,128]{2,1,0:T(8,128)(2,1)} %bitcast.10), calls=%async_computation.1 | async-start | bytes 524288 | tf_op jit(solution)/shard_map/all_to_all | solution.py:392
  45.2 0.7 copy-start.6
  45.2 0.7 copy-start.7
  65.8 3.0 %copy-start.1 = (f32[1024,128]{1,0:T(8,128)S(1)}, f32[1024,128]{1,0:T(8,128)}, u32[]{:S(2)}) copy-start(f32[1024,128]{1,0:T(8,128)} %refs_6_.1) | copy-start | bytes 1572868
  70.4 10.4 %collective-permute-start = (s16[256,1408]{1,0:T(8,128)(2,1)S(1)}, s16[256,1408]{1,0:T(8,128)(2,1)S(1)}, u32[]{:S(2)}, u32[]{:S(2)}) collective-permute-start(s16[256,1408]{1,0:T(8,128)(2,1)S(1)} %get-tuple-element.55), channel_id=1, source_target_pairs={{0,4},{4,0},{1,5},{5,1},{2,6},{6,2},{3,7},{7,3},{8,12},{12,8},{9,1... | collective-permute-start | bytes 2162696 | tf_op jit(solution)/shard_map/ppermute | solution.py:481
  72.7 28.6 %all-to-all-start.2 = ((bf16[128,8,128]{2,1,0:T(8,128)(2,1)}), bf16[128,8,128]{2,1,0:T(8,128)(2,1)S(1)}, u32[]{:S(2)}, u32[]{:S(2)}) async-start(bf16[128,8,128]{2,1,0:T(8,128)(2,1)} %bitcast.12), calls=%async_computation.2 | async-start | bytes 524288 | tf_op jit(solution)/shard_map/all_to_all | solution.py:392
  82.2 9.5 %collective-permute-start.1 = (s16[64,1408]{1,0:T(8,128)(2,1)S(1)}, s16[64,1408]{1,0:T(8,128)(2,1)S(1)}, u32[]{:S(2)}, u32[]{:S(2)}) collective-permute-start(s16[64,1408]{1,0:T(8,128)(2,1)S(1)} %get-tuple-element.57), channel_id=1, source_target_pairs={{0,2},{1,3},{2,0},{3,1},{4,6},{5,7},{6,4},{7,5},{8,10},{9,11},{10,... | collective-permute-start | bytes 540680 | tf_op jit(solution)/shard_map/ppermute | solution.py:396
  87.0 8.5 %collective-permute-start.2 = (s16[64,1408]{1,0:T(8,128)(2,1)S(1)}, s16[64,1408]{1,0:T(8,128)(2,1)S(1)}, u32[]{:S(2)}, u32[]{:S(2)}) collective-permute-start(s16[64,1408]{1,0:T(8,128)(2,1)S(1)} %get-tuple-element.58), channel_id=1, source_target_pairs={{0,1},{1,0},{2,3},{3,2},{4,5},{5,4},{6,7},{7,6},{8,9},{9,8},{10,11... | collective-permute-start | bytes 540680 | tf_op jit(solution)/shard_map/ppermute | solution.py:396
  89.3 7.7 %collective-permute-start.3 = (s16[64,1408]{1,0:T(8,128)(2,1)S(1)}, s16[64,1408]{1,0:T(8,128)(2,1)S(1)}, u32[]{:S(2)}, u32[]{:S(2)}) collective-permute-start(s16[64,1408]{1,0:T(8,128)(2,1)S(1)} %get-tuple-element.59), channel_id=1, source_target_pairs={{0,3},{1,2},{2,1},{3,0},{4,7},{5,6},{6,5},{7,4},{8,11},{9,10},{10,... | collective-permute-start | bytes 540680 | tf_op jit(solution)/shard_map/ppermute | solution.py:396
  101.3 10.4 %all-to-all-start.3 = ((s16[4,16,1408]{2,1,0:T(8,128)(2,1)}), s16[4,16,1408]{2,1,0:T(8,128)(2,1)S(1)}, u32[]{:S(2)}, u32[]{:S(2)}) async-start(s16[4,16,1408]{2,1,0:T(8,128)(2,1)} %bitcast.14), calls=%async_computation.3 | async-start | bytes 360448 | tf_op jit(solution)/shard_map/all_to_all | solution.py:392
  112.5 19.8 %all-to-all-start.4 = ((s32[16,1,2304]{2,1,0:T(1,128)}), s32[16,1,2304]{2,1,0:T(1,128)S(1)}, u32[]{:S(2)}, u32[]{:S(2)}) async-start(s32[16,1,2304]{2,1,0:T(1,128)} %bitcast.15), calls=%async_computation.4 | async-start | bytes 294912 | tf_op jit(solution)/shard_map/all_to_all | solution.py:392
  120.3 7.1 %collective-permute-start.4 = (f32[512,128]{1,0:T(8,128)S(1)}, f32[512,128]{1,0:T(8,128)S(1)}, u32[]{:S(2)}, u32[]{:S(2)}) collective-permute-start(f32[512,128]{1,0:T(8,128)S(1)} %shard_map.188.refs_0_), channel_id=1, source_target_pairs={{0,1},{1,0},{2,3},{3,2},{4,5},{5,4},{6,7},{7,6},{8,9},{9,8},{10,11... | collective-permute-start | bytes 786440 | tf_op jit(solution)/shard_map/ppermute | solution.py:396
  127.4 15.0 %collective-permute-start.5 = (f32[512,128]{1,0:T(8,128)S(1)}, f32[512,128]{1,0:T(8,128)S(1)}, u32[]{:S(2)}, u32[]{:S(2)}) collective-permute-start(f32[512,128]{1,0:T(8,128)S(1)} %shard_map.189.refs_0_), channel_id=1, source_target_pairs={{0,3},{1,2},{2,1},{3,0},{4,7},{5,6},{6,5},{7,4},{8,11},{9,10},{10,... | collective-permute-start | bytes 786440 | tf_op jit(solution)/shard_map/ppermute | solution.py:396
  133.2 16.3 %all-to-all-start.5 = ((f32[32,1,1664]{2,1,0:T(1,128)}), f32[32,1,1664]{2,1,0:T(1,128)S(1)}, u32[]{:S(2)}, u32[]{:S(2)}) async-start(f32[32,1,1664]{2,1,0:T(1,128)} %bitcast.17), calls=%async_computation.5 | async-start | bytes 425984 | tf_op jit(solution)/shard_map/all_to_all | solution.py:392
  141.6 1.0 copy-start.4
  141.6 1.2 copy-start.5
  142.4 7.1 %copy-start.2 = (f32[1024,128]{1,0:T(8,128)S(1)}, f32[1024,128]{1,0:T(8,128)}, u32[]{:S(2)}) copy-start(f32[1024,128]{1,0:T(8,128)} %refs_2_.5) | copy-start | bytes 1572868
  142.4 7.1 %copy-start.3 = (f32[1024,128]{1,0:T(8,128)S(1)}, f32[1024,128]{1,0:T(8,128)}, u32[]{:S(2)}) copy-start(f32[1024,128]{1,0:T(8,128)} %refs_3_.5) | copy-start | bytes 1572868
